TPU v7x, 32 devices: a whole 2x2x4 slice. The times are simulated.
32 devices in a mesh: replica: 1, expert: 32 (over z, y, x, core).
Axes of the slice: x: 2, y: 2, z: 4, core: 2. Of those that a mesh axis runs over, the one named last changes fastest.
Arguments:
- hidden_states: bfloat16 [4, 448, 4096], P(None, ('replica', 'expert')), may hold values from -6 to 6
- routes: int32 [4, 448, 8], P(None, ('replica', 'expert')), may hold values from 0 to 63, all different within a row; in each aligned block of 14 rows (0 to 13, 14 to 27, ..., all dimensions but the last counted through in order) at most 3 rows name the same one
- gates: float32 [4, 448, 8], P(None, ('replica', 'expert')), may hold values from 0.05 to 1
- w_gate: bfloat16 [64, 4096, 768], P('expert', 'replica'), may hold values from -0.09375 to 0.09375
- w_up: bfloat16 [64, 4096, 768], P('expert', 'replica'), may hold values from -0.09375 to 0.09375
- queries: bfloat16 [4, 448, 8192], P(None, ('replica', 'expert')), may hold values from -200 to 200
- new_keys: bfloat16 [4, 448, 512], P(None, ('replica', 'expert')), may hold values from -6 to 6
- new_values: bfloat16 [4, 448, 512], P(None, ('replica', 'expert')), may hold values from -6 to 6
- cache_keys: bfloat16 [448, 128, 512], P(('replica', 'expert')), may hold values from -6 to 6
- cache_values: bfloat16 [448, 128, 512], P(('replica', 'expert')), may hold values from -6 to 6
- lengths: int32 [448], P(('replica', 'expert')), may hold values from 2 to 128, as said below
Outputs:
- moe_hidden: bfloat16 [4, 448, 6144], P(None, ('replica', 'expert'))
- attn_out: bfloat16 [4, 448, 8192], P(None, ('replica', 'expert'))
Inputs may be any that keep to these rules, and one draw needn't show every extreme that they name: `routes`: each token names 8 different experts; among the 14 tokens of one device at one step no expert is named more than 3 times, and in some such blocks one expert is named exactly 3 times. `lengths`: some rollout holds exactly 128 cached entries.
All inputs are finite; a program needn't handle non-finite values.
Results may differ from a plain program's by a relative error of at most 0.0065.
Values may be sent and summed in bfloat16 or wider, within the bound.
No kernel may reach another device: no remote copies, remote signals or barrier semaphores. Data moves between devices by JAX's collectives and lax.ppermute only.
A program may use at most 128 MiB of HBM per device.

v0:
```python
import math

import jax
import jax.numpy as jnp
from jax import lax
from jax.sharding import PartitionSpec as P

HQ = 64
KVH = 4
HD = 128
TOPK = 8


def attention(queries, new_keys, new_values, cache_keys, cache_values, lengths):
    steps_total, local_rows, _ = queries.shape
    groups = HQ // KVH
    queried = queries.reshape(steps_total, local_rows, KVH, groups, HD)
    cache_len = cache_keys.shape[1]
    keys_cached = cache_keys.reshape(local_rows, cache_len, KVH, HD)
    values_cached = cache_values.reshape(local_rows, cache_len, KVH, HD)
    keys_new = new_keys.reshape(steps_total, local_rows, KVH, HD)
    values_new = new_values.reshape(steps_total, local_rows, KVH, HD)
    score_scale = 1.0 / math.sqrt(HD)
    valid_cache = (jnp.arange(cache_len, dtype=jnp.int32)[None, :] < lengths[:, None])[
        None, :, None, None, :
    ]
    valid_new = (
        jnp.arange(steps_total, dtype=jnp.int32)[None, :]
        <= jnp.arange(steps_total, dtype=jnp.int32)[:, None]
    )[:, None, None, None, :]
    scores_cache = (
        jnp.einsum("srghd,rlgd->srghl", queried, keys_cached, preferred_element_type=jnp.float32)
        * score_scale
    )
    scores_cache = jnp.where(valid_cache, scores_cache, -jnp.inf)
    scores_new = (
        jnp.einsum("srghd,jrgd->srghj", queried, keys_new, preferred_element_type=jnp.float32)
        * score_scale
    )
    scores_new = jnp.where(valid_new, scores_new, -jnp.inf)
    top_score = jnp.maximum(
        jnp.max(scores_cache, axis=-1, keepdims=True), jnp.max(scores_new, axis=-1, keepdims=True)
    )
    weights_cache = jnp.exp(scores_cache - top_score)
    weights_new = jnp.exp(scores_new - top_score)
    total_weight = jnp.sum(weights_cache, axis=-1, keepdims=True) + jnp.sum(
        weights_new, axis=-1, keepdims=True
    )
    probs_cache = (weights_cache / total_weight).astype(jnp.bfloat16)
    probs_new = (weights_new / total_weight).astype(jnp.bfloat16)
    attended = jnp.einsum(
        "srghl,rlgd->srghd", probs_cache, values_cached, preferred_element_type=jnp.float32
    )
    attended = attended + jnp.einsum(
        "srghj,jrgd->srghd", probs_new, values_new, preferred_element_type=jnp.float32
    )
    return attended.astype(jnp.bfloat16).reshape(steps_total, local_rows, HQ * HD)


def per_device(
    hidden_states,
    routes,
    gates,
    w_gate,
    w_up,
    queries,
    new_keys,
    new_values,
    cache_keys,
    cache_values,
    lengths,
):
    peers = lax.axis_size("expert")
    experts_local = w_gate.shape[0]
    experts = experts_local * peers
    steps_total, local_rows, model_width = hidden_states.shape
    capacity = local_rows * TOPK * 2 // experts
    gate_full, up_full = (
        lax.all_gather(w_gate, "replica", axis=1, tiled=True),
        lax.all_gather(w_up, "replica", axis=1, tiled=True),
    )
    hidden_width = gate_full.shape[2]
    states_f32 = hidden_states.astype(jnp.float32)
    normed = (
        states_f32 * lax.rsqrt(jnp.mean(states_f32 * states_f32, axis=-1, keepdims=True) + 1e-06)
    ).astype(jnp.bfloat16)
    mixing = gates / jnp.sum(gates, axis=-1, keepdims=True)
    pair_ids = routes.reshape(steps_total, local_rows * TOPK)
    onehot = (pair_ids[..., None] == jnp.arange(experts, dtype=jnp.int32)).astype(jnp.int32)
    earlier = jnp.cumsum(onehot, axis=1) - onehot
    slot_ids = jnp.sum(earlier * onehot, axis=-1).reshape(steps_total, local_rows, TOPK)
    slot_span = steps_total * capacity
    columns = (
        routes * slot_span
        + jnp.arange(steps_total, dtype=jnp.int32)[:, None, None] * capacity
        + slot_ids
    )
    column_marks = columns[..., None] == jnp.arange(experts * slot_span, dtype=jnp.int32)
    dispatch = jnp.any(column_marks, axis=2).astype(jnp.bfloat16)
    picker = column_marks.astype(jnp.bfloat16)
    dispatch, picker = (dispatch, picker)
    outgoing = jnp.einsum(
        "src,srd->cd", dispatch, normed, preferred_element_type=jnp.float32
    ).astype(jnp.bfloat16)
    outgoing = outgoing.reshape(experts, slot_span, model_width)
    received = lax.all_to_all(outgoing, "expert", split_axis=0, concat_axis=0, tiled=True)
    slots_here = received.shape[1]
    grouped = received.reshape(peers, experts_local, slots_here, model_width)
    gate_act = jnp.einsum("pecd,edf->pecf", grouped, gate_full, preferred_element_type=jnp.float32)
    up_act = jnp.einsum("pecd,edf->pecf", grouped, up_full, preferred_element_type=jnp.float32)
    inner_act = (jax.nn.silu(gate_act) * up_act).astype(jnp.bfloat16)
    inner_act = inner_act.reshape(peers * experts_local, slots_here, hidden_width)
    returned = lax.all_to_all(inner_act, "expert", split_axis=0, concat_axis=0, tiled=True)
    back_rows = returned.reshape(experts * slot_span, hidden_width)
    picked = jnp.einsum("srkc,cf->srkf", picker, back_rows, preferred_element_type=jnp.float32)
    moe_hidden = (
        (picked * mixing[..., None])
        .reshape(steps_total, local_rows, TOPK * hidden_width)
        .astype(jnp.bfloat16)
    )
    attn_out = attention(queries, new_keys, new_values, cache_keys, cache_values, lengths)
    return (moe_hidden, attn_out)


def solution(mesh):
    in_specs = (
        P(None, ("replica", "expert"), None),
        P(None, ("replica", "expert"), None),
        P(None, ("replica", "expert"), None),
        P("expert", "replica", None),
        P("expert", "replica", None),
        P(None, ("replica", "expert"), None),
        P(None, ("replica", "expert"), None),
        P(None, ("replica", "expert"), None),
        P(("replica", "expert"), None, None),
        P(("replica", "expert"), None, None),
        P(("replica", "expert")),
    )
    out_specs = (P(None, ("replica", "expert"), None), P(None, ("replica", "expert"), None))
    return jax.shard_map(
        per_device, mesh=mesh, in_specs=in_specs, out_specs=out_specs, check_vma=False
    )
```

profile of v0, /device:TPU:0, one launch (start us, length us, event | category | flops | bytes accessed | tf_op | source)
XLA Modules:
  0.0 293.6 jit_solution(4196460467780809332)
XLA Ops:
  0.6 0.0 copy-start
  0.6 0.0 copy-start.3
  0.7 0.9 copy.40
  1.5 0.1 eq.28
  1.6 0.1 fusion.45
  1.8 0.2 reduce_window_sum.11
  2.0 0.2 select_reduce_fusion
  2.2 0.1 reshape.97
  2.3 0.1 add_add_fusion
  2.4 0.5 fusion.22
  2.9 1.3 fusion.30
  4.3 0.0 copy-done.3
  4.3 0.3 fusion.31
  4.6 4.6 %bitcast_convert_fusion = bf16[768,4096]{1,0:T(8,128)(2,1)} fusion(pred[4,14,768]{2,1,0:T(8,128)(4,1)S(1)} %fusion.22, bf16[4,14,4096]{2,0,1:T(4,128)(2,1)S(1)} %fusion.31), kind=kOutput, calls=%fused_computation.4 | convolution fusion | flops 355467264 | bytes 6793216 | tf_op jit(solution)/shard_map/src,srd->cd/dot_general | solution.py:102
  9.1 9.8 %reshape.98 = bf16[64,12,4096]{2,1,0:T(8,128)(2,1)} reshape(bf16[768,4096]{1,0:T(8,128)(2,1)} %bitcast_convert_fusion) | data formatting | bytes 12582912 | tf_op jit(solution)/shard_map/reshape | solution.py:105
  18.9 0.0 copy-start.4
  18.9 7.6 %all-to-all-start = ((bf16[64,12,4096]{2,1,0:T(8,128)(2,1)}), bf16[64,12,4096]{2,1,0:T(8,128)(2,1)}, u32[]{:S(2)}, u32[]{:S(2)}) async-start(bf16[64,12,4096]{2,1,0:T(8,128)(2,1)} %reshape.98), calls=%async_computation | async-start | bytes 16777216 | tf_op jit(solution)/shard_map/all_to_all | solution.py:106
  26.5 0.0 copy-done.4
  26.6 185.9 %all-to-all-done = bf16[64,12,4096]{2,1,0:T(8,128)(2,1)} async-done(((bf16[64,12,4096]{2,1,0:T(8,128)(2,1)}), bf16[64,12,4096]{2,1,0:T(8,128)(2,1)}, u32[]{:S(2)}, u32[]{:S(2)}) %all-to-all-start) | async-done | bytes 6291488 | tf_op jit(solution)/shard_map/all_to_all | solution.py:106
  212.5 22.1 %fusion.2 = f32[2,32,12,768]{3,1,2,0:T(8,128)S(1)} fusion(bf16[2,4096,768]{2,1,0:T(8,128)(2,1)} %param.14, bf16[32,2,12,4096]{3,2,1,0:T(8,128)(2,1)} %bitcast.1), kind=kOutput, calls=%fused_computation.2 | convolution fusion | flops 4831838208 | bytes 21233664 | tf_op jit(solution)/shard_map/pecd,edf->pecf/dot_general | solution.py:109
  234.6 13.4 %fusion.6 = bf16[32,2,12,768]{3,0,2,1:T(8,128)(2,1)S(1)} fusion(f32[2,32,12,768]{3,1,2,0:T(8,128)S(1)} %fusion.2, bf16[2,4096,768]{2,1,0:T(8,128)(2,1)} %param.15, bf16[32,2,12,4096]{3,2,1,0:T(8,128)(2,1)} %bitcast.1), kind=kOutput, calls=%fused_computation.8 | convolution fusion | flops 4835377152 | bytes 22413312 | tf_op jit(solution)/shard_map/pecd,edf->pecf/dot_general | solution.py:110
  248.0 1.8 copy.67
  249.8 0.0 copy-start.1
  249.8 3.0 %all-to-all-start.1 = ((bf16[64,12,768]{2,1,0:T(8,128)(2,1)}), bf16[64,12,768]{2,1,0:T(8,128)(2,1)S(1)}, u32[]{:S(2)}, u32[]{:S(2)}) async-start(bf16[64,12,768]{2,1,0:T(8,128)(2,1)} %bitcast.8), calls=%async_computation.1 | async-start | bytes 3145728 | tf_op jit(solution)/shard_map/all_to_all | solution.py:113
  252.9 0.1 copy.48
  253.0 3.0 %reshape.103 = bf16[4,14,4,16,128]{4,3,2,0,1:T(8,128)(2,1)} reshape(bf16[4,14,8192]{2,0,1:T(4,128)(2,1)} %param.16) | data formatting | bytes 1835008 | tf_op jit(solution)/shard_map/reshape | solution.py:17
  256.0 0.0 copy-done.1
  256.0 1.5 reshape.102
  257.5 0.0 copy-start.5
  257.5 3.2 %reshape.105 = bf16[14,128,4,128]{3,2,1,0:T(4,128)(2,1)S(1)} reshape(bf16[14,128,512]{2,1,0:T(8,128)(2,1)} %param.20) | data formatting | bytes 3670016 | tf_op jit(solution)/shard_map/reshape | solution.py:20
  260.7 0.0 copy-start.2
  260.7 0.0 copy-done.5
  260.7 0.1 iota_compare_fusion.5
  260.8 3.6 %fusion.50 = (f32[4,14,4,16]{3,0,2,1:T(4,128)S(1)}, f32[4,14,4,16,4]{3,4,0,2,1:T(4,128)S(1)}) fusion(bf16[4,14,4,16,128]{4,3,2,0,1:T(8,128)(2,1)} %reshape.103, bf16[4,14,512]{2,0,1:T(4,128)(2,1)} %param.17, pred[4,4]{1,0:T(4,128)(4,1)S(1)} %iota_compare_fusion.6), kind=kOutput, calls=%fused_computation.66 | convolution fusion | flops 3709440 | bytes 1046544 | tf_op jit(solution)/shard_map/srghd,jrgd->srghj/dot_general | solution.py:37
  264.4 0.0 copy-done.2
  264.4 2.7 bitcast_reduce_fusion
  267.2 0.4 fusion.41
  267.6 1.1 fusion.21
  268.8 0.0 copy-done
  268.8 0.5 fusion.42
  269.3 1.4 fusion.24
  270.7 0.2 copy.56
  270.9 1.1 reshape.107
  272.1 18.5 %all-to-all-done.1 = bf16[64,12,768]{2,1,0:T(8,128)(2,1)S(1)} async-done(((bf16[64,12,768]{2,1,0:T(8,128)(2,1)}), bf16[64,12,768]{2,1,0:T(8,128)(2,1)S(1)}, u32[]{:S(2)}, u32[]{:S(2)}) %all-to-all-start.1) | async-done | bytes 1179680 | tf_op jit(solution)/shard_map/all_to_all | solution.py:113
  290.6 0.3 reshape.111
  290.9 0.8 fusion.23
  291.7 0.5 reshape.117
  292.2 1.4 copy.68
  (7 shorter events, 0.1 us)
Async XLA Ops:
  0.6 268.1 %copy-start = (bf16[4,14,512]{2,0,1:T(4,128)(2,1)S(1)}, bf16[4,14,512]{2,0,1:T(4,128)(2,1)}, u32[]{:S(2)}) copy-start(bf16[4,14,512]{2,0,1:T(4,128)(2,1)} %param.18) | copy-start | bytes 172036
  0.6 3.6 %copy-start.3 = (bf16[4,14,4096]{2,0,1:T(4,128)(2,1)S(1)}, bf16[4,14,4096]{2,0,1:T(4,128)(2,1)}, u32[]{:S(2)}) copy-start(bf16[4,14,4096]{2,0,1:T(4,128)(2,1)} %param.11) | copy-start | bytes 1376260
  18.9 7.6 %copy-start.4 = (f32[4,14,8]{1,2,0:T(8,128)S(1)}, f32[4,14,8]{1,2,0:T(8,128)}, u32[]{:S(2)}) copy-start(f32[4,14,8]{1,2,0:T(8,128)} %param.13) | copy-start | bytes 5380
  18.9 193.6 %all-to-all-start = ((bf16[64,12,4096]{2,1,0:T(8,128)(2,1)}), bf16[64,12,4096]{2,1,0:T(8,128)(2,1)}, u32[]{:S(2)}, u32[]{:S(2)}) async-start(bf16[64,12,4096]{2,1,0:T(8,128)(2,1)} %reshape.98), calls=%async_computation | async-start | bytes 16777216 | tf_op jit(solution)/shard_map/all_to_all | solution.py:106
  249.8 6.2 %copy-start.1 = (bf16[14,128,512]{2,1,0:T(8,128)(2,1)S(1)}, bf16[14,128,512]{2,1,0:T(8,128)(2,1)}, u32[]{:S(2)}) copy-start(bf16[14,128,512]{2,1,0:T(8,128)(2,1)} %param.19) | copy-start | bytes 5505028
  249.8 40.8 %all-to-all-start.1 = ((bf16[64,12,768]{2,1,0:T(8,128)(2,1)}), bf16[64,12,768]{2,1,0:T(8,128)(2,1)S(1)}, u32[]{:S(2)}, u32[]{:S(2)}) async-start(bf16[64,12,768]{2,1,0:T(8,128)(2,1)} %bitcast.8), calls=%async_computation.1 | async-start | bytes 3145728 | tf_op jit(solution)/shard_map/all_to_all | solution.py:113
  257.5 3.3 %copy-start.5 = (s32[14]{0:T(128)S(1)}, s32[14]{0:T(128)}, u32[]{:S(2)}) copy-start(s32[14]{0:T(128)} %param.21) | copy-start | bytes 172
  260.7 3.7 %copy-start.2 = (bf16[14,128,4,128]{3,2,1,0:T(4,128)(2,1)S(1)}, bf16[14,128,4,128]{3,2,1,0:T(4,128)(2,1)}, u32[]{:S(2)}) copy-start(bf16[14,128,4,128]{3,2,1,0:T(4,128)(2,1)} %reshape.102) | copy-start | bytes 5505028
where the time goes:
time: 294 us
  waiting for transfers between devices  204 us (69%)
  matrix products  49 us (17%)
  local copies, waits for them, and re-layouts  24.1 us (8%)
  starting transfers between devices  10.6 us (4%)
  other arithmetic  4.56 us (2%)
    all_to_all x1, waiting for transfers between devices, per_device(): lax.all_to_all(outgoing, 'expert', split_axis=0, concat_axis=0, tiled=True)  186 us
    dot_general x1, matrix products, per_device(): jnp.einsum('pecd,edf->pecf', grouped, gate_full, preferred_element_type=j...  22.1 us
    all_to_all x1, waiting for transfers between devices, per_device(): lax.all_to_all(inner_act, 'expert', split_axis=0, concat_axis=0, tiled=True)  18.5 us
    dot_general x1, matrix products, per_device(): jnp.einsum('pecd,edf->pecf', grouped, up_full, preferred_element_type=jnp...  13.4 us
    reshape x1, local copies, waits for them, and re-layouts, per_device(): outgoing = outgoing.reshape(experts, slot_span, model_width)  9.79 us
    all_to_all x1, starting transfers between devices, per_device(): lax.all_to_all(outgoing, 'expert', split_axis=0, concat_axis=0, tiled=True)  7.61 us
  transfers between devices with their start and end apart: 2, of which 2 were waited for; matrix products, arithmetic and copies ran while one was open for 7% of the time, Pallas kernels for 0%

commit v1 on v0

--- a/solution.py
+++ b/solution.py
@@ -2,13 +2,20 @@
 
 import jax
 import jax.numpy as jnp
+import numpy as np
 from jax import lax
+from jax.experimental import pallas as pl
+from jax.experimental.pallas import tpu as pltpu
 from jax.sharding import PartitionSpec as P
 
 HQ = 64
 KVH = 4
 HD = 128
 TOPK = 8
+LANES = 128
+EDGE = 2
+INNER = EDGE**3
+VMEM_BYTES = 48 * 1024 * 1024
 
 
 def attention(queries, new_keys, new_values, cache_keys, cache_values, lengths):
@@ -57,6 +64,141 @@
     return attended.astype(jnp.bfloat16).reshape(steps_total, local_rows, HQ * HD)
 
 
+def place(index):
+    return index // INNER, index // 4 % EDGE, index // 2 % EDGE, index % EDGE
+
+
+def device_at(line, row, column, side):
+    return ((line * EDGE + row) * EDGE + column) * EDGE + side
+
+
+def moves(peers, target):
+    return [(index, device_at(*target(*place(index)))) for index in range(peers)]
+
+
+def padded(rows):
+    return -(-rows // 16) * 16
+
+
+def prepare_kernel(states_ref, routes_ref, order_ref, payload_ref, *, capacity, experts):
+    width = states_ref.shape[1]
+    states = states_ref[...].astype(jnp.float32)
+    scale = lax.rsqrt(jnp.mean(states * states, axis=-1, keepdims=True) + 1e-06)
+    payload_ref[:, :width] = (states * scale).astype(payload_ref.dtype)
+    routes = routes_ref[...]
+    rows = routes.shape[0]
+    expert_ids = lax.broadcasted_iota(jnp.int32, (rows, experts), 1)
+    marks = [
+        (routes[:, choice : choice + 1] == expert_ids).astype(jnp.float32)
+        for choice in range(TOPK)
+    ]
+    named = sum(marks)
+    earlier = jnp.dot(
+        order_ref[...], named.astype(jnp.bfloat16), preferred_element_type=jnp.float32
+    )
+    lane_ids = lax.broadcasted_iota(jnp.int32, (rows, LANES), 1)
+    codes = jnp.full((rows, LANES), -1.0, jnp.float32)
+    for choice in range(TOPK):
+        slot = jnp.sum(earlier * marks[choice], axis=-1, keepdims=True)
+        expert = routes[:, choice : choice + 1].astype(jnp.float32)
+        codes = jnp.where(lane_ids == choice, expert, codes)
+        codes = jnp.where(lane_ids == TOPK + choice, slot, codes)
+    payload_ref[:, width:] = codes.astype(payload_ref.dtype)
+
+
+def prepare(states, routes, steps_total, capacity, experts):
+    rows, width = states.shape
+    local_rows = rows // steps_total
+    numbers = np.arange(rows)
+    order = (numbers[:, None] // local_rows == numbers[None, :] // local_rows) & (
+        numbers[:, None] > numbers[None, :]
+    )
+    return pl.pallas_call(
+        lambda *refs: prepare_kernel(*refs, capacity=capacity, experts=experts),
+        out_shape=jax.ShapeDtypeStruct((rows, width + LANES), jnp.bfloat16),
+        compiler_params=pltpu.CompilerParams(vmem_limit_bytes=VMEM_BYTES),
+        name="prepare",
+    )(states, routes, jnp.asarray(order, jnp.bfloat16))
+
+
+def pick_kernel(own_ref, near_ref, far_ref, same_ref, expert_ref, slot_ref, keep_ref, send_ref):
+    width = keep_ref.shape[1]
+    rows = jnp.concatenate([own_ref[...], near_ref[...], far_ref[...]], axis=0)
+    codes = rows[:, width:].astype(jnp.float32)
+    wanted_expert, wanted_slot = expert_ref[...], slot_ref[...]
+    hits = jnp.zeros((rows.shape[0], wanted_expert.shape[1]), jnp.float32)
+    for choice in range(TOPK):
+        match = (codes[:, choice : choice + 1] == wanted_expert) & (
+            codes[:, TOPK + choice : TOPK + choice + 1] == wanted_slot
+        )
+        hits = jnp.where(match, 1.0, hits)
+    onehot = (hits * same_ref[...]).astype(jnp.bfloat16)
+    kept = keep_ref.shape[0]
+    picked = lax.dot_general(
+        onehot,
+        rows[:, :width],
+        (((0,), (0,)), ((), ())),
+        preferred_element_type=jnp.float32,
+    ).astype(keep_ref.dtype)
+    keep_ref[...] = picked[:kept]
+    send_ref[...] = picked[kept:]
+
+
+def slot_tables(steps_total, local_rows, capacity, experts_local):
+    entries = []
+    for side, blocks in ((0, (0, 1, 2, 3, 4)), (1, (2, 3, 4))):
+        for expert in range(experts_local):
+            group = [
+                (side, expert, block, step, slot)
+                for block in blocks
+                for step in range(steps_total)
+                for slot in range(capacity)
+            ]
+            entries += group + [(side, expert, -1, -1, -1)] * (padded(len(group)) - len(group))
+    return np.array(entries, np.int32)
+
+
+def expert_kernel(*refs, pairs, kept, sent):
+    x_refs, (gate_ref, up_ref, out_ref, rows_ref) = refs[: 2 * pairs], refs[2 * pairs :]
+
+    @pl.when(pl.program_id(1) == 0)
+    def _():
+        expert, at = pl.program_id(0), 0
+        for number, x_ref in enumerate(x_refs):
+            part = sent if number % 2 else kept
+            rows_ref[at : at + part, :] = x_ref[pl.ds(pl.multiple_of(expert * part, 16), part), :]
+            at += part
+
+    rows = rows_ref[...]
+    gate = jnp.dot(rows, gate_ref[0], preferred_element_type=jnp.float32)
+    up = jnp.dot(rows, up_ref[0], preferred_element_type=jnp.float32)
+    out_ref[0] = (gate / (1.0 + jnp.exp(-gate)) * up).astype(out_ref.dtype)
+
+
+def run_experts(arrays, w_gate, w_up):
+    experts_local, width, hidden = w_gate.shape
+    kept, sent = arrays[0].shape[0] // experts_local, arrays[1].shape[0] // experts_local
+    pairs = len(arrays) // 2
+    rows = pairs * (kept + sent)
+    block = 2 * LANES
+    return pl.pallas_call(
+        lambda *refs: expert_kernel(*refs, pairs=pairs, kept=kept, sent=sent),
+        grid=(experts_local, hidden // block),
+        in_specs=[pl.BlockSpec(a.shape, lambda e, f: (0, 0)) for a in arrays]
+        + [pl.BlockSpec((1, width, block), lambda e, f: (e, 0, f))] * 2,
+        out_specs=pl.BlockSpec((1, rows, block), lambda e, f: (e, 0, f)),
+        out_shape=jax.ShapeDtypeStruct((experts_local, rows, hidden), jnp.bfloat16),
+        scratch_shapes=[pltpu.VMEM((rows, width), jnp.bfloat16)],
+        compiler_params=pltpu.CompilerParams(vmem_limit_bytes=VMEM_BYTES),
+        cost_estimate=pl.CostEstimate(
+            flops=4 * experts_local * rows * width * hidden,
+            bytes_accessed=4 * experts_local * width * hidden,
+            transcendentals=experts_local * rows * hidden,
+        ),
+        name="experts",
+    )(*arrays, w_gate, w_up)
+
+
 def per_device(
     hidden_states,
     routes,
@@ -71,47 +213,118 @@
     lengths,
 ):
     peers = lax.axis_size("expert")
+    me = lax.axis_index("expert")
+    lines = peers // INNER
     experts_local = w_gate.shape[0]
     experts = experts_local * peers
     steps_total, local_rows, model_width = hidden_states.shape
     capacity = local_rows * TOPK * 2 // experts
+    slot_span = steps_total * capacity
     gate_full, up_full = (
         lax.all_gather(w_gate, "replica", axis=1, tiled=True),
         lax.all_gather(w_up, "replica", axis=1, tiled=True),
     )
     hidden_width = gate_full.shape[2]
-    states_f32 = hidden_states.astype(jnp.float32)
-    normed = (
-        states_f32 * lax.rsqrt(jnp.mean(states_f32 * states_f32, axis=-1, keepdims=True) + 1e-06)
-    ).astype(jnp.bfloat16)
+    block_rows = steps_total * local_rows
+
+    send = lambda array, target: lax.ppermute(array, "expert", moves(peers, target))
+    to_line = lambda offset: lambda z, y, x, c: (z ^ offset, y, x, c)
+    first_hop = lambda z, y, x, c: (z, y ^ c, x ^ (1 - c), c)
+    second_hop = lambda z, y, x, c: (z, y ^ (1 - c), x ^ c, c)
+    other_side = lambda z, y, x, c: (z, y, x, 1 - c)
+    sides = [[EDGE * chip + side for side in range(EDGE)] for chip in range(peers // EDGE)]
+    z, y, x, side = place(me)
+
+    payload = prepare(
+        hidden_states.reshape(block_rows, model_width),
+        routes.reshape(block_rows, TOPK),
+        steps_total,
+        capacity,
+        experts,
+    )
+    tables = slot_tables(steps_total, local_rows, capacity, experts_local)
+    kept_rows = int((tables[:, 0] == 0).sum())
+    token_block = np.arange(5 * block_rows) // block_rows
+    token_step = np.arange(5 * block_rows) % block_rows // local_rows
+    same = (token_block[:, None] == tables[None, :, 2]) & (token_step[:, None] == tables[None, :, 3])
+    wanted_expert = (
+        jnp.where(tables[:, 0] == 0, me, me ^ 1) * experts_local + tables[:, 1]
+    ).astype(jnp.float32)[None]
+    wanted_slot = jnp.asarray(tables[:, 4], jnp.float32)[None]
+    pick = pl.pallas_call(
+        pick_kernel,
+        out_shape=(
+            jax.ShapeDtypeStruct((kept_rows, model_width), jnp.bfloat16),
+            jax.ShapeDtypeStruct((len(tables) - kept_rows, model_width), jnp.bfloat16),
+        ),
+        compiler_params=pltpu.CompilerParams(vmem_limit_bytes=VMEM_BYTES),
+        name="pick",
+    )
+
+    arrived, last = [payload], payload
+    for offset in range(1, lines):
+        source = payload
+        if offset > 2:
+            source, last = lax.optimization_barrier((payload, last))
+            arrived[-1] = last
+        last = send(source, to_line(offset))
+        arrived.append(last)
+    blocks = []
+    for own in arrived:
+        pair = lax.all_gather(own, "expert", axis_index_groups=sides, tiled=True)
+        near = send(pair, first_hop)
+        half = lax.dynamic_slice_in_dim(near, side * block_rows, block_rows)
+        far = send(half, second_hop)
+        keep, give = pick(
+            pair, near, far, jnp.asarray(same, jnp.float32), wanted_expert, wanted_slot
+        )
+        blocks.append((keep, send(give, other_side)))
+    inner = []
+    batch = max(1, lines // 2)
+    for start in range(0, lines, batch):
+        arrays = [array for pair in blocks[start : start + batch] for array in pair]
+        inner.append(run_experts(arrays, gate_full, up_full))
+    kept, sent = kept_rows // experts_local, (len(tables) - kept_rows) // experts_local
+    computed = jnp.concatenate([part.reshape(-1, hidden_width) for part in inner], axis=0)
+    numbers = jnp.arange(experts * slot_span, dtype=jnp.int32)
+    owner, expert, rest = (
+        numbers // (experts_local * slot_span),
+        numbers // slot_span % experts_local,
+        numbers % slot_span,
+    )
+    oz, oy, ox, oc = place(owner)
+    item = oz ^ z
+    own_chip, far_chip = (oy == y) & (ox == x), (oy != y) & (ox != x)
+    mine = jnp.where(side == 0, oy == y, ox == x)
+    kept_block = jnp.where(own_chip, oc, jnp.where(far_chip, 4, 2 + oc))
+    sent_block = jnp.where(far_chip, 2, oc)
+    kept_here = own_chip | jnp.where(far_chip, oc == side, mine)
+    in_item = jnp.where(kept_here, kept_block * slot_span, kept + sent_block * slot_span) + rest
+    call = item // batch
+    row_of = (
+        (call * experts_local + expert) * batch + item % batch
+    ) * (kept + sent) + in_item
+    row_marks = (row_of[:, None] == jnp.arange(computed.shape[0], dtype=jnp.int32)).astype(
+        jnp.bfloat16
+    )
+    outgoing = jnp.dot(row_marks, computed, preferred_element_type=jnp.float32).astype(jnp.bfloat16)
+    outgoing = outgoing.reshape(peers, experts_local * slot_span, hidden_width)
+    returned = lax.all_to_all(outgoing, "expert", split_axis=0, concat_axis=0, tiled=True)
+    back_rows = returned.reshape(experts * slot_span, hidden_width)
+
     mixing = gates / jnp.sum(gates, axis=-1, keepdims=True)
     pair_ids = routes.reshape(steps_total, local_rows * TOPK)
     onehot = (pair_ids[..., None] == jnp.arange(experts, dtype=jnp.int32)).astype(jnp.int32)
     earlier = jnp.cumsum(onehot, axis=1) - onehot
     slot_ids = jnp.sum(earlier * onehot, axis=-1).reshape(steps_total, local_rows, TOPK)
-    slot_span = steps_total * capacity
     columns = (
         routes * slot_span
         + jnp.arange(steps_total, dtype=jnp.int32)[:, None, None] * capacity
         + slot_ids
     )
-    column_marks = columns[..., None] == jnp.arange(experts * slot_span, dtype=jnp.int32)
-    dispatch = jnp.any(column_marks, axis=2).astype(jnp.bfloat16)
-    picker = column_marks.astype(jnp.bfloat16)
-    dispatch, picker = (dispatch, picker)
-    outgoing = jnp.einsum(
-        "src,srd->cd", dispatch, normed, preferred_element_type=jnp.float32
-    ).astype(jnp.bfloat16)
-    outgoing = outgoing.reshape(experts, slot_span, model_width)
-    received = lax.all_to_all(outgoing, "expert", split_axis=0, concat_axis=0, tiled=True)
-    slots_here = received.shape[1]
-    grouped = received.reshape(peers, experts_local, slots_here, model_width)
-    gate_act = jnp.einsum("pecd,edf->pecf", grouped, gate_full, preferred_element_type=jnp.float32)
-    up_act = jnp.einsum("pecd,edf->pecf", grouped, up_full, preferred_element_type=jnp.float32)
-    inner_act = (jax.nn.silu(gate_act) * up_act).astype(jnp.bfloat16)
-    inner_act = inner_act.reshape(peers * experts_local, slots_here, hidden_width)
-    returned = lax.all_to_all(inner_act, "expert", split_axis=0, concat_axis=0, tiled=True)
-    back_rows = returned.reshape(experts * slot_span, hidden_width)
+    picker = (columns[..., None] == jnp.arange(experts * slot_span, dtype=jnp.int32)).astype(
+        jnp.bfloat16
+    )
     picked = jnp.einsum("srkc,cf->srkf", picker, back_rows, preferred_element_type=jnp.float32)
     moe_hidden = (
         (picked * mixing[..., None])

time: 294 us -> 175 us (0.60)
  waiting for transfers between devices: 204 us -> 57.7 us
  Pallas kernels: 0 us -> 39.7 us
  matrix products: 49 us -> 10.2 us
  starting transfers between devices: 10.6 us -> 24.1 us
  blocking collectives: 0 us -> 10.4 us
    all_to_all x1, waiting for transfers between devices: 186 us -> 17.8 us  [per_device(): lax.all_to_all(outgoing, 'expert', split_axis=0, concat_axis=0, tiled=True)]
    ppermute x0 -> x15, waiting for transfers between devices: none -> 39.9 us  [per_device(): lax.ppermute(array, 'expert', moves(peers, target))]
    pallas_call x0 -> x7, Pallas kernels: none -> 39.7 us  [the longest x2 24.9 us: run_experts(): pl.pallas_call(lambda *refs: expert_kernel(*refs, pairs=pairs, kept=kept,...]
    dot_general x3 -> x1, matrix products: 40.1 us -> 2.49 us  [per_device(): jnp.dot(row_marks, computed, preferred_element_type=jnp.float32)]
    all_to_all x1 -> x0, waiting for transfers between devices: 18.5 us -> none  [per_device(): lax.all_to_all(inner_act, 'expert', split_axis=0, concat_axis=0, tiled=True)]
    ppermute x0 -> x15, starting transfers between devices: none -> 17.6 us  [per_device(): lax.ppermute(array, 'expert', moves(peers, target))]
    reshape x3, local copies, waits for them, and re-layouts: 11.9 us -> 0.31 us  [the longest x2 0.17 us: per_device(): routes.reshape(block_rows, TOPK)]
    all_gather x0 -> x4, blocking collectives: none -> 10.4 us  [per_device(): pair = lax.all_gather(own, 'expert', axis_index_groups=sides, tiled=True)]
  transfers between devices with their start and end apart: 2 -> 16, of which waited for: 2 -> 8; matrix products, arithmetic and copies ran while one was open for 7% -> 16% of each run, Pallas kernels for 0% -> 15%
where the time goes in v1:
time: 175 us; the launch traced here: 174 us
  waiting for transfers between devices  57.7 us (33%)
  Pallas kernels  39.7 us (23%)
  local copies, waits for them, and re-layouts  25.7 us (15%)
  starting transfers between devices  24.1 us (14%)
  blocking collectives  10.4 us (6%)
  matrix products  10.2 us (6%)
  other arithmetic  5.51 us (3%)
    ppermute x15, waiting for transfers between devices, per_device(): lax.ppermute(array, 'expert', moves(peers, target))  39.9 us
    pallas_call x2, Pallas kernels, run_experts(): pl.pallas_call(lambda *refs: expert_kernel(*refs, pairs=pairs, kept=kept,...  24.9 us
    all_to_all x1, waiting for transfers between devices, per_device(): lax.all_to_all(outgoing, 'expert', split_axis=0, concat_axis=0, tiled=True)  17.8 us
    ppermute x15, starting transfers between devices, per_device(): lax.ppermute(array, 'expert', moves(peers, target))  17.6 us
    pallas_call x4, Pallas kernels, per_device(): pick(pair, near, far, jnp.asarray(same, jnp.float32), wanted_expert, want...  13.2 us
    all_gather x4, blocking collectives, per_device(): pair = lax.all_gather(own, 'expert', axis_index_groups=sides, tiled=True)  10.4 us
    unnamed x55, local copies, waits for them, and re-layouts  7.76 us
    all_to_all x1, starting transfers between devices, per_device(): lax.all_to_all(outgoing, 'expert', split_axis=0, concat_axis=0, tiled=True)  6.53 us
  transfers between devices with their start and end apart: 16, of which 8 were waited for; matrix products, arithmetic and copies ran while one was open for 16% of the time, Pallas kernels for 15%

profile of v1, /device:TPU:0, one launch (start us, length us, event | category | flops | bytes accessed | tf_op | source)
XLA Modules:
  0.0 174.4 jit_solution(11506475944359892562)
XLA Ops:
  0.7 1.3 copy.34
  2.0 0.1 reshape.252.refs_0_
  2.3 1.5 prepare.1
  3.8 3.0 %collective-permute-start.3 = (bf16[56,4224]{1,0:T(8,128)(2,1)}, bf16[56,4224]{1,0:T(8,128)(2,1)S(1)}, u32[]{:S(2)}, u32[]{:S(2)}) collective-permute-start(bf16[56,4224]{1,0:T(8,128)(2,1)} %prepare.1), channel_id=1, source_target_pairs={{0,8},{1,9},{2,10},{3,11},{4,12},{5,13},{6,14},{7,15},{8,0},{9,1},... | collective-permute-start | bytes 1419272 | tf_op jit(solution)/shard_map/ppermute | solution.py:230
  6.9 2.7 %all_gather.14.own_ref = bf16[112,4224]{1,0:T(8,128)(2,1)S(1)} all-gather(bf16[56,4224]{1,0:T(8,128)(2,1)} %prepare.1), channel_id=1, replica_groups={{0,1},{2,3},{4,5},{6,7},{8,9},{10,11},{12,13},{14,15},{16,17},{18,19},{..., dimensions={0}, use_global_device_ids=true | all-gather | bytes 1419264 | tf_op jit(solution)/shard_map/all_gather | solution.py:274
  9.5 1.5 collective-permute-start
  11.0 2.6 %collective-permute-start.7 = (bf16[56,4224]{1,0:T(8,128)(2,1)}, bf16[56,4224]{1,0:T(8,128)(2,1)S(1)}, u32[]{:S(2)}, u32[]{:S(2)}) collective-permute-start(bf16[56,4224]{1,0:T(8,128)(2,1)} %prepare.1), channel_id=1, source_target_pairs={{0,16},{1,17},{2,18},{3,19},{4,20},{5,21},{6,22},{7,23},{8,24},{9,... | collective-permute-start | bytes 1419272 | tf_op jit(solution)/shard_map/ppermute | solution.py:230
  13.7 0.7 eq.89
  14.4 9.0 %collective-permute-done.3 = bf16[56,4224]{1,0:T(8,128)(2,1)S(1)} collective-permute-done((bf16[56,4224]{1,0:T(8,128)(2,1)}, bf16[56,4224]{1,0:T(8,128)(2,1)S(1)}, u32[]{:S(2)}, u32[]{:S(2)}) %collective-permute-start.3) | collective-permute-done | bytes 473120 | tf_op jit(solution)/shard_map/ppermute | solution.py:230
  23.4 2.5 %all_gather.15.own_ref = bf16[112,4224]{1,0:T(8,128)(2,1)S(1)} all-gather(bf16[56,4224]{1,0:T(8,128)(2,1)S(1)} %collective-permute-done.3), channel_id=1, replica_groups={{0,1},{2,3},{4,5},{6,7},{8,9},{10,11},{12,13},{14,15},{16,17},{18,19},{..., dimensions={0}, use_global_device_ids=true | all-gather | bytes 1419264 | tf_op jit(solution)/shard_map/all_gather | solution.py:274
  25.9 1.7 collective-permute-start.4
  27.5 7.4 %collective-permute-done.7 = bf16[56,4224]{1,0:T(8,128)(2,1)S(1)} collective-permute-done((bf16[56,4224]{1,0:T(8,128)(2,1)}, bf16[56,4224]{1,0:T(8,128)(2,1)S(1)}, u32[]{:S(2)}, u32[]{:S(2)}) %collective-permute-start.7) | collective-permute-done | bytes 473120 | tf_op jit(solution)/shard_map/ppermute | solution.py:230
  35.0 0.8 copy-done.19
  35.7 2.5 %collective-permute-start.11 = (bf16[56,4224]{1,0:T(8,128)(2,1)}, bf16[56,4224]{1,0:T(8,128)(2,1)S(1)}, u32[]{:S(2)}, u32[]{:S(2)}) collective-permute-start(bf16[56,4224]{1,0:T(8,128)(2,1)} %prepare.1), channel_id=1, source_target_pairs={{0,24},{1,25},{2,26},{3,27},{4,28},{5,29},{6,30},{7,31},{8,16},{9,... | collective-permute-start | bytes 1419272 | tf_op jit(solution)/shard_map/ppermute | solution.py:230
  38.2 2.7 %all_gather.16.own_ref = bf16[112,4224]{1,0:T(8,128)(2,1)S(1)} all-gather(bf16[56,4224]{1,0:T(8,128)(2,1)} %copy-done.19), channel_id=1, replica_groups={{0,1},{2,3},{4,5},{6,7},{8,9},{10,11},{12,13},{14,15},{16,17},{18,19},{..., dimensions={0}, use_global_device_ids=true | all-gather | bytes 1419264 | tf_op jit(solution)/shard_map/all_gather | solution.py:274
  40.9 1.5 collective-permute-start.8
  42.4 0.6 collective-permute-start.1
  43.0 0.3 copy-done.6
  43.3 6.3 %collective-permute-done.11 = bf16[56,4224]{1,0:T(8,128)(2,1)S(1)} collective-permute-done((bf16[56,4224]{1,0:T(8,128)(2,1)}, bf16[56,4224]{1,0:T(8,128)(2,1)S(1)}, u32[]{:S(2)}, u32[]{:S(2)}) %collective-permute-start.11) | collective-permute-done | bytes 473120 | tf_op jit(solution)/shard_map/ppermute | solution.py:230
  49.6 2.6 %all_gather.17.own_ref = bf16[112,4224]{1,0:T(8,128)(2,1)S(1)} all-gather(bf16[56,4224]{1,0:T(8,128)(2,1)S(1)} %collective-permute-done.11), channel_id=1, replica_groups={{0,1},{2,3},{4,5},{6,7},{8,9},{10,11},{12,13},{14,15},{16,17},{18,19},{..., dimensions={0}, use_global_device_ids=true | all-gather | bytes 1419264 | tf_op jit(solution)/shard_map/all_gather | solution.py:274
  52.2 2.4 %collective-permute-start.12 = (bf16[112,4224]{1,0:T(8,128)(2,1)S(1)}, bf16[112,4224]{1,0:T(8,128)(2,1)S(1)}, u32[]{:S(2)}, u32[]{:S(2)}) collective-permute-start(bf16[112,4224]{1,0:T(8,128)(2,1)S(1)} %all_gather.17.own_ref), channel_id=1, source_target_pairs={{0,2},{1,5},{2,0},{3,7},{4,6},{5,1},{6,4},{7,3},{8,10},{9,13},{10,... | collective-permute-start | bytes 2838536 | tf_op jit(solution)/shard_map/ppermute | solution.py:230
  54.8 1.5 collective-permute-done.1.far_ref
  56.3 2.9 %pick.4 = (bf16[128,4096]{1,0:T(8,128)(2,1)S(1)}, bf16[96,4096]{1,0:T(8,128)(2,1)}) custom-call(bf16[112,4224]{1,0:T(8,128)(2,1)S(1)} %all_gather.14.own_ref, bf16[112,4224]{1,0:T(8,128)(2,1)S(1)} %copy-done.7, bf16[56,4224]{1,0:T(8,128)(2,1)S(1)} %collective-permute-done.1.far_ref, f32[280,224]{1,0:T(8,128)S(1)} %copy-done.1, f32[1,224]{1,0:T(1,128)S(1)} %bitcast.56, ...), custom_call_target="tpu_custom_call" | custom-call | tf_op jit(solution)/shard_map/pick/pallas_call | solution.py:278
  59.1 1.0 copy-done.8
  60.1 3.0 %collective-permute-done.8.near_ref = bf16[112,4224]{1,0:T(8,128)(2,1)S(1)} collective-permute-done((bf16[112,4224]{1,0:T(8,128)(2,1)S(1)}, bf16[112,4224]{1,0:T(8,128)(2,1)S(1)}, u32[]{:S(2)}, u32[]{:S(2)}) %collective-permute-start.8) | collective-permute-done | bytes 946208 | tf_op jit(solution)/shard_map/ppermute | solution.py:230
  63.1 0.9 constant_dynamic-slice_fusion
  63.9 0.3 collective-permute-start.9
  64.2 4.3 %collective-permute-done.5.far_ref = bf16[56,4224]{1,0:T(8,128)(2,1)S(1)} collective-permute-done((bf16[56,4224]{1,0:T(8,128)(2,1)S(1)}, bf16[56,4224]{1,0:T(8,128)(2,1)S(1)}, u32[]{:S(2)}, u32[]{:S(2)}) %collective-permute-start.5) | collective-permute-done | bytes 473120 | tf_op jit(solution)/shard_map/ppermute | solution.py:230
  68.5 2.8 %pick.5 = (bf16[128,4096]{1,0:T(8,128)(2,1)S(1)}, bf16[96,4096]{1,0:T(8,128)(2,1)}) custom-call(bf16[112,4224]{1,0:T(8,128)(2,1)S(1)} %all_gather.15.own_ref, bf16[112,4224]{1,0:T(8,128)(2,1)S(1)} %collective-permute-done.4.near_ref, bf16[56,4224]{1,0:T(8,128)(2,1)S(1)} %collective-permute-done.5.far_ref, f32[280,224]{1,0:T(8,128)S(1)} %copy-done.1, ...), custom_call_target="tpu_custom_call" | custom-call | tf_op jit(solution)/shard_map/pick/pallas_call | solution.py:278
  71.3 8.4 %collective-permute-done.12.near_ref = bf16[112,4224]{1,0:T(8,128)(2,1)S(1)} collective-permute-done((bf16[112,4224]{1,0:T(8,128)(2,1)S(1)}, bf16[112,4224]{1,0:T(8,128)(2,1)S(1)}, u32[]{:S(2)}, u32[]{:S(2)}) %collective-permute-start.12) | collective-permute-done | bytes 946208 | tf_op jit(solution)/shard_map/ppermute | solution.py:230
  79.7 0.9 constant_dynamic-slice_fusion.3
  80.6 1.0 collective-permute-start.13
  81.6 0.1 fusion.32
  81.8 0.9 reduce_window_sum.11
  82.7 0.7 reduce_sum.37
  83.4 1.2 select_reduce_fusion
  84.6 0.7 broadcast_divide_fusion
  85.4 1.2 copy-done.3
  86.5 3.8 %pick.6 = (bf16[128,4096]{1,0:T(8,128)(2,1)S(1)}, bf16[96,4096]{1,0:T(8,128)(2,1)}) custom-call(bf16[112,4224]{1,0:T(8,128)(2,1)S(1)} %all_gather.16.own_ref, bf16[112,4224]{1,0:T(8,128)(2,1)S(1)} %copy-done.3, bf16[56,4224]{1,0:T(8,128)(2,1)} %collective-permute-done.9.far_ref, f32[280,224]{1,0:T(8,128)S(1)} %copy-done.1, f32[1,224]{1,0:T(1,128)S(1)} %bitcast.58, ...), custom_call_target="tpu_custom_call" | custom-call | tf_op jit(solution)/shard_map/pick/pallas_call | solution.py:278
  90.4 1.0 copy-done.10
  91.4 3.8 %pick.7 = (bf16[128,4096]{1,0:T(8,128)(2,1)S(1)}, bf16[96,4096]{1,0:T(8,128)(2,1)}) custom-call(bf16[112,4224]{1,0:T(8,128)(2,1)S(1)} %all_gather.17.own_ref, bf16[112,4224]{1,0:T(8,128)(2,1)S(1)} %copy-done.5, bf16[56,4224]{1,0:T(8,128)(2,1)} %collective-permute-done.13.far_ref, f32[280,224]{1,0:T(8,128)S(1)} %copy-done.1, f32[1,224]{1,0:T(1,128)S(1)} %bitcast.59, ...), custom_call_target="tpu_custom_call" | custom-call | tf_op jit(solution)/shard_map/pick/pallas_call | solution.py:278
  95.2 1.0 copy-done.12
  96.2 0.5 collective-permute-start.14
  96.8 0.1 copy.37
  96.9 3.2 %reshape.259 = bf16[4,14,4,16,128]{4,3,2,0,1:T(8,128)(2,1)} reshape(bf16[4,14,8192]{2,0,1:T(4,128)(2,1)} %param.24) | data formatting | bytes 1835008 | tf_op jit(solution)/shard_map/reshape | solution.py:24
  100.1 4.2 %reshape.258 = bf16[14,128,4,128]{3,2,1,0:T(4,128)(2,1)} reshape(bf16[14,128,512]{2,1,0:T(8,128)(2,1)} %param.27) | data formatting | bytes 3670016 | tf_op jit(solution)/shard_map/reshape | solution.py:26
  104.3 4.3 %reshape.261 = bf16[14,128,4,128]{3,2,1,0:T(4,128)(2,1)} reshape(bf16[14,128,512]{2,1,0:T(8,128)(2,1)} %param.28) | data formatting | bytes 3670016 | tf_op jit(solution)/shard_map/reshape | solution.py:27
  108.8 12.6 %experts.2 = bf16[2,224,768]{2,1,0:T(8,128)(2,1)S(1)} custom-call(bf16[128,4096]{1,0:T(8,128)(2,1)S(1)} %copy-done.9, bf16[96,4096]{1,0:T(8,128)(2,1)} %collective-permute-done.2.refs_1_, bf16[128,4096]{1,0:T(8,128)(2,1)S(1)} %get-tuple-element.14.refs_2_, bf16[96,4096]{1,0:T(8,128)(2,1)} %collective-permute-done.6.refs_3_, bf16[2,4096,768]{2,1,0:T(8,128)(2,1)} %refs_4_.1, ...), custom_call_target="tpu_custom_call" | custom-call | flops 5637144576 | bytes 25165824 | tf_op jit(solution)/shard_map/experts/pallas_call | solution.py:184
  121.5 12.3 %experts.3 = bf16[2,224,768]{2,1,0:T(8,128)(2,1)S(1)} custom-call(bf16[128,4096]{1,0:T(8,128)(2,1)S(1)} %copy-done.11, bf16[96,4096]{1,0:T(8,128)(2,1)} %collective-permute-done.10.refs_1_, bf16[128,4096]{1,0:T(8,128)(2,1)S(1)} %copy-done.13, bf16[96,4096]{1,0:T(8,128)(2,1)S(1)} %collective-permute-done.14.refs_3_, bf16[2,4096,768]{2,1,0:T(8,128)(2,1)} %refs_4_.1, ...), custom_call_target="tpu_custom_call" | custom-call | flops 5637144576 | bytes 25165824 | tf_op jit(solution)/shard_map/experts/pallas_call | solution.py:184
  133.8 2.5 %fusion.8 = bf16[768,768]{1,0:T(8,128)(2,1)} fusion(bf16[448,768]{1,0:T(8,128)(2,1)S(1)} %bitcast.55, bf16[448,768]{1,0:T(8,128)(2,1)S(1)} %bitcast.54, s32[768]{0:T(1024)S(1)} %fusion.46), kind=kOutput, calls=%fused_computation.12 | convolution fusion | flops 1060995072 | bytes 2558976 | tf_op jit(solution)/shard_map/dot_general | solution.py:310
  136.3 6.5 %all-to-all-start = ((bf16[32,24,768]{2,1,0:T(8,128)(2,1)}), bf16[32,24,768]{2,1,0:T(8,128)(2,1)S(1)}, u32[]{:S(2)}, u32[]{:S(2)}) async-start(bf16[32,24,768]{2,1,0:T(8,128)(2,1)} %bitcast.63), calls=%async_computation | async-start | bytes 2359296 | tf_op jit(solution)/shard_map/all_to_all | solution.py:312
  142.8 3.5 %fusion.65 = (f32[4,14,4,16]{3,0,2,1:T(4,128)S(1)}, f32[4,14,4,16,4]{3,4,0,2,1:T(4,128)S(1)}) fusion(bf16[4,14,4,16,128]{4,3,2,0,1:T(8,128)(2,1)} %reshape.259, bf16[4,14,512]{2,0,1:T(4,128)(2,1)S(1)} %copy-done.25, pred[4,4]{1,0:T(4,128)(4,1)S(1)} %iota_compare_fusion.10), kind=kOutput, calls=%fused_computation.119 | convolution fusion | flops 3709440 | bytes 1046544 | tf_op jit(solution)/shard_map/srghd,jrgd->srghj/dot_general | solution.py:44
  146.4 1.5 bitcast_reduce_fusion
  147.9 0.4 fusion.28
  148.3 1.1 fusion.9
  149.5 0.5 fusion.29
  150.1 1.0 copy-done.16
  151.0 1.4 fusion.15
  152.4 0.2 copy.45
  152.6 1.1 reshape.263
  153.9 17.8 %all-to-all-done = bf16[32,24,768]{2,1,0:T(8,128)(2,1)S(1)} async-done(((bf16[32,24,768]{2,1,0:T(8,128)(2,1)}), bf16[32,24,768]{2,1,0:T(8,128)(2,1)S(1)}, u32[]{:S(2)}, u32[]{:S(2)}) %all-to-all-start) | async-done | bytes 1179680 | tf_op jit(solution)/shard_map/all_to_all | solution.py:312
  171.7 0.8 fusion.14
  172.4 0.5 reshape.269
  173.0 1.4 copy.51
  (72 shorter events, 0.9 us)
Async XLA Ops:
  0.6 148.9 %copy-start = (bf16[4,14,512]{2,0,1:T(4,128)(2,1)S(1)}, bf16[4,14,512]{2,0,1:T(4,128)(2,1)}, u32[]{:S(2)}) copy-start(bf16[4,14,512]{2,0,1:T(4,128)(2,1)} %param.26) | copy-start | bytes 172036
  0.6 1.7 copy-start.15
  0.7 1.5 copy-start.20
  2.0 12.4 %copy-start.22 = (s32[224]{0:T(256)S(1)}, s32[224]{0:T(256)}, u32[]{:S(2)}) copy-start(s32[224]{0:T(256)} %constant.170.clone) | copy-start | bytes 2692
  2.0 12.4 %copy-start.24 = (pred[224]{0:T(512)(128)(4,1)S(1)}, pred[224]{0:T(512)(128)(4,1)}, u32[]{:S(2)}) copy-start(pred[224]{0:T(512)(128)(4,1)} %constant.169.clone) | copy-start | bytes 676
  3.8 19.6 %collective-permute-start.3 = (bf16[56,4224]{1,0:T(8,128)(2,1)}, bf16[56,4224]{1,0:T(8,128)(2,1)S(1)}, u32[]{:S(2)}, u32[]{:S(2)}) collective-permute-start(bf16[56,4224]{1,0:T(8,128)(2,1)} %prepare.1), channel_id=1, source_target_pairs={{0,8},{1,9},{2,10},{3,11},{4,12},{5,13},{6,14},{7,15},{8,0},{9,1},... | collective-permute-start | bytes 1419272 | tf_op jit(solution)/shard_map/ppermute | solution.py:230
  9.5 32.8 %collective-permute-start = (bf16[112,4224]{1,0:T(8,128)(2,1)S(1)}, bf16[112,4224]{1,0:T(8,128)(2,1)S(1)}, u32[]{:S(2)}, u32[]{:S(2)}) collective-permute-start(bf16[112,4224]{1,0:T(8,128)(2,1)S(1)} %all_gather.14.own_ref), channel_id=1, source_target_pairs={{0,2},{1,5},{2,0},{3,7},{4,6},{5,1},{6,4},{7,3},{8,10},{9,13},{10,... | collective-permute-start | bytes 2838536 | tf_op jit(solution)/shard_map/ppermute | solution.py:230
  11.0 23.9 %collective-permute-start.7 = (bf16[56,4224]{1,0:T(8,128)(2,1)}, bf16[56,4224]{1,0:T(8,128)(2,1)S(1)}, u32[]{:S(2)}, u32[]{:S(2)}) collective-permute-start(bf16[56,4224]{1,0:T(8,128)(2,1)} %prepare.1), channel_id=1, source_target_pairs={{0,16},{1,17},{2,18},{3,19},{4,20},{5,21},{6,22},{7,23},{8,24},{9,... | collective-permute-start | bytes 1419272 | tf_op jit(solution)/shard_map/ppermute | solution.py:230
  25.9 28.8 %collective-permute-start.4 = (bf16[112,4224]{1,0:T(8,128)(2,1)S(1)}, bf16[112,4224]{1,0:T(8,128)(2,1)S(1)}, u32[]{:S(2)}, u32[]{:S(2)}) collective-permute-start(bf16[112,4224]{1,0:T(8,128)(2,1)S(1)} %all_gather.15.own_ref), channel_id=1, source_target_pairs={{0,2},{1,5},{2,0},{3,7},{4,6},{5,1},{6,4},{7,3},{8,10},{9,13},{10,... | collective-permute-start | bytes 2838536 | tf_op jit(solution)/shard_map/ppermute | solution.py:230
  35.0 0.8 copy-start.19
  35.7 13.9 %collective-permute-start.11 = (bf16[56,4224]{1,0:T(8,128)(2,1)}, bf16[56,4224]{1,0:T(8,128)(2,1)S(1)}, u32[]{:S(2)}, u32[]{:S(2)}) collective-permute-start(bf16[56,4224]{1,0:T(8,128)(2,1)} %prepare.1), channel_id=1, source_target_pairs={{0,24},{1,25},{2,26},{3,27},{4,28},{5,29},{6,30},{7,31},{8,16},{9,... | collective-permute-start | bytes 1419272 | tf_op jit(solution)/shard_map/ppermute | solution.py:230
  40.9 15.4 %copy-start.1 = (f32[280,224]{1,0:T(8,128)S(1)}, f32[280,224]{1,0:T(8,128)}, u32[]{:S(2)}) copy-start(f32[280,224]{1,0:T(8,128)} %constant.172.clone.same_ref) | copy-start | bytes 752644
  40.9 15.4 %copy-start.14 = (f32[1,224]{1,0:T(1,128)S(1)}, f32[1,224]{1,0:T(1,128)}, u32[]{:S(2)}) copy-start(f32[1,224]{1,0:T(1,128)} %constant.184.slot_ref) | copy-start | bytes 2692
  40.9 22.2 %collective-permute-start.8 = (bf16[112,4224]{1,0:T(8,128)(2,1)S(1)}, bf16[112,4224]{1,0:T(8,128)(2,1)S(1)}, u32[]{:S(2)}, u32[]{:S(2)}) collective-permute-start(bf16[112,4224]{1,0:T(8,128)(2,1)S(1)} %all_gather.16.own_ref), channel_id=1, source_target_pairs={{0,2},{1,5},{2,0},{3,7},{4,6},{5,1},{6,4},{7,3},{8,10},{9,13},{10,... | collective-permute-start | bytes 2838536 | tf_op jit(solution)/shard_map/ppermute | solution.py:230
  42.4 1.0 copy-start.6
  42.4 13.8 %collective-permute-start.1 = (bf16[56,4224]{1,0:T(8,128)(2,1)S(1)}, bf16[56,4224]{1,0:T(8,128)(2,1)S(1)}, u32[]{:S(2)}, u32[]{:S(2)}) collective-permute-start(bf16[56,4224]{1,0:T(8,128)(2,1)S(1)} %constant_dynamic-slice_fusion.2), channel_id=1, source_target_pairs={{0,4},{1,3},{2,6},{3,1},{4,0},{5,7},{6,2},{7,5},{8,12},{9,11},{10,... | collective-permute-start | bytes 1419272 | tf_op jit(solution)/shard_map/ppermute | solution.py:230
  49.6 6.6 %copy-start.7 = (bf16[112,4224]{1,0:T(8,128)(2,1)S(1)}, bf16[112,4224]{1,0:T(8,128)(2,1)}, u32[]{:S(2)}) copy-start(bf16[112,4224]{1,0:T(8,128)(2,1)} %copy-done.6) | copy-start | bytes 2838532
  52.2 27.5 %collective-permute-start.12 = (bf16[112,4224]{1,0:T(8,128)(2,1)S(1)}, bf16[112,4224]{1,0:T(8,128)(2,1)S(1)}, u32[]{:S(2)}, u32[]{:S(2)}) collective-permute-start(bf16[112,4224]{1,0:T(8,128)(2,1)S(1)} %all_gather.17.own_ref), channel_id=1, source_target_pairs={{0,2},{1,5},{2,0},{3,7},{4,6},{5,1},{6,4},{7,3},{8,10},{9,13},{10,... | collective-permute-start | bytes 2838536 | tf_op jit(solution)/shard_map/ppermute | solution.py:230
  54.7 13.8 %collective-permute-start.5 = (bf16[56,4224]{1,0:T(8,128)(2,1)S(1)}, bf16[56,4224]{1,0:T(8,128)(2,1)S(1)}, u32[]{:S(2)}, u32[]{:S(2)}) collective-permute-start(bf16[56,4224]{1,0:T(8,128)(2,1)S(1)} %constant_dynamic-slice_fusion.1), channel_id=1, source_target_pairs={{0,4},{1,3},{2,6},{3,1},{4,0},{5,7},{6,2},{7,5},{8,12},{9,11},{10,... | collective-permute-start | bytes 1419272 | tf_op jit(solution)/shard_map/ppermute | solution.py:230
  59.1 1.0 copy-start.8
  60.1 48.7 %collective-permute-start.2 = (bf16[96,4096]{1,0:T(8,128)(2,1)}, bf16[96,4096]{1,0:T(8,128)(2,1)}, u32[]{:S(2)}, u32[]{:S(2)}) collective-permute-start(bf16[96,4096]{1,0:T(8,128)(2,1)} %get-tuple-element.13), channel_id=1, source_target_pairs={{0,1},{1,0},{2,3},{3,2},{4,5},{5,4},{6,7},{7,6},{8,9},{9,8},{10,11... | collective-permute-start | bytes 2359304 | tf_op jit(solution)/shard_map/ppermute | solution.py:230
  63.1 17.5 %copy-start.2 = (bf16[112,4224]{1,0:T(8,128)(2,1)}, bf16[112,4224]{1,0:T(8,128)(2,1)S(1)}, u32[]{:S(2)}) copy-start(bf16[112,4224]{1,0:T(8,128)(2,1)S(1)} %collective-permute-done.8.near_ref) | copy-start | bytes 2838532
  63.9 17.7 %copy-start.21 = (s32[4,112]{1,0:T(4,128)S(1)}, s32[4,112]{1,0:T(4,128)}, u32[]{:S(2)}) copy-start(s32[4,112]{1,0:T(4,128)} %eq.89) | copy-start | bytes 5380
  63.9 21.4 %collective-permute-start.9 = (bf16[56,4224]{1,0:T(8,128)(2,1)}, bf16[56,4224]{1,0:T(8,128)(2,1)}, u32[]{:S(2)}, u32[]{:S(2)}) collective-permute-start(bf16[56,4224]{1,0:T(8,128)(2,1)} %constant_dynamic-slice_fusion), channel_id=1, source_target_pairs={{0,4},{1,3},{2,6},{3,1},{4,0},{5,7},{6,2},{7,5},{8,12},{9,11},{10,... | collective-permute-start | bytes 1419272 | tf_op jit(solution)/shard_map/ppermute | solution.py:230
  71.3 37.5 %collective-permute-start.6 = (bf16[96,4096]{1,0:T(8,128)(2,1)}, bf16[96,4096]{1,0:T(8,128)(2,1)}, u32[]{:S(2)}, u32[]{:S(2)}) collective-permute-start(bf16[96,4096]{1,0:T(8,128)(2,1)} %get-tuple-element.15), channel_id=1, source_target_pairs={{0,1},{1,0},{2,3},{3,2},{4,5},{5,4},{6,7},{7,6},{8,9},{9,8},{10,11... | collective-permute-start | bytes 2359304 | tf_op jit(solution)/shard_map/ppermute | solution.py:230
  79.7 1.9 %copy-start.4 = (bf16[112,4224]{1,0:T(8,128)(2,1)}, bf16[112,4224]{1,0:T(8,128)(2,1)S(1)}, u32[]{:S(2)}) copy-start(bf16[112,4224]{1,0:T(8,128)(2,1)S(1)} %collective-permute-done.12.near_ref) | copy-start | bytes 2838532
  80.6 10.8 %collective-permute-start.13 = (bf16[56,4224]{1,0:T(8,128)(2,1)}, bf16[56,4224]{1,0:T(8,128)(2,1)}, u32[]{:S(2)}, u32[]{:S(2)}) collective-permute-start(bf16[56,4224]{1,0:T(8,128)(2,1)} %constant_dynamic-slice_fusion.3), channel_id=1, source_target_pairs={{0,4},{1,3},{2,6},{3,1},{4,0},{5,7},{6,2},{7,5},{8,12},{9,11},{10,... | collective-permute-start | bytes 1419272 | tf_op jit(solution)/shard_map/ppermute | solution.py:230
  85.3 1.2 copy-start.3
  86.5 4.9 %copy-start.5 = (bf16[112,4224]{1,0:T(8,128)(2,1)S(1)}, bf16[112,4224]{1,0:T(8,128)(2,1)}, u32[]{:S(2)}) copy-start(bf16[112,4224]{1,0:T(8,128)(2,1)} %copy-done.4) | copy-start | bytes 2838532
  90.4 1.0 copy-start.10
  91.4 30.0 %collective-permute-start.10 = (bf16[96,4096]{1,0:T(8,128)(2,1)}, bf16[96,4096]{1,0:T(8,128)(2,1)}, u32[]{:S(2)}, u32[]{:S(2)}) collective-permute-start(bf16[96,4096]{1,0:T(8,128)(2,1)} %get-tuple-element.18), channel_id=1, source_target_pairs={{0,1},{1,0},{2,3},{3,2},{4,5},{5,4},{6,7},{7,6},{8,9},{9,8},{10,11... | collective-permute-start | bytes 2359304 | tf_op jit(solution)/shard_map/ppermute | solution.py:230
  95.2 1.0 copy-start.12
  96.2 25.3 %collective-permute-start.14 = (bf16[96,4096]{1,0:T(8,128)(2,1)}, bf16[96,4096]{1,0:T(8,128)(2,1)S(1)}, u32[]{:S(2)}, u32[]{:S(2)}) collective-permute-start(bf16[96,4096]{1,0:T(8,128)(2,1)} %get-tuple-element.21), channel_id=1, source_target_pairs={{0,1},{1,0},{2,3},{3,2},{4,5},{5,4},{6,7},{7,6},{8,9},{9,8},{10,11... | collective-permute-start | bytes 2359304 | tf_op jit(solution)/shard_map/ppermute | solution.py:230
  104.3 4.3 %copy-start.23 = (s32[14]{0:T(128)S(1)}, s32[14]{0:T(128)}, u32[]{:S(2)}) copy-start(s32[14]{0:T(128)} %param.29) | copy-start | bytes 172
  104.3 4.4 %copy-start.9 = (bf16[128,4096]{1,0:T(8,128)(2,1)S(1)}, bf16[128,4096]{1,0:T(8,128)(2,1)}, u32[]{:S(2)}) copy-start(bf16[128,4096]{1,0:T(8,128)(2,1)} %copy-done.8) | copy-start | bytes 3145732
  108.8 12.7 %copy-start.11 = (bf16[128,4096]{1,0:T(8,128)(2,1)S(1)}, bf16[128,4096]{1,0:T(8,128)(2,1)}, u32[]{:S(2)}) copy-start(bf16[128,4096]{1,0:T(8,128)(2,1)} %copy-done.10) | copy-start | bytes 3145732
  108.8 12.7 %copy-start.13 = (bf16[128,4096]{1,0:T(8,128)(2,1)S(1)}, bf16[128,4096]{1,0:T(8,128)(2,1)}, u32[]{:S(2)}) copy-start(bf16[128,4096]{1,0:T(8,128)(2,1)} %copy-done.12) | copy-start | bytes 3145732
  136.3 6.6 %copy-start.25 = (bf16[4,14,512]{2,0,1:T(4,128)(2,1)S(1)}, bf16[4,14,512]{2,0,1:T(4,128)(2,1)}, u32[]{:S(2)}) copy-start(bf16[4,14,512]{2,0,1:T(4,128)(2,1)} %param.25) | copy-start | bytes 172036
  136.3 10.1 %copy-start.17 = (bf16[14,128,4,128]{3,2,1,0:T(4,128)(2,1)S(1)}, bf16[14,128,4,128]{3,2,1,0:T(4,128)(2,1)}, u32[]{:S(2)}) copy-start(bf16[14,128,4,128]{3,2,1,0:T(4,128)(2,1)} %reshape.258) | copy-start | bytes 5505028
  136.3 35.4 %all-to-all-start = ((bf16[32,24,768]{2,1,0:T(8,128)(2,1)}), bf16[32,24,768]{2,1,0:T(8,128)(2,1)S(1)}, u32[]{:S(2)}, u32[]{:S(2)}) async-start(bf16[32,24,768]{2,1,0:T(8,128)(2,1)} %bitcast.63), calls=%async_computation | async-start | bytes 2359296 | tf_op jit(solution)/shard_map/all_to_all | solution.py:312
  142.8 3.6 %copy-start.18 = (bf16[4,14,4,16,128]{4,3,2,0,1:T(8,128)(2,1)S(1)}, bf16[4,14,4,16,128]{4,3,2,0,1:T(8,128)(2,1)}, u32[]{:S(2)}) copy-start(bf16[4,14,4,16,128]{4,3,2,0,1:T(8,128)(2,1)} %reshape.259) | copy-start | bytes 2752516
  149.5 1.5 copy-start.16

commit v2 on v0

v2 whole, which is shorter than its diff:
```python
import functools
import math

import jax
import jax.numpy as jnp
import numpy as np
from jax import lax
from jax.experimental import pallas as pl
from jax.experimental.pallas import tpu as pltpu
from jax.sharding import PartitionSpec as P

HQ = 64
KVH = 4
HD = 128
TOPK = 8
LANES = 128
EDGE = 2
INNER = EDGE**3
VMEM_BYTES = 60 * 1024 * 1024


def attention_kernel(lengths_ref, q_ref, nk_ref, nv_ref, k_ref, v_ref, out_ref, *, groups):
    rows, steps, _ = q_ref.shape
    cache = k_ref.shape[1]
    extra = 16
    many = steps*groups
    scale = 1.0/math.sqrt(HD)
    shape = (cache+extra, 2*many)
    position = lax.broadcasted_iota(jnp.int32, shape, 0)
    step = lax.broadcasted_iota(jnp.int32, shape, 1) % steps
    first = pl.program_id(0)*rows
    pad = jnp.zeros((extra-steps, 2*HD), jnp.float32)
    none = jnp.zeros((many, HD), jnp.float32)
    for r in range(rows):
        limit = jnp.where(position < cache, lengths_ref[first + r], step + (cache + 1))
        valid = position < limit
        for pair in range(KVH//2):
            wide = pl.ds(pair*2*HD, 2*HD)
            def with_new(cached, new):
                fresh = jnp.concatenate([new[r, :, wide].astype(jnp.float32), pad], axis=0)
                return jnp.concatenate([cached[r, :, wide], fresh.astype(jnp.bfloat16)], axis=0)
            heads = [q_ref[r, :, (pair*2*groups+h)*HD:(pair*2*groups+h+1)*HD].astype(jnp.float32) for h in range(2*groups)]
            low = jnp.concatenate(heads[:groups], axis=0)
            high = jnp.concatenate(heads[groups:], axis=0)
            asked = jnp.concatenate([jnp.concatenate([low, none], axis=1), jnp.concatenate([none, high], axis=1)], axis=0).astype(jnp.bfloat16)
            scores = lax.dot_general(with_new(k_ref, nk_ref), asked, (((1,),(1,)),((),())), preferred_element_type=jnp.float32)*scale
            scores = jnp.where(valid, scores, -jnp.inf)
            weights = jnp.exp(scores - jnp.max(scores, axis=0, keepdims=True))
            probs = (weights * (1.0/jnp.sum(weights, axis=0, keepdims=True))).astype(jnp.bfloat16)
            mixed = lax.dot_general(probs, with_new(v_ref, nv_ref), (((0,),(0,)),((),())), preferred_element_type=jnp.float32)
            for h in range(2*groups):
                at = h//groups*HD
                out_ref[r, :, (pair*2*groups+h)*HD:(pair*2*groups+h+1)*HD] = mixed[h*steps:(h+1)*steps, at:at+HD].astype(out_ref.dtype)

def attention(queries,new_keys,new_values,cache_keys,cache_values,lengths):
    steps, rows, _ = queries.shape
    groups = HQ//KVH
    cache = cache_keys.shape[1]
    part = max(n for n in range(1,8) if rows % n == 0)
    turn = lambda a: jnp.swapaxes(a,0,1)
    spec = lambda a: pl.BlockSpec((part,)+a.shape[1:], lambda i:(i,0,0))
    arrays = (turn(queries), turn(new_keys), turn(new_values), cache_keys, cache_values)
    out= pl.pallas_call(
        functools.partial(attention_kernel, groups=groups),
        grid=(rows//part,),
        in_specs=[pl.BlockSpec(memory_space=pltpu.SMEM)]+[spec(a) for a in arrays],
        out_specs=spec(arrays[0]),
        out_shape=jax.ShapeDtypeStruct(arrays[0].shape, queries.dtype),
        compiler_params=pltpu.CompilerParams(vmem_limit_bytes=16 * 1024 * 1024),
        name="attention",
    )(lengths, *arrays)
    return turn(out)


def place(index):
    return index // INNER, index // 4 % EDGE, index // 2 % EDGE, index % EDGE


def device_at(line, row, column, side):
    return ((line * EDGE + row) * EDGE + column) * EDGE + side


def moves(peers, target):
    return [(index, device_at(*target(*place(index)))) for index in range(peers)]


def padded(rows):
    return -(-rows // 16) * 16


def prepare_kernel(states_ref, routes_ref, order_ref, payload_ref, columns_ref, *, capacity, experts):
    tokens, steps, width = states_ref.shape
    states = jnp.concatenate(
        [states_ref[token].astype(jnp.float32) for token in range(tokens)], axis=0
    )
    scale = lax.rsqrt(jnp.mean(states * states, axis=-1, keepdims=True) + 1e-06)
    payload_ref[:, :width] = (states * scale).astype(payload_ref.dtype)
    routes = routes_ref[...]
    rows = tokens * steps
    expert_ids = lax.broadcasted_iota(jnp.int32, (rows, experts), 1)
    marks = [
        (routes[:, choice : choice + 1] == expert_ids).astype(jnp.float32)
        for choice in range(TOPK)
    ]
    named = sum(marks)
    earlier = jnp.dot(
        order_ref[...], named.astype(jnp.bfloat16), preferred_element_type=jnp.float32
    )
    lane_ids = lax.broadcasted_iota(jnp.int32, (rows, LANES), 1)
    step = lax.broadcasted_iota(jnp.int32, (rows, 1), 0) % steps
    codes = jnp.zeros((rows, LANES), jnp.float32)
    columns = jnp.zeros((rows, LANES), jnp.int32)
    for choice in range(TOPK):
        slot = jnp.sum(earlier * marks[choice], axis=-1, keepdims=True)
        expert = routes[:, choice : choice + 1]
        code = expert.astype(jnp.float32) * capacity + slot
        codes = jnp.where(lane_ids == choice, code, codes)
        column = (expert * steps + step) * capacity + slot.astype(jnp.int32)
        columns = jnp.where(lane_ids == choice, column, columns)
    payload_ref[:, width:] = codes.astype(payload_ref.dtype)
    columns_ref[...] = columns


def prepare(states, routes, capacity, experts):
    tokens, steps, width = states.shape
    rows = tokens * steps
    numbers = np.arange(rows)
    order = (numbers[:, None] % steps == numbers[None, :] % steps) & (
        numbers[:, None] > numbers[None, :]
    )
    return pl.pallas_call(
        functools.partial(prepare_kernel, capacity=capacity, experts=experts),
        out_shape=(
            jax.ShapeDtypeStruct((rows, width + LANES), jnp.bfloat16),
            jax.ShapeDtypeStruct((rows, LANES), jnp.int32),
        ),
        compiler_params=pltpu.CompilerParams(vmem_limit_bytes=VMEM_BYTES),
        name="prepare",
    )(states, routes, jnp.asarray(order, jnp.bfloat16))


def pick_kernel(*refs, parts):
    sources, codes_refs = refs[:parts], refs[parts : 2 * parts]
    group_ref, wanted_ref, keep_ref, send_ref, onehot_ref = refs[2 * parts :]

    @pl.when(pl.program_id(0) == 0)
    def _():
        codes = jnp.concatenate([ref[...].astype(jnp.float32) for ref in codes_refs], axis=0).T
        wanted, group = wanted_ref[:, :1], group_ref[...]
        hits = jnp.zeros((wanted.shape[0], group.shape[1]), jnp.float32)
        for choice in range(TOPK):
            hits = jnp.where(codes[choice : choice + 1] + group == wanted, 1.0, hits)
        onehot_ref[...] = hits.astype(jnp.bfloat16)

    rows = jnp.concatenate([ref[...] for ref in sources], axis=0)
    kept = keep_ref.shape[0]
    picked = jnp.dot(onehot_ref[...], rows, preferred_element_type=jnp.float32)
    picked = picked.astype(keep_ref.dtype)
    keep_ref[...] = picked[:kept]
    send_ref[...] = picked[kept:]


def pick(sources, group, wanted, width):
    rows, slots = group.shape[1], wanted.shape[0]
    cuts = 2 if width % (2 * LANES) == 0 else 1
    block = width // cuts
    piece = lambda a: pl.BlockSpec((a.shape[0], block), lambda i: (0, i))
    codes = lambda a: pl.BlockSpec((a.shape[0], LANES), lambda i: (0, width // LANES))
    whole = lambda a: pl.BlockSpec(a.shape, lambda i: (0, 0))
    return pl.pallas_call(
        functools.partial(pick_kernel, parts=len(sources)),
        grid=(cuts,),
        in_specs=[piece(a) for a in sources]
        + [codes(a) for a in sources]
        + [whole(group), whole(wanted)],
        out_specs=[pl.BlockSpec((slots // 2, block), lambda i: (0, i))] * 2,
        out_shape=[jax.ShapeDtypeStruct((slots // 2, width), jnp.bfloat16)] * 2,
        scratch_shapes=[pltpu.VMEM((slots, rows), jnp.bfloat16)],
        compiler_params=pltpu.CompilerParams(vmem_limit_bytes=VMEM_BYTES),
        name="pick",
    )(*sources, *sources, group, wanted)


def expert_kernel(*refs, pairs, kept, sent, experts_local):
    x_refs, (place_ref, gate_ref, up_ref, out_ref, rows_ref) = refs[: 2 * pairs], refs[2 * pairs :]
    expert = pl.program_id(1)

    @pl.when(pl.program_id(0) == 0)
    def _():
        at = 0
        for number, x_ref in enumerate(x_refs):
            part = sent if number % 2 else kept
            rows_ref[expert, at : at + part, :] = x_ref[
                pl.ds(pl.multiple_of(expert * part, 16), part), :
            ]
            at += part

    rows = rows_ref[expert]
    gate = jnp.dot(rows, gate_ref[0], preferred_element_type=jnp.float32)
    up = jnp.dot(rows, up_ref[0], preferred_element_type=jnp.float32)
    inner = (gate / (1.0 + jnp.exp(-gate)) * up).astype(jnp.bfloat16)
    wanted = place_ref[...]
    base = expert * rows.shape[0]
    row_ids = lax.broadcasted_iota(jnp.int32, (wanted.shape[0], rows.shape[0]), 1) + base
    marks = (wanted == row_ids).astype(jnp.float32).astype(jnp.bfloat16)
    placed = jnp.dot(marks, inner, preferred_element_type=jnp.float32).astype(out_ref.dtype)

    @pl.when(expert == 0)
    def _():
        out_ref[...] = placed

    @pl.when(expert != 0)
    def _():
        out_ref[...] += placed


def run_experts(arrays, places, w_gate, w_up):
    experts_local, width, hidden = w_gate.shape
    kept, sent = arrays[0].shape[0] // experts_local, arrays[1].shape[0] // experts_local
    pairs = len(arrays) // 2
    rows = pairs * (kept + sent)
    block = 2 * LANES
    slots = places.shape[0]
    return pl.pallas_call(
        functools.partial(
            expert_kernel, pairs=pairs, kept=kept, sent=sent, experts_local=experts_local
        ),
        grid=(hidden // block, experts_local),
        in_specs=[pl.BlockSpec(a.shape, lambda f, e: (0, 0)) for a in arrays]
        + [pl.BlockSpec(places.shape, lambda f, e: (0, 0))]
        + [pl.BlockSpec((1, width, block), lambda f, e: (e, 0, f))] * 2,
        out_specs=pl.BlockSpec((slots, block), lambda f, e: (0, f)),
        out_shape=jax.ShapeDtypeStruct((slots, hidden), jnp.bfloat16),
        scratch_shapes=[pltpu.VMEM((experts_local, rows, width), jnp.bfloat16)],
        compiler_params=pltpu.CompilerParams(vmem_limit_bytes=VMEM_BYTES),
        name="experts",
    )(*arrays, places, w_gate, w_up)


def combine_kernel(back_ref, columns_ref, gates_ref, out_ref):
    tokens, steps, _ = out_ref.shape
    rows = tokens * steps
    slots, hidden = back_ref.shape
    gates = gates_ref[...]
    mixing = gates / jnp.sum(gates, axis=-1, keepdims=True)
    ids = lax.broadcasted_iota(jnp.int32, (rows, slots), 1)
    marks = [
        (columns_ref[:, choice : choice + 1] == ids).astype(jnp.float32) for choice in range(TOPK)
    ]
    picked = jnp.dot(
        jnp.concatenate(marks, axis=0).astype(jnp.bfloat16),
        back_ref[...],
        preferred_element_type=jnp.float32,
    )
    for choice in range(TOPK):
        scaled = picked[choice * rows : (choice + 1) * rows] * mixing[:, choice : choice + 1]
        scaled = scaled.astype(out_ref.dtype)
        for token in range(tokens):
            out_ref[token, :, choice * hidden : (choice + 1) * hidden] = scaled[
                token * steps : (token + 1) * steps
            ]


def combine(back, columns, gates, tokens, steps):
    return pl.pallas_call(
        combine_kernel,
        out_shape=jax.ShapeDtypeStruct((tokens, steps, TOPK * back.shape[1]), jnp.bfloat16),
        compiler_params=pltpu.CompilerParams(vmem_limit_bytes=12 * 1024 * 1024),
        name="combine",
    )(back, columns, gates)


def per_device(
    hidden_states,
    routes,
    gates,
    w_gate,
    w_up,
    queries,
    new_keys,
    new_values,
    cache_keys,
    cache_values,
    lengths,
):
    peers = lax.axis_size("expert")
    me = lax.axis_index("expert")
    lines = peers // INNER
    experts_local = w_gate.shape[0]
    experts = experts_local * peers
    steps_total, local_rows, model_width = hidden_states.shape
    capacity = local_rows * TOPK * 2 // experts
    slot_span = steps_total * capacity
    gate_full, up_full = (
        lax.all_gather(w_gate, "replica", axis=1, tiled=True),
        lax.all_gather(w_up, "replica", axis=1, tiled=True),
    )
    hidden_width = gate_full.shape[2]
    block_rows = steps_total * local_rows

    assert experts * capacity <= 256
    send = lambda array, target: lax.ppermute(array, "expert", moves(peers, target))
    to_line = lambda offset: lambda z, y, x, c: (z ^ offset, y, x, c)
    to_column = lambda z, y, x, c: (z, y, 1 - x, c)
    to_row = lambda z, y, x, c: (z, 1 - y, x, c)
    other_side = lambda z, y, x, c: (z, y, x, 1 - c)
    after = lambda array, *others: lax.optimization_barrier((array,) + others)[0]
    z, y, x, side = place(me)

    by_token = lambda a: jnp.swapaxes(a, 0, 1)
    payload, columns = prepare(
        by_token(hidden_states),
        by_token(routes).reshape(block_rows, TOPK),
        capacity,
        experts,
    )
    token = np.arange(4 * block_rows)
    group = (token // block_rows * steps_total + token % steps_total) * 256
    group = jnp.asarray(group, jnp.float32)[None]
    slots = np.arange(2 * experts_local * 4 * slot_span).reshape(
        2, experts_local, 4, steps_total, capacity
    )
    of_side, of_expert, of_block, of_step, of_slot = [
        number.reshape(-1) for number in np.indices(slots.shape)
    ]
    wanted_expert = jnp.where(of_side == 0, me, me ^ 1) * experts_local + of_expert
    wanted = wanted_expert * capacity + of_slot + (of_block * steps_total + of_step) * 256
    wanted = jnp.broadcast_to(wanted.astype(jnp.float32)[:, None], (slots.size, LANES))

    arrived = {0: payload}
    for offset in sorted(range(1, lines), key=lambda n: (n != 2, n)):
        source = after(payload, arrived[2]) if offset > 2 else payload
        arrived[offset] = send(source, to_line(offset))
    kept = 4 * slot_span
    numbers = jnp.arange(experts * slot_span, dtype=jnp.int32)
    owner, expert, rest = (
        numbers // (experts_local * slot_span),
        numbers // slot_span % experts_local,
        numbers % slot_span,
    )
    oz, oy, ox, oc = place(owner)
    within = jnp.where(oc == side, 0, kept) + ((oy ^ y) * 2 + (ox ^ x)) * slot_span + rest
    places = (expert * lines + (oz ^ z)) * 2 * kept + within

    blocks, cut = [], padded(block_rows // 2)
    hops, fars, keeps = [], [], []
    for offset in range(lines):
        own = arrived[offset]
        if offset == 1:
            own = after(own, *fars[0], places)
        elif offset > 2:
            own = after(own, *hops[offset - 2], keeps[0])
        column, row = send(own, to_column), send(own, to_row)
        hops.append((column, row))
        far = send(column[:cut], to_row), send(row[cut:], to_column)
        fars.append(far)
        keep, give = pick([own, column, row, *far], group, wanted, model_width)
        keeps.append(keep)
        blocks += [keep, send(give, other_side)]

    outgoing = run_experts(blocks, places[:, None], gate_full, up_full)
    outgoing = outgoing.reshape(peers, experts_local * slot_span, hidden_width)
    returned = lax.all_to_all(outgoing, "expert", split_axis=0, concat_axis=0, tiled=True)
    attn_out = attention(
        queries, new_keys, new_values, cache_keys, cache_values, after(lengths, outgoing)
    )
    back_rows = returned.reshape(experts * slot_span, hidden_width)
    moe_hidden = combine(
        back_rows, columns, by_token(gates).reshape(block_rows, TOPK), local_rows, steps_total
    )
    return (by_token(moe_hidden), attn_out)


def solution(mesh):
    in_specs = (
        P(None, ("replica", "expert"), None),
        P(None, ("replica", "expert"), None),
        P(None, ("replica", "expert"), None),
        P("expert", "replica", None),
        P("expert", "replica", None),
        P(None, ("replica", "expert"), None),
        P(None, ("replica", "expert"), None),
        P(None, ("replica", "expert"), None),
        P(("replica", "expert"), None, None),
        P(("replica", "expert"), None, None),
        P(("replica", "expert")),
    )
    out_specs = (P(None, ("replica", "expert"), None), P(None, ("replica", "expert"), None))
    return jax.shard_map(
        per_device, mesh=mesh, in_specs=in_specs, out_specs=out_specs, check_vma=False
    )
```

time: 294 us -> 149 us (0.51)
  waiting for transfers between devices: 204 us -> 57 us
  matrix products: 49 us -> 0 us
  Pallas kernels: 0 us -> 44.7 us
  starting transfers between devices: 10.6 us -> 30.2 us
  local copies, waits for them, and re-layouts: 24.1 us -> 12.7 us
    all_to_all x1, waiting for transfers between devices: 186 us -> 18.2 us  [per_device(): lax.all_to_all(outgoing, 'expert', split_axis=0, concat_axis=0, tiled=True)]
    dot_general x8 -> x0, matrix products: 49 us -> none  [the longest x1 22.1 us: per_device(): jnp.einsum('pecd,edf->pecf', grouped, gate_full, preferred_element_type=j...]
    pallas_call x0 -> x8, Pallas kernels: none -> 44.7 us  [the longest x1 19 us: run_experts(): pl.pallas_call(functools.partial(expert_kernel, pairs=pairs, kept=kept, s...]
    ppermute x0 -> x23, waiting for transfers between devices: none -> 38.9 us  [per_device(): lax.ppermute(array, 'expert', moves(peers, target))]
    ppermute x0 -> x23, starting transfers between devices: none -> 27.4 us  [per_device(): lax.ppermute(array, 'expert', moves(peers, target))]
    reshape x8 -> x0, local copies, waits for them, and re-layouts: 20.8 us -> none  [the longest x1 9.79 us: per_device(): outgoing = outgoing.reshape(experts, slot_span, model_width)]
    all_to_all x1 -> x0, waiting for transfers between devices: 18.5 us -> none  [per_device(): lax.all_to_all(inner_act, 'expert', split_axis=0, concat_axis=0, tiled=True)]
    unnamed x13 -> x54, local copies, waits for them, and re-layouts: 0.9 us -> 7.48 us
  transfers between devices with their start and end apart: 2 -> 24, of which waited for: 2 -> 12; matrix products, arithmetic and copies ran while one was open for 7% -> 4% of each run, Pallas kernels for 0% -> 14%
where the time goes in v2:
time: 149 us; the launch traced here: 148 us
  waiting for transfers between devices  57 us (38%)
  Pallas kernels  44.7 us (30%)
  starting transfers between devices  30.2 us (20%)
  local copies, waits for them, and re-layouts  12.7 us (9%)
  other arithmetic  2.84 us (2%)
    ppermute x23, waiting for transfers between devices, per_device(): lax.ppermute(array, 'expert', moves(peers, target))  38.9 us
    ppermute x23, starting transfers between devices, per_device(): lax.ppermute(array, 'expert', moves(peers, target))  27.4 us
    pallas_call x1, Pallas kernels, run_experts(): pl.pallas_call(functools.partial(expert_kernel, pairs=pairs, kept=kept, s...  19 us
    all_to_all x1, waiting for transfers between devices, per_device(): lax.all_to_all(outgoing, 'expert', split_axis=0, concat_axis=0, tiled=True)  18.2 us
    pallas_call x4, Pallas kernels, pick(): pl.pallas_call(functools.partial(pick_kernel, parts=len(sources)), grid=(...  13.2 us
    pallas_call x1, Pallas kernels, attention(): pl.pallas_call(functools.partial(attention_kernel, groups=groups), grid=(...  8.08 us
    unnamed x54, local copies, waits for them, and re-layouts  7.48 us
    slice x8, local copies, waits for them, and re-layouts, per_device(): far = (send(column[:cut], to_row), send(row[cut:], to_column))  2.98 us
  transfers between devices with their start and end apart: 24, of which 12 were waited for; matrix products, arithmetic and copies ran while one was open for 4% of the time, Pallas kernels for 14%

profile of v2, /device:TPU:0, one launch (start us, length us, event | category | flops | bytes accessed | tf_op | source)
XLA Modules:
  0.0 148.4 jit_solution(2074106484769219859)
XLA Ops:
  0.6 1.4 copy.19
  2.1 2.8 %prepare.1 = (bf16[56,4224]{1,0:T(8,128)(2,1)}, s32[56,128]{1,0:T(8,128)}) custom-call(bf16[14,4,4096]{2,1,0:T(4,128)(2,1)} %bitcast.20, s32[56,8]{1,0:T(8,128)} %bitcast.21, bf16[56,56]{1,0:T(8,128)(2,1)} %constant.145.clone.order_ref), custom_call_target="tpu_custom_call" | custom-call | tf_op jit(solution)/shard_map/prepare/pallas_call | solution.py:131
  4.9 2.9 %collective-permute-start = (bf16[56,4224]{1,0:T(8,128)(2,1)}, bf16[56,4224]{1,0:T(8,128)(2,1)S(1)}, u32[]{:S(2)}, u32[]{:S(2)}) collective-permute-start(bf16[56,4224]{1,0:T(8,128)(2,1)} %get-tuple-element.24.refs_0_.refs_5_), channel_id=1, source_target_pairs={{0,2},{1,3},{2,0},{3,1},{4,6},{5,7},{6,4},{7,5},{8,10},{9,11},{10,... | collective-permute-start | bytes 1419272 | tf_op jit(solution)/shard_map/ppermute | solution.py:302
  7.8 1.5 %collective-permute-start.1 = (bf16[56,4224]{1,0:T(8,128)(2,1)}, bf16[56,4224]{1,0:T(8,128)(2,1)S(1)}, u32[]{:S(2)}, u32[]{:S(2)}) collective-permute-start(bf16[56,4224]{1,0:T(8,128)(2,1)} %get-tuple-element.24.refs_0_.refs_5_), channel_id=1, source_target_pairs={{0,4},{1,5},{2,6},{3,7},{4,0},{5,1},{6,2},{7,3},{8,12},{9,13},{10,... | collective-permute-start | bytes 1419272 | tf_op jit(solution)/shard_map/ppermute | solution.py:302
  9.3 2.6 %collective-permute-start.11 = (bf16[56,4224]{1,0:T(8,128)(2,1)}, bf16[56,4224]{1,0:T(8,128)(2,1)}, u32[]{:S(2)}, u32[]{:S(2)}) collective-permute-start(bf16[56,4224]{1,0:T(8,128)(2,1)} %get-tuple-element.24.refs_0_.refs_5_), channel_id=1, source_target_pairs={{0,16},{1,17},{2,18},{3,19},{4,20},{5,21},{6,22},{7,23},{8,24},{9,... | collective-permute-start | bytes 1419272 | tf_op jit(solution)/shard_map/ppermute | solution.py:302
  11.9 1.6 %collective-permute-start.5 = (bf16[56,4224]{1,0:T(8,128)(2,1)}, bf16[56,4224]{1,0:T(8,128)(2,1)S(1)}, u32[]{:S(2)}, u32[]{:S(2)}) collective-permute-start(bf16[56,4224]{1,0:T(8,128)(2,1)} %get-tuple-element.24.refs_0_.refs_5_), channel_id=1, source_target_pairs={{0,8},{1,9},{2,10},{3,11},{4,12},{5,13},{6,14},{7,15},{8,0},{9,1},... | collective-permute-start | bytes 1419272 | tf_op jit(solution)/shard_map/ppermute | solution.py:302
  13.5 5.3 %collective-permute-done.refs_1_.refs_6_ = bf16[56,4224]{1,0:T(8,128)(2,1)S(1)} collective-permute-done((bf16[56,4224]{1,0:T(8,128)(2,1)}, bf16[56,4224]{1,0:T(8,128)(2,1)S(1)}, u32[]{:S(2)}, u32[]{:S(2)}) %collective-permute-start) | collective-permute-done | bytes 473120 | tf_op jit(solution)/shard_map/ppermute | solution.py:302
  18.9 1.8 %collective-permute-start.2 = (bf16[32,4224]{1,0:T(8,128)(2,1)S(1)}, bf16[32,4224]{1,0:T(8,128)(2,1)S(1)}, u32[]{:S(2)}, u32[]{:S(2)}) collective-permute-start(bf16[32,4224]{1,0:T(8,128)(2,1)S(1)} %slice.32), channel_id=1, source_target_pairs={{0,4},{1,5},{2,6},{3,7},{4,0},{5,1},{6,2},{7,3},{8,12},{9,13},{10,... | collective-permute-start | bytes 811016 | tf_op jit(solution)/shard_map/ppermute | solution.py:302
  20.7 1.6 %collective-permute-start.3 = (bf16[24,4224]{1,0:T(8,128)(2,1)S(1)}, bf16[24,4224]{1,0:T(8,128)(2,1)S(1)}, u32[]{:S(2)}, u32[]{:S(2)}) collective-permute-start(bf16[24,4224]{1,0:T(8,128)(2,1)S(1)} %slice.33), channel_id=1, source_target_pairs={{0,2},{1,3},{2,0},{3,1},{4,6},{5,7},{6,4},{7,5},{8,10},{9,11},{10,... | collective-permute-start | bytes 608264 | tf_op jit(solution)/shard_map/ppermute | solution.py:302
  22.3 10.5 %collective-permute-done.11.refs_0_.refs_5_ = bf16[56,4224]{1,0:T(8,128)(2,1)} collective-permute-done((bf16[56,4224]{1,0:T(8,128)(2,1)}, bf16[56,4224]{1,0:T(8,128)(2,1)}, u32[]{:S(2)}, u32[]{:S(2)}) %collective-permute-start.11) | collective-permute-done | bytes 473120 | tf_op jit(solution)/shard_map/ppermute | solution.py:302
  32.8 3.4 %collective-permute-start.17 = (bf16[56,4224]{1,0:T(8,128)(2,1)}, bf16[56,4224]{1,0:T(8,128)(2,1)}, u32[]{:S(2)}, u32[]{:S(2)}) collective-permute-start(bf16[56,4224]{1,0:T(8,128)(2,1)} %get-tuple-element.24.refs_0_.refs_5_), channel_id=1, source_target_pairs={{0,24},{1,25},{2,26},{3,27},{4,28},{5,29},{6,30},{7,31},{8,16},{9,... | collective-permute-start | bytes 1419272 | tf_op jit(solution)/shard_map/ppermute | solution.py:302
  36.2 0.8 copy-done.17
  37.0 0.5 collective-permute-start.6
  37.5 0.5 collective-permute-start.7
  38.0 1.5 %collective-permute-start.12 = (bf16[56,4224]{1,0:T(8,128)(2,1)}, bf16[56,4224]{1,0:T(8,128)(2,1)S(1)}, u32[]{:S(2)}, u32[]{:S(2)}) collective-permute-start(bf16[56,4224]{1,0:T(8,128)(2,1)} %collective-permute-done.11.refs_0_.refs_5_), channel_id=1, source_target_pairs={{0,2},{1,3},{2,0},{3,1},{4,6},{5,7},{6,4},{7,5},{8,10},{9,11},{10,... | collective-permute-start | bytes 1419272 | tf_op jit(solution)/shard_map/ppermute | solution.py:302
  39.5 1.5 %collective-permute-start.13 = (bf16[56,4224]{1,0:T(8,128)(2,1)}, bf16[56,4224]{1,0:T(8,128)(2,1)S(1)}, u32[]{:S(2)}, u32[]{:S(2)}) collective-permute-start(bf16[56,4224]{1,0:T(8,128)(2,1)} %collective-permute-done.11.refs_0_.refs_5_), channel_id=1, source_target_pairs={{0,4},{1,5},{2,6},{3,7},{4,0},{5,1},{6,2},{7,3},{8,12},{9,13},{10,... | collective-permute-start | bytes 1419272 | tf_op jit(solution)/shard_map/ppermute | solution.py:302
  41.0 0.7 add_convert_fusion
  41.7 0.7 broadcast_in_dim.25.refs_11_
  42.5 3.3 %pick.4 = (bf16[96,4096]{1,0:T(8,128)(2,1)}, bf16[96,4096]{1,0:T(8,128)(2,1)}) custom-call(bf16[56,4224]{1,0:T(8,128)(2,1)} %get-tuple-element.24.refs_0_.refs_5_, bf16[56,4224]{1,0:T(8,128)(2,1)} %copy-done.10, bf16[56,4224]{1,0:T(8,128)(2,1)} %copy-done.14, bf16[32,4224]{1,0:T(8,128)(2,1)} %copy-done.17, bf16[24,4224]{1,0:T(8,128)(2,1)} %copy-done.21, ...), custom_call_target="tpu_custom_call" | custom-call | tf_op jit(solution)/shard_map/pick/pallas_call | solution.py:170
  45.8 1.8 %collective-permute-done.17.refs_0_.refs_5_ = bf16[56,4224]{1,0:T(8,128)(2,1)} collective-permute-done((bf16[56,4224]{1,0:T(8,128)(2,1)}, bf16[56,4224]{1,0:T(8,128)(2,1)}, u32[]{:S(2)}, u32[]{:S(2)}) %collective-permute-start.17) | collective-permute-done | bytes 473120 | tf_op jit(solution)/shard_map/ppermute | solution.py:302
  47.6 3.1 %collective-permute-done.6.refs_1_.refs_6_ = bf16[56,4224]{1,0:T(8,128)(2,1)S(1)} collective-permute-done((bf16[56,4224]{1,0:T(8,128)(2,1)S(1)}, bf16[56,4224]{1,0:T(8,128)(2,1)S(1)}, u32[]{:S(2)}, u32[]{:S(2)}) %collective-permute-start.6) | collective-permute-done | bytes 473120 | tf_op jit(solution)/shard_map/ppermute | solution.py:302
  50.7 0.6 collective-permute-done.7.refs_2_.refs_7_
  51.3 1.5 %collective-permute-start.18 = (bf16[56,4224]{1,0:T(8,128)(2,1)}, bf16[56,4224]{1,0:T(8,128)(2,1)S(1)}, u32[]{:S(2)}, u32[]{:S(2)}) collective-permute-start(bf16[56,4224]{1,0:T(8,128)(2,1)} %collective-permute-done.17.refs_0_.refs_5_), channel_id=1, source_target_pairs={{0,2},{1,3},{2,0},{3,1},{4,6},{5,7},{6,4},{7,5},{8,10},{9,11},{10,... | collective-permute-start | bytes 1419272 | tf_op jit(solution)/shard_map/ppermute | solution.py:302
  52.8 0.5 collective-permute-start.19
  53.3 8.1 %collective-permute-done.13.refs_2_.refs_7_ = bf16[56,4224]{1,0:T(8,128)(2,1)S(1)} collective-permute-done((bf16[56,4224]{1,0:T(8,128)(2,1)}, bf16[56,4224]{1,0:T(8,128)(2,1)S(1)}, u32[]{:S(2)}, u32[]{:S(2)}) %collective-permute-start.13) | collective-permute-done | bytes 473120 | tf_op jit(solution)/shard_map/ppermute | solution.py:302
  61.4 1.6 %collective-permute-start.15 = (bf16[24,4224]{1,0:T(8,128)(2,1)S(1)}, bf16[24,4224]{1,0:T(8,128)(2,1)S(1)}, u32[]{:S(2)}, u32[]{:S(2)}) collective-permute-start(bf16[24,4224]{1,0:T(8,128)(2,1)S(1)} %slice.37), channel_id=1, source_target_pairs={{0,2},{1,3},{2,0},{3,1},{4,6},{5,7},{6,4},{7,5},{8,10},{9,11},{10,... | collective-permute-start | bytes 608264 | tf_op jit(solution)/shard_map/ppermute | solution.py:302
  63.0 0.6 collective-permute-start.14
  63.6 0.7 slice.34
  64.3 1.5 %collective-permute-start.8 = (bf16[32,4224]{1,0:T(8,128)(2,1)}, bf16[32,4224]{1,0:T(8,128)(2,1)S(1)}, u32[]{:S(2)}, u32[]{:S(2)}) collective-permute-start(bf16[32,4224]{1,0:T(8,128)(2,1)} %slice.34), channel_id=1, source_target_pairs={{0,4},{1,5},{2,6},{3,7},{4,0},{5,1},{6,2},{7,3},{8,12},{9,13},{10,... | collective-permute-start | bytes 811016 | tf_op jit(solution)/shard_map/ppermute | solution.py:302
  65.9 5.1 %collective-permute-done.18.refs_1_.refs_6_ = bf16[56,4224]{1,0:T(8,128)(2,1)S(1)} collective-permute-done((bf16[56,4224]{1,0:T(8,128)(2,1)}, bf16[56,4224]{1,0:T(8,128)(2,1)S(1)}, u32[]{:S(2)}, u32[]{:S(2)}) %collective-permute-start.18) | collective-permute-done | bytes 473120 | tf_op jit(solution)/shard_map/ppermute | solution.py:302
  71.0 0.8 slice.38
  71.7 0.5 collective-permute-start.20
  72.3 0.7 slice.35
  73.0 0.5 collective-permute-start.9
  73.5 0.7 slice.39
  74.2 0.8 collective-permute-done.15.refs_4_.refs_9_
  75.0 0.7 collective-permute-start.21
  75.7 1.6 %collective-permute-done.14.refs_3_.refs_8_ = bf16[32,4224]{1,0:T(8,128)(2,1)S(1)} collective-permute-done((bf16[32,4224]{1,0:T(8,128)(2,1)S(1)}, bf16[32,4224]{1,0:T(8,128)(2,1)S(1)}, u32[]{:S(2)}, u32[]{:S(2)}) %collective-permute-start.14) | collective-permute-done | bytes 270368 | tf_op jit(solution)/shard_map/ppermute | solution.py:302
  77.4 0.7 copy-done.19
  78.1 3.3 %pick.6 = (bf16[96,4096]{1,0:T(8,128)(2,1)}, bf16[96,4096]{1,0:T(8,128)(2,1)}) custom-call(bf16[56,4224]{1,0:T(8,128)(2,1)} %collective-permute-done.11.refs_0_.refs_5_, bf16[56,4224]{1,0:T(8,128)(2,1)} %copy-done.9, bf16[56,4224]{1,0:T(8,128)(2,1)} %copy-done.13, bf16[32,4224]{1,0:T(8,128)(2,1)} %copy-done.19, bf16[24,4224]{1,0:T(8,128)(2,1)} %copy-done.22, ...), custom_call_target="tpu_custom_call" | custom-call | tf_op jit(solution)/shard_map/pick/pallas_call | solution.py:170
  81.4 0.1 collective-permute-start.16
  81.5 1.6 %collective-permute-done.8.refs_3_.refs_8_ = bf16[32,4224]{1,0:T(8,128)(2,1)S(1)} collective-permute-done((bf16[32,4224]{1,0:T(8,128)(2,1)}, bf16[32,4224]{1,0:T(8,128)(2,1)S(1)}, u32[]{:S(2)}, u32[]{:S(2)}) %collective-permute-start.8) | collective-permute-done | bytes 270368 | tf_op jit(solution)/shard_map/ppermute | solution.py:302
  83.1 0.7 copy-done.18
  83.8 3.3 %pick.5 = (bf16[96,4096]{1,0:T(8,128)(2,1)}, bf16[96,4096]{1,0:T(8,128)(2,1)}) custom-call(bf16[56,4224]{1,0:T(8,128)(2,1)} %copy-done.15, bf16[56,4224]{1,0:T(8,128)(2,1)} %copy-done.7, bf16[56,4224]{1,0:T(8,128)(2,1)} %copy-done.11, bf16[32,4224]{1,0:T(8,128)(2,1)} %copy-done.18, bf16[24,4224]{1,0:T(8,128)(2,1)} %collective-permute-done.9.refs_4_.refs_9_, ...), custom_call_target="tpu_custom_call" | custom-call | tf_op jit(solution)/shard_map/pick/pallas_call | solution.py:170
  87.2 0.2 collective-permute-done.20.refs_3_.refs_8_
  87.4 0.5 copy-done.20
  87.9 0.7 copy-done.16
  88.6 3.3 %pick.7 = (bf16[96,4096]{1,0:T(8,128)(2,1)}, bf16[96,4096]{1,0:T(8,128)(2,1)}) custom-call(bf16[56,4224]{1,0:T(8,128)(2,1)} %collective-permute-done.17.refs_0_.refs_5_, bf16[56,4224]{1,0:T(8,128)(2,1)} %copy-done.8, bf16[56,4224]{1,0:T(8,128)(2,1)} %copy-done.12, bf16[32,4224]{1,0:T(8,128)(2,1)} %copy-done.16, bf16[24,4224]{1,0:T(8,128)(2,1)} %copy-done.20, ...), custom_call_target="tpu_custom_call" | custom-call | tf_op jit(solution)/shard_map/pick/pallas_call | solution.py:170
  91.9 0.5 collective-permute-start.22
  92.4 2.1 %fusion.10.refs_8_ = s32[768,1]{1,0:T(8,128)} fusion(s32[]{:T(128)S(6)} %select_n.171, s32[]{:T(128)S(6)} %select_n.167, s32[]{:T(128)S(6)} %select_n.162, s32[]{:T(128)S(6)} %select_n.160), kind=kLoop, calls=%fused_computation.37 | loop fusion | flops 79872 | bytes 3088 | tf_op jit(solution)/shard_map/add | solution.py:343
  94.6 0.8 copy-done.23
  95.4 0.2 copy-done.24
  95.7 0.3 copy-done.25
  95.9 19.0 %experts.1 = bf16[768,768]{1,0:T(8,128)(2,1)} custom-call(bf16[96,4096]{1,0:T(8,128)(2,1)} %get-tuple-element.17.refs_0_, bf16[96,4096]{1,0:T(8,128)(2,1)} %collective-permute-done.4.refs_1_, bf16[96,4096]{1,0:T(8,128)(2,1)} %get-tuple-element.20.refs_2_, bf16[96,4096]{1,0:T(8,128)(2,1)} %copy-done.24, bf16[96,4096]{1,0:T(8,128)(2,1)} %get-tuple-element.22.refs_4_, ...), custom_call_target="tpu_custom_call" | custom-call | tf_op jit(solution)/shard_map/experts/pallas_call | solution.py:224
  114.9 0.0 copy-start.3
  114.9 0.0 copy-start.4
  114.9 0.0 copy-start.6
  114.9 2.8 %all-to-all-start = ((bf16[32,24,768]{2,1,0:T(8,128)(2,1)}), bf16[32,24,768]{2,1,0:T(8,128)(2,1)S(1)}, u32[]{:S(2)}, u32[]{:S(2)}) async-start(bf16[32,24,768]{2,1,0:T(8,128)(2,1)} %bitcast.17), calls=%async_computation | async-start | bytes 2359296 | tf_op jit(solution)/shard_map/all_to_all | solution.py:363
  117.8 0.1 copy.20
  117.9 1.5 %copy-done.1 = bf16[14,128,512]{2,1,0:T(8,128)(2,1)S(1)} copy-done((bf16[14,128,512]{2,1,0:T(8,128)(2,1)S(1)}, bf16[14,128,512]{2,1,0:T(8,128)(2,1)}, u32[]{:S(2)}) %copy-start.1) | copy-done | bytes 1835032
  119.4 1.2 copy-done.2
  120.6 8.1 %attention.1 = bf16[14,4,8192]{2,1,0:T(4,128)(2,1)} custom-call(s32[14]{0:T(128)S(1)} %copy-done.6, bf16[14,4,8192]{2,1,0:T(4,128)(2,1)S(1)} %bitcast.13, bf16[14,4,512]{2,1,0:T(4,128)(2,1)S(1)} %bitcast.15, bf16[14,4,512]{2,1,0:T(4,128)(2,1)S(1)} %bitcast.16, bf16[14,128,512]{2,1,0:T(8,128)(2,1)S(1)} %copy-done, bf16[14,128,512]{2,1,0:T(8,128)(2,1)S(1)} %copy-done.1), custom_call_target="tpu_custom_call" | custom-call | tf_op jit(solution)/shard_map/attention/pallas_call | solution.py:63
  128.6 18.2 %all-to-all-done = bf16[32,24,768]{2,1,0:T(8,128)(2,1)S(1)} async-done(((bf16[32,24,768]{2,1,0:T(8,128)(2,1)}), bf16[32,24,768]{2,1,0:T(8,128)(2,1)S(1)}, u32[]{:S(2)}, u32[]{:S(2)}) %all-to-all-start) | async-done | bytes 1179680 | tf_op jit(solution)/shard_map/all_to_all | solution.py:363
  146.8 1.6 %combine.1 = bf16[14,4,6144]{2,1,0:T(4,128)(2,1)} custom-call(bf16[768,768]{1,0:T(8,128)(2,1)S(1)} %bitcast.12, s32[56,128]{1,0:T(8,128)S(1)} %copy-done.5, f32[56,8]{1,0:T(8,128)S(1)} %bitcast.14), custom_call_target="tpu_custom_call" | custom-call | tf_op jit(solution)/shard_map/combine/pallas_call | solution.py:265
  (59 shorter events, 0.2 us)
Async XLA Ops:
  4.9 14.0 %collective-permute-start = (bf16[56,4224]{1,0:T(8,128)(2,1)}, bf16[56,4224]{1,0:T(8,128)(2,1)S(1)}, u32[]{:S(2)}, u32[]{:S(2)}) collective-permute-start(bf16[56,4224]{1,0:T(8,128)(2,1)} %get-tuple-element.24.refs_0_.refs_5_), channel_id=1, source_target_pairs={{0,2},{1,3},{2,0},{3,1},{4,6},{5,7},{6,4},{7,5},{8,10},{9,11},{10,... | collective-permute-start | bytes 1419272 | tf_op jit(solution)/shard_map/ppermute | solution.py:302
  7.8 12.9 %collective-permute-start.1 = (bf16[56,4224]{1,0:T(8,128)(2,1)}, bf16[56,4224]{1,0:T(8,128)(2,1)S(1)}, u32[]{:S(2)}, u32[]{:S(2)}) collective-permute-start(bf16[56,4224]{1,0:T(8,128)(2,1)} %get-tuple-element.24.refs_0_.refs_5_), channel_id=1, source_target_pairs={{0,4},{1,5},{2,6},{3,7},{4,0},{5,1},{6,2},{7,3},{8,12},{9,13},{10,... | collective-permute-start | bytes 1419272 | tf_op jit(solution)/shard_map/ppermute | solution.py:302
  9.3 23.5 %collective-permute-start.11 = (bf16[56,4224]{1,0:T(8,128)(2,1)}, bf16[56,4224]{1,0:T(8,128)(2,1)}, u32[]{:S(2)}, u32[]{:S(2)}) collective-permute-start(bf16[56,4224]{1,0:T(8,128)(2,1)} %get-tuple-element.24.refs_0_.refs_5_), channel_id=1, source_target_pairs={{0,16},{1,17},{2,18},{3,19},{4,20},{5,21},{6,22},{7,23},{8,24},{9,... | collective-permute-start | bytes 1419272 | tf_op jit(solution)/shard_map/ppermute | solution.py:302
  11.9 24.3 %collective-permute-start.5 = (bf16[56,4224]{1,0:T(8,128)(2,1)}, bf16[56,4224]{1,0:T(8,128)(2,1)S(1)}, u32[]{:S(2)}, u32[]{:S(2)}) collective-permute-start(bf16[56,4224]{1,0:T(8,128)(2,1)} %get-tuple-element.24.refs_0_.refs_5_), channel_id=1, source_target_pairs={{0,8},{1,9},{2,10},{3,11},{4,12},{5,13},{6,14},{7,15},{8,0},{9,1},... | collective-permute-start | bytes 1419272 | tf_op jit(solution)/shard_map/ppermute | solution.py:302
  18.8 23.6 %copy-start.10 = (bf16[56,4224]{1,0:T(8,128)(2,1)}, bf16[56,4224]{1,0:T(8,128)(2,1)S(1)}, u32[]{:S(2)}) copy-start(bf16[56,4224]{1,0:T(8,128)(2,1)S(1)} %collective-permute-done.refs_1_.refs_6_) | copy-start | bytes 1419268
  18.9 17.3 %collective-permute-start.2 = (bf16[32,4224]{1,0:T(8,128)(2,1)S(1)}, bf16[32,4224]{1,0:T(8,128)(2,1)S(1)}, u32[]{:S(2)}, u32[]{:S(2)}) collective-permute-start(bf16[32,4224]{1,0:T(8,128)(2,1)S(1)} %slice.32), channel_id=1, source_target_pairs={{0,4},{1,5},{2,6},{3,7},{4,0},{5,1},{6,2},{7,3},{8,12},{9,13},{10,... | collective-permute-start | bytes 811016 | tf_op jit(solution)/shard_map/ppermute | solution.py:302
  20.7 21.8 %copy-start.14 = (bf16[56,4224]{1,0:T(8,128)(2,1)}, bf16[56,4224]{1,0:T(8,128)(2,1)S(1)}, u32[]{:S(2)}) copy-start(bf16[56,4224]{1,0:T(8,128)(2,1)S(1)} %collective-permute-done.1.refs_2_.refs_7_) | copy-start | bytes 1419268
  20.7 15.5 %collective-permute-start.3 = (bf16[24,4224]{1,0:T(8,128)(2,1)S(1)}, bf16[24,4224]{1,0:T(8,128)(2,1)S(1)}, u32[]{:S(2)}, u32[]{:S(2)}) collective-permute-start(bf16[24,4224]{1,0:T(8,128)(2,1)S(1)} %slice.33), channel_id=1, source_target_pairs={{0,2},{1,3},{2,0},{3,1},{4,6},{5,7},{6,4},{7,5},{8,10},{9,11},{10,... | collective-permute-start | bytes 608264 | tf_op jit(solution)/shard_map/ppermute | solution.py:302
  32.8 14.8 %collective-permute-start.17 = (bf16[56,4224]{1,0:T(8,128)(2,1)}, bf16[56,4224]{1,0:T(8,128)(2,1)}, u32[]{:S(2)}, u32[]{:S(2)}) collective-permute-start(bf16[56,4224]{1,0:T(8,128)(2,1)} %get-tuple-element.24.refs_0_.refs_5_), channel_id=1, source_target_pairs={{0,24},{1,25},{2,26},{3,27},{4,28},{5,29},{6,30},{7,31},{8,16},{9,... | collective-permute-start | bytes 1419272 | tf_op jit(solution)/shard_map/ppermute | solution.py:302
  36.2 9.6 %copy-start.15 = (bf16[56,4224]{1,0:T(8,128)(2,1)}, bf16[56,4224]{1,0:T(8,128)(2,1)S(1)}, u32[]{:S(2)}) copy-start(bf16[56,4224]{1,0:T(8,128)(2,1)S(1)} %collective-permute-done.5.refs_0_.refs_5_) | copy-start | bytes 1419268
  36.2 6.3 %copy-start.21 = (bf16[24,4224]{1,0:T(8,128)(2,1)}, bf16[24,4224]{1,0:T(8,128)(2,1)S(1)}, u32[]{:S(2)}) copy-start(bf16[24,4224]{1,0:T(8,128)(2,1)S(1)} %collective-permute-done.3.refs_4_.refs_9_) | copy-start | bytes 608260
  36.2 0.8 copy-start.17
  37.0 13.7 %collective-permute-start.6 = (bf16[56,4224]{1,0:T(8,128)(2,1)S(1)}, bf16[56,4224]{1,0:T(8,128)(2,1)S(1)}, u32[]{:S(2)}, u32[]{:S(2)}) collective-permute-start(bf16[56,4224]{1,0:T(8,128)(2,1)S(1)} %collective-permute-done.5.refs_0_.refs_5_), channel_id=1, source_target_pairs={{0,2},{1,3},{2,0},{3,1},{4,6},{5,7},{6,4},{7,5},{8,10},{9,11},{10,... | collective-permute-start | bytes 1419272 | tf_op jit(solution)/shard_map/ppermute | solution.py:302
  37.5 13.8 %collective-permute-start.7 = (bf16[56,4224]{1,0:T(8,128)(2,1)S(1)}, bf16[56,4224]{1,0:T(8,128)(2,1)S(1)}, u32[]{:S(2)}, u32[]{:S(2)}) collective-permute-start(bf16[56,4224]{1,0:T(8,128)(2,1)S(1)} %collective-permute-done.5.refs_0_.refs_5_), channel_id=1, source_target_pairs={{0,4},{1,5},{2,6},{3,7},{4,0},{5,1},{6,2},{7,3},{8,12},{9,13},{10,... | collective-permute-start | bytes 1419272 | tf_op jit(solution)/shard_map/ppermute | solution.py:302
  38.0 25.0 %collective-permute-start.12 = (bf16[56,4224]{1,0:T(8,128)(2,1)}, bf16[56,4224]{1,0:T(8,128)(2,1)S(1)}, u32[]{:S(2)}, u32[]{:S(2)}) collective-permute-start(bf16[56,4224]{1,0:T(8,128)(2,1)} %collective-permute-done.11.refs_0_.refs_5_), channel_id=1, source_target_pairs={{0,2},{1,3},{2,0},{3,1},{4,6},{5,7},{6,4},{7,5},{8,10},{9,11},{10,... | collective-permute-start | bytes 1419272 | tf_op jit(solution)/shard_map/ppermute | solution.py:302
  39.5 21.9 %collective-permute-start.13 = (bf16[56,4224]{1,0:T(8,128)(2,1)}, bf16[56,4224]{1,0:T(8,128)(2,1)S(1)}, u32[]{:S(2)}, u32[]{:S(2)}) collective-permute-start(bf16[56,4224]{1,0:T(8,128)(2,1)} %collective-permute-done.11.refs_0_.refs_5_), channel_id=1, source_target_pairs={{0,4},{1,5},{2,6},{3,7},{4,0},{5,1},{6,2},{7,3},{8,12},{9,13},{10,... | collective-permute-start | bytes 1419272 | tf_op jit(solution)/shard_map/ppermute | solution.py:302
  50.7 30.7 %copy-start.7 = (bf16[56,4224]{1,0:T(8,128)(2,1)}, bf16[56,4224]{1,0:T(8,128)(2,1)S(1)}, u32[]{:S(2)}) copy-start(bf16[56,4224]{1,0:T(8,128)(2,1)S(1)} %collective-permute-done.6.refs_1_.refs_6_) | copy-start | bytes 1419268
  51.3 30.1 %copy-start.11 = (bf16[56,4224]{1,0:T(8,128)(2,1)}, bf16[56,4224]{1,0:T(8,128)(2,1)S(1)}, u32[]{:S(2)}) copy-start(bf16[56,4224]{1,0:T(8,128)(2,1)S(1)} %collective-permute-done.7.refs_2_.refs_7_) | copy-start | bytes 1419268
  51.3 19.7 %collective-permute-start.18 = (bf16[56,4224]{1,0:T(8,128)(2,1)}, bf16[56,4224]{1,0:T(8,128)(2,1)S(1)}, u32[]{:S(2)}, u32[]{:S(2)}) collective-permute-start(bf16[56,4224]{1,0:T(8,128)(2,1)} %collective-permute-done.17.refs_0_.refs_5_), channel_id=1, source_target_pairs={{0,2},{1,3},{2,0},{3,1},{4,6},{5,7},{6,4},{7,5},{8,10},{9,11},{10,... | collective-permute-start | bytes 1419272 | tf_op jit(solution)/shard_map/ppermute | solution.py:302
  52.8 20.2 %collective-permute-start.19 = (bf16[56,4224]{1,0:T(8,128)(2,1)}, bf16[56,4224]{1,0:T(8,128)(2,1)S(1)}, u32[]{:S(2)}, u32[]{:S(2)}) collective-permute-start(bf16[56,4224]{1,0:T(8,128)(2,1)} %collective-permute-done.17.refs_0_.refs_5_), channel_id=1, source_target_pairs={{0,4},{1,5},{2,6},{3,7},{4,0},{5,1},{6,2},{7,3},{8,12},{9,13},{10,... | collective-permute-start | bytes 1419272 | tf_op jit(solution)/shard_map/ppermute | solution.py:302
  61.4 15.9 %copy-start.13 = (bf16[56,4224]{1,0:T(8,128)(2,1)}, bf16[56,4224]{1,0:T(8,128)(2,1)S(1)}, u32[]{:S(2)}) copy-start(bf16[56,4224]{1,0:T(8,128)(2,1)S(1)} %collective-permute-done.13.refs_2_.refs_7_) | copy-start | bytes 1419268
  61.4 13.6 %collective-permute-start.15 = (bf16[24,4224]{1,0:T(8,128)(2,1)S(1)}, bf16[24,4224]{1,0:T(8,128)(2,1)S(1)}, u32[]{:S(2)}, u32[]{:S(2)}) collective-permute-start(bf16[24,4224]{1,0:T(8,128)(2,1)S(1)} %slice.37), channel_id=1, source_target_pairs={{0,2},{1,3},{2,0},{3,1},{4,6},{5,7},{6,4},{7,5},{8,10},{9,11},{10,... | collective-permute-start | bytes 608264 | tf_op jit(solution)/shard_map/ppermute | solution.py:302
  63.0 14.4 %copy-start.9 = (bf16[56,4224]{1,0:T(8,128)(2,1)}, bf16[56,4224]{1,0:T(8,128)(2,1)S(1)}, u32[]{:S(2)}) copy-start(bf16[56,4224]{1,0:T(8,128)(2,1)S(1)} %collective-permute-done.12.refs_1_.refs_6_) | copy-start | bytes 1419268
  63.0 14.3 %collective-permute-start.14 = (bf16[32,4224]{1,0:T(8,128)(2,1)S(1)}, bf16[32,4224]{1,0:T(8,128)(2,1)S(1)}, u32[]{:S(2)}, u32[]{:S(2)}) collective-permute-start(bf16[32,4224]{1,0:T(8,128)(2,1)S(1)} %slice.36), channel_id=1, source_target_pairs={{0,4},{1,5},{2,6},{3,7},{4,0},{5,1},{6,2},{7,3},{8,12},{9,13},{10,... | collective-permute-start | bytes 811016 | tf_op jit(solution)/shard_map/ppermute | solution.py:302
  64.3 18.8 %collective-permute-start.8 = (bf16[32,4224]{1,0:T(8,128)(2,1)}, bf16[32,4224]{1,0:T(8,128)(2,1)S(1)}, u32[]{:S(2)}, u32[]{:S(2)}) collective-permute-start(bf16[32,4224]{1,0:T(8,128)(2,1)} %slice.34), channel_id=1, source_target_pairs={{0,4},{1,5},{2,6},{3,7},{4,0},{5,1},{6,2},{7,3},{8,12},{9,13},{10,... | collective-permute-start | bytes 811016 | tf_op jit(solution)/shard_map/ppermute | solution.py:302
  71.0 10.4 %copy-start.8 = (bf16[56,4224]{1,0:T(8,128)(2,1)}, bf16[56,4224]{1,0:T(8,128)(2,1)S(1)}, u32[]{:S(2)}) copy-start(bf16[56,4224]{1,0:T(8,128)(2,1)S(1)} %collective-permute-done.18.refs_1_.refs_6_) | copy-start | bytes 1419268
  71.7 15.6 %collective-permute-start.20 = (bf16[32,4224]{1,0:T(8,128)(2,1)}, bf16[32,4224]{1,0:T(8,128)(2,1)S(1)}, u32[]{:S(2)}, u32[]{:S(2)}) collective-permute-start(bf16[32,4224]{1,0:T(8,128)(2,1)} %slice.38), channel_id=1, source_target_pairs={{0,4},{1,5},{2,6},{3,7},{4,0},{5,1},{6,2},{7,3},{8,12},{9,13},{10,... | collective-permute-start | bytes 811016 | tf_op jit(solution)/shard_map/ppermute | solution.py:302
  73.0 8.4 %copy-start.12 = (bf16[56,4224]{1,0:T(8,128)(2,1)}, bf16[56,4224]{1,0:T(8,128)(2,1)S(1)}, u32[]{:S(2)}) copy-start(bf16[56,4224]{1,0:T(8,128)(2,1)S(1)} %collective-permute-done.19.refs_2_.refs_7_) | copy-start | bytes 1419268
  73.0 8.5 %collective-permute-start.9 = (bf16[24,4224]{1,0:T(8,128)(2,1)}, bf16[24,4224]{1,0:T(8,128)(2,1)}, u32[]{:S(2)}, u32[]{:S(2)}) collective-permute-start(bf16[24,4224]{1,0:T(8,128)(2,1)} %slice.35), channel_id=1, source_target_pairs={{0,2},{1,3},{2,0},{3,1},{4,6},{5,7},{6,4},{7,5},{8,10},{9,11},{10,... | collective-permute-start | bytes 608264 | tf_op jit(solution)/shard_map/ppermute | solution.py:302
  75.0 2.4 %copy-start.22 = (bf16[24,4224]{1,0:T(8,128)(2,1)}, bf16[24,4224]{1,0:T(8,128)(2,1)S(1)}, u32[]{:S(2)}) copy-start(bf16[24,4224]{1,0:T(8,128)(2,1)S(1)} %collective-permute-done.15.refs_4_.refs_9_) | copy-start | bytes 608260
  75.0 12.1 %collective-permute-start.21 = (bf16[24,4224]{1,0:T(8,128)(2,1)}, bf16[24,4224]{1,0:T(8,128)(2,1)S(1)}, u32[]{:S(2)}, u32[]{:S(2)}) collective-permute-start(bf16[24,4224]{1,0:T(8,128)(2,1)} %slice.39), channel_id=1, source_target_pairs={{0,2},{1,3},{2,0},{3,1},{4,6},{5,7},{6,4},{7,5},{8,10},{9,11},{10,... | collective-permute-start | bytes 608264 | tf_op jit(solution)/shard_map/ppermute | solution.py:302
  77.3 0.7 copy-start.19
  77.4 17.2 %collective-permute-start.4 = (bf16[96,4096]{1,0:T(8,128)(2,1)}, bf16[96,4096]{1,0:T(8,128)(2,1)}, u32[]{:S(2)}, u32[]{:S(2)}) collective-permute-start(bf16[96,4096]{1,0:T(8,128)(2,1)} %get-tuple-element.18), channel_id=1, source_target_pairs={{0,1},{1,0},{2,3},{3,2},{4,5},{5,4},{6,7},{7,6},{8,9},{9,8},{10,11... | collective-permute-start | bytes 2359304 | tf_op jit(solution)/shard_map/ppermute | solution.py:302
  81.4 13.1 %collective-permute-start.16 = (bf16[96,4096]{1,0:T(8,128)(2,1)}, bf16[96,4096]{1,0:T(8,128)(2,1)S(1)}, u32[]{:S(2)}, u32[]{:S(2)}) collective-permute-start(bf16[96,4096]{1,0:T(8,128)(2,1)} %get-tuple-element.23), channel_id=1, source_target_pairs={{0,1},{1,0},{2,3},{3,2},{4,5},{5,4},{6,7},{7,6},{8,9},{9,8},{10,11... | collective-permute-start | bytes 2359304 | tf_op jit(solution)/shard_map/ppermute | solution.py:302
  83.1 0.7 copy-start.18
  87.1 7.4 %collective-permute-start.10 = (bf16[96,4096]{1,0:T(8,128)(2,1)}, bf16[96,4096]{1,0:T(8,128)(2,1)S(1)}, u32[]{:S(2)}, u32[]{:S(2)}) collective-permute-start(bf16[96,4096]{1,0:T(8,128)(2,1)} %get-tuple-element.21), channel_id=1, source_target_pairs={{0,1},{1,0},{2,3},{3,2},{4,5},{5,4},{6,7},{7,6},{8,9},{9,8},{10,11... | collective-permute-start | bytes 2359304 | tf_op jit(solution)/shard_map/ppermute | solution.py:302
  87.1 0.7 copy-start.20
  87.9 0.7 copy-start.16
  91.9 2.7 %collective-permute-start.22 = (bf16[96,4096]{1,0:T(8,128)(2,1)}, bf16[96,4096]{1,0:T(8,128)(2,1)S(1)}, u32[]{:S(2)}, u32[]{:S(2)}) collective-permute-start(bf16[96,4096]{1,0:T(8,128)(2,1)} %get-tuple-element.27), channel_id=1, source_target_pairs={{0,1},{1,0},{2,3},{3,2},{4,5},{5,4},{6,7},{7,6},{8,9},{9,8},{10,11... | collective-permute-start | bytes 2359304 | tf_op jit(solution)/shard_map/ppermute | solution.py:302
  94.5 0.9 copy-start.23
  94.5 1.1 copy-start.24
  94.5 1.4 copy-start.25
  114.9 2.9 %copy-start.26 = (f32[4,14,8]{1,2,0:T(8,128)S(1)}, f32[4,14,8]{1,2,0:T(8,128)}, u32[]{:S(2)}) copy-start(f32[4,14,8]{1,2,0:T(8,128)} %param.19) | copy-start | bytes 5380
  114.9 3.0 %copy-start = (bf16[14,128,512]{2,1,0:T(8,128)(2,1)S(1)}, bf16[14,128,512]{2,1,0:T(8,128)(2,1)}, u32[]{:S(2)}) copy-start(bf16[14,128,512]{2,1,0:T(8,128)(2,1)} %k_ref.1) | copy-start | bytes 5505028
  114.9 3.0 %copy-start.3 = (bf16[4,14,512]{2,0,1:T(4,128)(2,1)S(1)}, bf16[4,14,512]{2,0,1:T(4,128)(2,1)}, u32[]{:S(2)}) copy-start(bf16[4,14,512]{2,0,1:T(4,128)(2,1)} %param.23) | copy-start | bytes 172036
  114.9 3.0 %copy-start.4 = (bf16[4,14,512]{2,0,1:T(4,128)(2,1)S(1)}, bf16[4,14,512]{2,0,1:T(4,128)(2,1)}, u32[]{:S(2)}) copy-start(bf16[4,14,512]{2,0,1:T(4,128)(2,1)} %param.24) | copy-start | bytes 172036
  114.9 3.0 %copy-start.6 = (s32[14]{0:T(128)S(1)}, s32[14]{0:T(128)}, u32[]{:S(2)}) copy-start(s32[14]{0:T(128)} %lengths_ref) | copy-start | bytes 172
  114.9 31.9 %all-to-all-start = ((bf16[32,24,768]{2,1,0:T(8,128)(2,1)}), bf16[32,24,768]{2,1,0:T(8,128)(2,1)S(1)}, u32[]{:S(2)}, u32[]{:S(2)}) async-start(bf16[32,24,768]{2,1,0:T(8,128)(2,1)} %bitcast.17), calls=%async_computation | async-start | bytes 2359296 | tf_op jit(solution)/shard_map/all_to_all | solution.py:363
  117.9 1.5 %copy-start.1 = (bf16[14,128,512]{2,1,0:T(8,128)(2,1)S(1)}, bf16[14,128,512]{2,1,0:T(8,128)(2,1)}, u32[]{:S(2)}) copy-start(bf16[14,128,512]{2,1,0:T(8,128)(2,1)} %v_ref.1) | copy-start | bytes 5505028
  119.4 1.2 copy-start.2
  120.6 26.2 %copy-start.5 = (s32[56,128]{1,0:T(8,128)S(1)}, s32[56,128]{1,0:T(8,128)}, u32[]{:S(2)}) copy-start(s32[56,128]{1,0:T(8,128)} %get-tuple-element.28.columns_ref) | copy-start | bytes 86020

commit v3 on v2

--- a/solution.py
+++ b/solution.py
@@ -16,7 +16,8 @@
 LANES = 128
 EDGE = 2
 INNER = EDGE**3
-VMEM_BYTES = 60 * 1024 * 1024
+VMEM_BYTES = 50 * 1024 * 1024
+EXPERT_VMEM = 50 * 1024 * 1024
 
 
 def attention_kernel(lengths_ref, q_ref, nk_ref, nv_ref, k_ref, v_ref, out_ref, *, groups):
@@ -81,22 +82,36 @@
 
 
 def moves(peers, target):
-    return [(index, device_at(*target(*place(index)))) for index in range(peers)]
+    pairs = [(index, target(*place(index))) for index in range(peers)]
+    return [(index, device_at(*to)) for index, to in pairs if to is not None]
 
 
 def padded(rows):
     return -(-rows // 16) * 16
 
 
-def prepare_kernel(states_ref, routes_ref, order_ref, payload_ref, columns_ref, *, capacity, experts):
+def prepare_kernel(states_ref, routes_ref, payload_ref, columns_ref, *, capacity, experts):
     tokens, steps, width = states_ref.shape
     states = jnp.concatenate(
         [states_ref[token].astype(jnp.float32) for token in range(tokens)], axis=0
     )
     scale = lax.rsqrt(jnp.mean(states * states, axis=-1, keepdims=True) + 1e-06)
     payload_ref[:, :width] = (states * scale).astype(payload_ref.dtype)
-    routes = routes_ref[...]
     rows = tokens * steps
+    row_ids = lax.broadcasted_iota(jnp.int32, (rows, tokens), 0)
+    row_tokens = row_ids // steps == lax.broadcasted_iota(jnp.int32, (rows, tokens), 1)
+    routes = sum(
+        lax.dot_general(
+            (row_tokens & (row_ids % steps == step)).astype(jnp.float32).astype(jnp.bfloat16),
+            routes_ref[step].astype(jnp.float32).astype(jnp.bfloat16),
+            (((1,), (1,)), ((), ())),
+            preferred_element_type=jnp.float32,
+        )
+        for step in range(steps)
+    ).astype(jnp.int32)
+    first = lax.broadcasted_iota(jnp.int32, (rows, rows), 0)
+    second = lax.broadcasted_iota(jnp.int32, (rows, rows), 1)
+    order = ((first % steps == second % steps) & (first > second)).astype(jnp.float32)
     expert_ids = lax.broadcasted_iota(jnp.int32, (rows, experts), 1)
     marks = [
         (routes[:, choice : choice + 1] == expert_ids).astype(jnp.float32)
@@ -104,7 +119,7 @@
     ]
     named = sum(marks)
     earlier = jnp.dot(
-        order_ref[...], named.astype(jnp.bfloat16), preferred_element_type=jnp.float32
+        order.astype(jnp.bfloat16), named.astype(jnp.bfloat16), preferred_element_type=jnp.float32
     )
     lane_ids = lax.broadcasted_iota(jnp.int32, (rows, LANES), 1)
     step = lax.broadcasted_iota(jnp.int32, (rows, 1), 0) % steps
@@ -124,10 +139,6 @@
 def prepare(states, routes, capacity, experts):
     tokens, steps, width = states.shape
     rows = tokens * steps
-    numbers = np.arange(rows)
-    order = (numbers[:, None] % steps == numbers[None, :] % steps) & (
-        numbers[:, None] > numbers[None, :]
-    )
     return pl.pallas_call(
         functools.partial(prepare_kernel, capacity=capacity, experts=experts),
         out_shape=(
@@ -136,7 +147,7 @@
         ),
         compiler_params=pltpu.CompilerParams(vmem_limit_bytes=VMEM_BYTES),
         name="prepare",
-    )(states, routes, jnp.asarray(order, jnp.bfloat16))
+    )(states, routes)
 
 
 def pick_kernel(*refs, parts):
@@ -164,77 +175,89 @@
     rows, slots = group.shape[1], wanted.shape[0]
     cuts = 2 if width % (2 * LANES) == 0 else 1
     block = width // cuts
-    piece = lambda a: pl.BlockSpec((a.shape[0], block), lambda i: (0, i))
-    codes = lambda a: pl.BlockSpec((a.shape[0], LANES), lambda i: (0, width // LANES))
+    sources = [source if isinstance(source, tuple) else (source, 0, 1) for source in sources]
+    arrays = [source[0] for source in sources]
+    piece = lambda a, n, of: pl.BlockSpec((a.shape[0] // of, block), lambda i: (n, i))
+    codes = lambda a, n, of: pl.BlockSpec((a.shape[0] // of, LANES), lambda i: (n, width // LANES))
     whole = lambda a: pl.BlockSpec(a.shape, lambda i: (0, 0))
     return pl.pallas_call(
         functools.partial(pick_kernel, parts=len(sources)),
         grid=(cuts,),
-        in_specs=[piece(a) for a in sources]
-        + [codes(a) for a in sources]
+        in_specs=[piece(*source) for source in sources]
+        + [codes(*source) for source in sources]
         + [whole(group), whole(wanted)],
         out_specs=[pl.BlockSpec((slots // 2, block), lambda i: (0, i))] * 2,
         out_shape=[jax.ShapeDtypeStruct((slots // 2, width), jnp.bfloat16)] * 2,
         scratch_shapes=[pltpu.VMEM((slots, rows), jnp.bfloat16)],
         compiler_params=pltpu.CompilerParams(vmem_limit_bytes=VMEM_BYTES),
         name="pick",
-    )(*sources, *sources, group, wanted)
-
-
-def expert_kernel(*refs, pairs, kept, sent, experts_local):
-    x_refs, (place_ref, gate_ref, up_ref, out_ref, rows_ref) = refs[: 2 * pairs], refs[2 * pairs :]
-    expert = pl.program_id(1)
-
-    @pl.when(pl.program_id(0) == 0)
+    )(*arrays, *arrays, group, wanted)
+
+
+def expert_kernel(owners_ref, *refs, count, part):
+    x_refs, (gate_ref, up_ref, out_ref, rows_ref, arrived) = refs[:count], refs[count:]
+    hidden_part, expert = pl.program_id(0), pl.program_id(1)
+    experts_local = rows_ref.shape[0]
+    span = out_ref.shape[1] // experts_local
+
+    def copy(number, which):
+        return pltpu.make_async_copy(
+            x_refs[number].at[pl.ds(which * part, part)],
+            rows_ref.at[which, pl.ds(number * part, part)],
+            arrived.at[which, number],
+        )
+
+    @pl.when((hidden_part == 0) & (expert == 0))
     def _():
-        at = 0
-        for number, x_ref in enumerate(x_refs):
-            part = sent if number % 2 else kept
-            rows_ref[expert, at : at + part, :] = x_ref[
-                pl.ds(pl.multiple_of(expert * part, 16), part), :
-            ]
-            at += part
+        for which in range(experts_local):
+            for number in range(count):
+                copy(number, which).start()
+
+    for which in range(experts_local):
+
+        @pl.when((hidden_part == 0) & (expert == which))
+        def _():
+            for number in range(count):
+                copy(number, which).wait()
 
     rows = rows_ref[expert]
     gate = jnp.dot(rows, gate_ref[0], preferred_element_type=jnp.float32)
     up = jnp.dot(rows, up_ref[0], preferred_element_type=jnp.float32)
-    inner = (gate / (1.0 + jnp.exp(-gate)) * up).astype(jnp.bfloat16)
-    wanted = place_ref[...]
-    base = expert * rows.shape[0]
-    row_ids = lax.broadcasted_iota(jnp.int32, (wanted.shape[0], rows.shape[0]), 1) + base
-    marks = (wanted == row_ids).astype(jnp.float32).astype(jnp.bfloat16)
-    placed = jnp.dot(marks, inner, preferred_element_type=jnp.float32).astype(out_ref.dtype)
-
-    @pl.when(expert == 0)
-    def _():
-        out_ref[...] = placed
-
-    @pl.when(expert != 0)
-    def _():
-        out_ref[...] += placed
-
-
-def run_experts(arrays, places, w_gate, w_up):
+    inner = (gate / (1.0 + jnp.exp(-gate)) * up).astype(out_ref.dtype)
+    for which in range(experts_local):
+
+        @pl.when(expert == which)
+        def _():
+            for group in range(owners_ref.shape[0]):
+                out_ref[owners_ref[group], which * span : (which + 1) * span, :] = inner[
+                    group * span : (group + 1) * span
+                ]
+
+
+def run_experts(arrays, owners, span, w_gate, w_up):
     experts_local, width, hidden = w_gate.shape
-    kept, sent = arrays[0].shape[0] // experts_local, arrays[1].shape[0] // experts_local
-    pairs = len(arrays) // 2
-    rows = pairs * (kept + sent)
+    part, count = arrays[0].shape[0] // experts_local, len(arrays)
+    rows = count * part
     block = 2 * LANES
-    slots = places.shape[0]
     return pl.pallas_call(
-        functools.partial(
-            expert_kernel, pairs=pairs, kept=kept, sent=sent, experts_local=experts_local
+        functools.partial(expert_kernel, count=count, part=part),
+        grid=(hidden // block, experts_local),
+        in_specs=[pl.BlockSpec(memory_space=pltpu.SMEM)]
+        + [pl.BlockSpec(memory_space=pl.ANY)] * count
+        + [pl.BlockSpec((1, width, block), lambda f, e: (e, 0, f))] * 2,
+        out_specs=pl.BlockSpec(
+            (owners.shape[0], experts_local * span, block), lambda f, e: (0, 0, f)
         ),
-        grid=(hidden // block, experts_local),
-        in_specs=[pl.BlockSpec(a.shape, lambda f, e: (0, 0)) for a in arrays]
-        + [pl.BlockSpec(places.shape, lambda f, e: (0, 0))]
-        + [pl.BlockSpec((1, width, block), lambda f, e: (e, 0, f))] * 2,
-        out_specs=pl.BlockSpec((slots, block), lambda f, e: (0, f)),
-        out_shape=jax.ShapeDtypeStruct((slots, hidden), jnp.bfloat16),
-        scratch_shapes=[pltpu.VMEM((experts_local, rows, width), jnp.bfloat16)],
-        compiler_params=pltpu.CompilerParams(vmem_limit_bytes=VMEM_BYTES),
+        out_shape=jax.ShapeDtypeStruct(
+            (owners.shape[0], experts_local * span, hidden), jnp.bfloat16
+        ),
+        scratch_shapes=[
+            pltpu.VMEM((experts_local, rows, width), jnp.bfloat16),
+            pltpu.SemaphoreType.DMA((experts_local, count)),
+        ],
+        compiler_params=pltpu.CompilerParams(vmem_limit_bytes=EXPERT_VMEM),
         name="experts",
-    )(*arrays, places, w_gate, w_up)
+    )(owners, *arrays, w_gate, w_up)
 
 
 def combine_kernel(back_ref, columns_ref, gates_ref, out_ref):
@@ -305,15 +328,16 @@
     to_row = lambda z, y, x, c: (z, 1 - y, x, c)
     other_side = lambda z, y, x, c: (z, y, x, 1 - c)
     after = lambda array, *others: lax.optimization_barrier((array,) + others)[0]
-    z, y, x, side = place(me)
 
     by_token = lambda a: jnp.swapaxes(a, 0, 1)
     payload, columns = prepare(
         by_token(hidden_states),
-        by_token(routes).reshape(block_rows, TOPK),
+        jnp.swapaxes(routes, 1, 2),
         capacity,
         experts,
     )
+    me = after(me, columns)
+    z, y, x, side = place(me)
     token = np.arange(4 * block_rows)
     group = (token // block_rows * steps_total + token % steps_total) * 256
     group = jnp.asarray(group, jnp.float32)[None]
@@ -327,39 +351,60 @@
     wanted = wanted_expert * capacity + of_slot + (of_block * steps_total + of_step) * 256
     wanted = jnp.broadcast_to(wanted.astype(jnp.float32)[:, None], (slots.size, LANES))
 
-    arrived = {0: payload}
-    for offset in sorted(range(1, lines), key=lambda n: (n != 2, n)):
-        source = after(payload, arrived[2]) if offset > 2 else payload
-        arrived[offset] = send(source, to_line(offset))
-    kept = 4 * slot_span
-    numbers = jnp.arange(experts * slot_span, dtype=jnp.int32)
-    owner, expert, rest = (
-        numbers // (experts_local * slot_span),
-        numbers // slot_span % experts_local,
-        numbers % slot_span,
-    )
-    oz, oy, ox, oc = place(owner)
-    within = jnp.where(oc == side, 0, kept) + ((oy ^ y) * 2 + (ox ^ x)) * slot_span + rest
-    places = (expert * lines + (oz ^ z)) * 2 * kept + within
-
-    blocks, cut = [], padded(block_rows // 2)
-    hops, fars, keeps = [], [], []
-    for offset in range(lines):
-        own = arrived[offset]
-        if offset == 1:
-            own = after(own, *fars[0], places)
-        elif offset > 2:
-            own = after(own, *hops[offset - 2], keeps[0])
+    planes = [z ^ offset for offset in range(lines)]
+    if lines == 4:
+        inner, beyond = (z == 1) | (z == 2), z // 2 * 2 ^ 2
+        planes[2:] = [beyond + z // 2, beyond + 1 - z // 2]
+    group_id = np.arange(peers)
+    owners = device_at(
+        jnp.stack(planes)[group_id // INNER],
+        y ^ group_id // 2 % EDGE,
+        x ^ group_id % EDGE,
+        side ^ group_id // 4 % EDGE,
+    ).astype(jnp.int32)
+
+    blocks, keeps, cut = [], [], padded(block_rows // 2)
+
+    def add_item(sources):
+        keep, give = pick(sources, group, wanted, model_width)
+        keeps.append(keep)
+        blocks.extend([keep, send(give, other_side)])
+
+    column, row = send(payload, to_column), send(payload, to_row)
+    if lines == 4:
+        middle = lambda z, y, x, c: (3 - z, y, x, c) if z in (1, 2) else None
+        outward = lambda z, y, x, c: (z ^ 1, y, x, c) if z in (1, 2) else None
+        next_line = send(payload, to_line(1))
+        near_plane = send(after(payload, wanted), middle)
+        far_plane = send(next_line, middle)
+        near_out = send(near_plane, outward)
+        far_out = send(far_plane, outward)
+        halves = column[:cut], row[cut:]
+        far = send(halves[0], to_row), send(halves[1], to_column)
+        add_item([after(payload, far_plane), column, row, *far])
+        own = after(next_line, *halves, owners)
         column, row = send(own, to_column), send(own, to_row)
-        hops.append((column, row))
-        far = send(column[:cut], to_row), send(row[cut:], to_column)
-        fars.append(far)
-        keep, give = pick([own, column, row, *far], group, wanted, model_width)
-        keeps.append(keep)
-        blocks += [keep, send(give, other_side)]
-
-    outgoing = run_experts(blocks, places[:, None], gate_full, up_full)
-    outgoing = outgoing.reshape(peers, experts_local * slot_span, hidden_width)
+        halves = column, row
+        far = send(far[0], to_line(1)), send(far[1], to_line(1))
+        add_item([own, column, row, *far])
+        own = after(jnp.where(inner, near_plane, near_out), *halves)
+        column, row = send(own, to_column), send(own, to_row)
+        halves = column[:cut], row[cut:]
+        past, far = far, (send(halves[0], to_row), send(halves[1], to_column))
+        add_item([own, column, row, *far])
+        own = after(jnp.where(inner, far_plane, far_out), *halves, *past, keeps[0])
+        column, row = send(own, to_column), send(own, to_row)
+        halves = lax.optimization_barrier((column[:cut], row[cut:], *far, keeps[1]))[:2]
+        far = send(halves[0], to_row), send(halves[1], to_column)
+        add_item([own, column, row, *far])
+    else:
+        for offset in range(lines):
+            own = send(payload, to_line(offset)) if offset else payload
+            if offset:
+                column, row = send(own, to_column), send(own, to_row)
+            far = send(column[:cut], to_row), send(row[cut:], to_column)
+            add_item([own, column, row, *far])
+    outgoing = run_experts(blocks, owners, slot_span, gate_full, up_full)
     returned = lax.all_to_all(outgoing, "expert", split_axis=0, concat_axis=0, tiled=True)
     attn_out = attention(
         queries, new_keys, new_values, cache_keys, cache_values, after(lengths, outgoing)

time: 149 us -> 138 us (0.926)
  Pallas kernels: 44.7 us -> 35.9 us
  local copies, waits for them, and re-layouts: 12.7 us -> 6.49 us
  starting transfers between devices: 30.2 us -> 32.8 us
  waiting for transfers between devices: 57 us -> 58.7 us
    pallas_call x4, Pallas kernels: 13.2 us -> 7.38 us  [pick(): pl.pallas_call(functools.partial(pick_kernel, parts=len(sources)), grid=(...]
    slice x8 -> x6, local copies, waits for them, and re-layouts: 2.98 us -> 0.1 us  [the longest x4 0.07 us: per_device(): halves = (column[:cut], row[cut:])]
    ppermute x23 -> x25, starting transfers between devices: 27.4 us -> 30 us  [per_device(): lax.ppermute(array, 'expert', moves(peers, target))]
    pallas_call x1, Pallas kernels: 2.82 us -> 0.92 us  [prepare(): pl.pallas_call(functools.partial(prepare_kernel, capacity=capacity, exper...]
    ppermute x23 -> x25, waiting for transfers between devices: 38.9 us -> 40.5 us  [per_device(): lax.ppermute(array, 'expert', moves(peers, target))]
    unnamed x54 -> x26, local copies, waits for them, and re-layouts: 7.48 us -> 6.2 us
  transfers between devices with their start and end apart: 24 -> 26, of which waited for: 12 -> 12; matrix products, arithmetic and copies ran while one was open for 4% -> 2% of each run, Pallas kernels for 14% -> 11%
where the time goes in v3:
time: 138 us; the launch traced here: 137 us
  waiting for transfers between devices  58.7 us (43%)
  Pallas kernels  35.9 us (26%)
  starting transfers between devices  32.8 us (24%)
  local copies, waits for them, and re-layouts  6.49 us (5%)
  other arithmetic  2.63 us (2%)
    ppermute x25, waiting for transfers between devices, per_device(): lax.ppermute(array, 'expert', moves(peers, target))  40.5 us
    ppermute x25, starting transfers between devices, per_device(): lax.ppermute(array, 'expert', moves(peers, target))  30 us
    all_to_all x1, waiting for transfers between devices, per_device(): lax.all_to_all(outgoing, 'expert', split_axis=0, concat_axis=0, tiled=True)  18.2 us
    pallas_call x1, Pallas kernels, run_experts(): pl.pallas_call(functools.partial(expert_kernel, count=count, part=part),...  17.9 us
    pallas_call x1, Pallas kernels, attention(): pl.pallas_call(functools.partial(attention_kernel, groups=groups), grid=(...  8.08 us
    pallas_call x4, Pallas kernels, pick(): pl.pallas_call(functools.partial(pick_kernel, parts=len(sources)), grid=(...  7.38 us
    unnamed x26, local copies, waits for them, and re-layouts  6.2 us
    all_to_all x1, starting transfers between devices, per_device(): lax.all_to_all(outgoing, 'expert', split_axis=0, concat_axis=0, tiled=True)  2.83 us
  transfers between devices with their start and end apart: 26, of which 12 were waited for; matrix products, arithmetic and copies ran while one was open for 2% of the time, Pallas kernels for 11%

profile of v3, /device:TPU:0, one launch (start us, length us, event | category | flops | bytes accessed | tf_op | source)
XLA Modules:
  0.0 137.5 jit_solution(3476142054309161307)
XLA Ops:
  0.6 0.0 copy-start.7
  0.7 1.0 copy-done.4
  1.7 0.7 copy-done.8
  2.4 0.9 prepare.1
  3.3 3.1 %collective-permute-start = (bf16[56,4224]{1,0:T(8,128)(2,1)S(1)}, bf16[56,4224]{1,0:T(8,128)(2,1)S(1)}, u32[]{:S(2)}, u32[]{:S(2)}) collective-permute-start(bf16[56,4224]{1,0:T(8,128)(2,1)S(1)} %get-tuple-element.30.refs_0_.refs_5_), channel_id=1, source_target_pairs={{0,8},{1,9},{2,10},{3,11},{4,12},{5,13},{6,14},{7,15},{8,0},{9,1},... | collective-permute-start | bytes 1419272 | tf_op jit(solution)/shard_map/ppermute | solution.py:325
  6.4 0.7 add_convert_fusion
  7.1 0.1 broadcast_in_dim.24.refs_11_
  7.2 0.7 collective-permute-start.12
  7.9 1.6 %collective-permute-start.2 = (bf16[56,4224]{1,0:T(8,128)(2,1)S(1)}, bf16[56,4224]{1,0:T(8,128)(2,1)S(1)}, u32[]{:S(2)}, u32[]{:S(2)}) collective-permute-start(bf16[56,4224]{1,0:T(8,128)(2,1)S(1)} %get-tuple-element.30.refs_0_.refs_5_), channel_id=1, source_target_pairs={{0,2},{1,3},{2,0},{3,1},{4,6},{5,7},{6,4},{7,5},{8,10},{9,11},{10,... | collective-permute-start | bytes 1419272 | tf_op jit(solution)/shard_map/ppermute | solution.py:325
  9.4 1.5 %collective-permute-start.3 = (bf16[56,4224]{1,0:T(8,128)(2,1)S(1)}, bf16[56,4224]{1,0:T(8,128)(2,1)S(1)}, u32[]{:S(2)}, u32[]{:S(2)}) collective-permute-start(bf16[56,4224]{1,0:T(8,128)(2,1)S(1)} %get-tuple-element.30.refs_0_.refs_5_), channel_id=1, source_target_pairs={{0,4},{1,5},{2,6},{3,7},{4,0},{5,1},{6,2},{7,3},{8,12},{9,13},{10,... | collective-permute-start | bytes 1419272 | tf_op jit(solution)/shard_map/ppermute | solution.py:325
  11.0 6.3 %collective-permute-done.refs_0_.refs_5_ = bf16[56,4224]{1,0:T(8,128)(2,1)S(1)} collective-permute-done((bf16[56,4224]{1,0:T(8,128)(2,1)S(1)}, bf16[56,4224]{1,0:T(8,128)(2,1)S(1)}, u32[]{:S(2)}, u32[]{:S(2)}) %collective-permute-start) | collective-permute-done | bytes 473120 | tf_op jit(solution)/shard_map/ppermute | solution.py:325
  17.2 1.4 %collective-permute-start.1 = (bf16[56,4224]{1,0:T(8,128)(2,1)S(1)}, bf16[56,4224]{1,0:T(8,128)(2,1)}, u32[]{:S(2)}, u32[]{:S(2)}) collective-permute-start(bf16[56,4224]{1,0:T(8,128)(2,1)S(1)} %collective-permute-done.refs_0_.refs_5_), channel_id=1, source_target_pairs={{8,16},{9,17},{10,18},{11,19},{12,20},{13,21},{14,22},{15,23},{16,... | collective-permute-start | bytes 1419272 | tf_op jit(solution)/shard_map/ppermute | solution.py:325
  18.7 1.3 collective-permute-start.13
  19.9 0.3 collective-permute-done.2.refs_1_.refs_6_
  20.3 1.6 %collective-permute-start.4 = (bf16[32,4224]{1,0:T(8,128)(2,1)S(1)}, bf16[32,4224]{1,0:T(8,128)(2,1)S(1)}, u32[]{:S(2)}, u32[]{:S(2)}) collective-permute-start(bf16[32,4224]{1,0:T(8,128)(2,1)S(1)} %slice.29), channel_id=1, source_target_pairs={{0,4},{1,5},{2,6},{3,7},{4,0},{5,1},{6,2},{7,3},{8,12},{9,13},{10,... | collective-permute-start | bytes 811016 | tf_op jit(solution)/shard_map/ppermute | solution.py:325
  21.9 1.6 %collective-permute-start.5 = (bf16[24,4224]{1,0:T(8,128)(2,1)S(1)}, bf16[24,4224]{1,0:T(8,128)(2,1)S(1)}, u32[]{:S(2)}, u32[]{:S(2)}) collective-permute-start(bf16[24,4224]{1,0:T(8,128)(2,1)S(1)} %slice.30), channel_id=1, source_target_pairs={{0,2},{1,3},{2,0},{3,1},{4,6},{5,7},{6,4},{7,5},{8,10},{9,11},{10,... | collective-permute-start | bytes 608264 | tf_op jit(solution)/shard_map/ppermute | solution.py:325
  23.4 0.7 xor_add_fusion.owners_ref
  24.2 0.6 collective-permute-start.7
  24.8 5.1 %collective-permute-done.5.refs_4_.refs_9_ = bf16[24,4224]{1,0:T(8,128)(2,1)S(1)} collective-permute-done((bf16[24,4224]{1,0:T(8,128)(2,1)S(1)}, bf16[24,4224]{1,0:T(8,128)(2,1)S(1)}, u32[]{:S(2)}, u32[]{:S(2)}) %collective-permute-start.5) | collective-permute-done | bytes 202784 | tf_op jit(solution)/shard_map/ppermute | solution.py:325
  29.9 1.1 collective-permute-start.8
  31.0 4.4 %collective-permute-start.10 = (bf16[24,4224]{1,0:T(8,128)(2,1)S(1)}, bf16[24,4224]{1,0:T(8,128)(2,1)S(1)}, u32[]{:S(2)}, u32[]{:S(2)}) collective-permute-start(bf16[24,4224]{1,0:T(8,128)(2,1)S(1)} %collective-permute-done.5.refs_4_.refs_9_), channel_id=1, source_target_pairs={{0,8},{1,9},{2,10},{3,11},{4,12},{5,13},{6,14},{7,15},{8,0},{9,1},... | collective-permute-start | bytes 608264 | tf_op jit(solution)/shard_map/ppermute | solution.py:325
  35.4 0.1 collective-permute-start.9
  35.5 0.8 collective-permute-done.13
  36.2 1.3 collective-permute-start.19
  37.5 1.1 broadcast_select_fusion.1.refs_0_.refs_5_
  38.6 1.7 %collective-permute-start.14 = (bf16[56,4224]{1,0:T(8,128)(2,1)S(1)}, bf16[56,4224]{1,0:T(8,128)(2,1)S(1)}, u32[]{:S(2)}, u32[]{:S(2)}) collective-permute-start(bf16[56,4224]{1,0:T(8,128)(2,1)S(1)} %broadcast_select_fusion.1.refs_0_.refs_5_), channel_id=1, source_target_pairs={{0,2},{1,3},{2,0},{3,1},{4,6},{5,7},{6,4},{7,5},{8,10},{9,11},{10,... | collective-permute-start | bytes 1419272 | tf_op jit(solution)/shard_map/ppermute | solution.py:325
  40.3 1.4 collective-permute-start.15
  41.7 1.8 %pick.4 = (bf16[96,4096]{1,0:T(8,128)(2,1)S(1)}, bf16[96,4096]{1,0:T(8,128)(2,1)S(1)}) custom-call(bf16[56,4224]{1,0:T(8,128)(2,1)S(1)} %get-tuple-element.30.refs_0_.refs_5_, bf16[56,4224]{1,0:T(8,128)(2,1)S(1)} %collective-permute-done.2.refs_1_.refs_6_, bf16[56,4224]{1,0:T(8,128)(2,1)S(1)} %collective-permute-done.3.refs_2_.refs_7_, ...), custom_call_target="tpu_custom_call" | custom-call | tf_op jit(solution)/shard_map/pick/pallas_call | solution.py:183
  43.6 10.7 %collective-permute-done.19 = bf16[56,4224]{1,0:T(8,128)(2,1)S(1)} collective-permute-done((bf16[56,4224]{1,0:T(8,128)(2,1)}, bf16[56,4224]{1,0:T(8,128)(2,1)S(1)}, u32[]{:S(2)}, u32[]{:S(2)}) %collective-permute-start.19) | collective-permute-done | bytes 473120 | tf_op jit(solution)/shard_map/ppermute | solution.py:325
  54.3 0.1 broadcast_select_fusion.refs_0_.refs_5_
  54.5 1.6 %collective-permute-start.20 = (bf16[56,4224]{1,0:T(8,128)(2,1)S(1)}, bf16[56,4224]{1,0:T(8,128)(2,1)S(1)}, u32[]{:S(2)}, u32[]{:S(2)}) collective-permute-start(bf16[56,4224]{1,0:T(8,128)(2,1)S(1)} %broadcast_select_fusion.refs_0_.refs_5_), channel_id=1, source_target_pairs={{0,2},{1,3},{2,0},{3,1},{4,6},{5,7},{6,4},{7,5},{8,10},{9,11},{10,... | collective-permute-start | bytes 1419272 | tf_op jit(solution)/shard_map/ppermute | solution.py:325
  56.0 1.5 %collective-permute-start.21 = (bf16[56,4224]{1,0:T(8,128)(2,1)S(1)}, bf16[56,4224]{1,0:T(8,128)(2,1)S(1)}, u32[]{:S(2)}, u32[]{:S(2)}) collective-permute-start(bf16[56,4224]{1,0:T(8,128)(2,1)S(1)} %broadcast_select_fusion.refs_0_.refs_5_), channel_id=1, source_target_pairs={{0,4},{1,5},{2,6},{3,7},{4,0},{5,1},{6,2},{7,3},{8,12},{9,13},{10,... | collective-permute-start | bytes 1419272 | tf_op jit(solution)/shard_map/ppermute | solution.py:325
  57.5 0.5 collective-permute-start.16
  58.0 0.5 collective-permute-start.17
  58.6 1.8 %pick.5 = (bf16[96,4096]{1,0:T(8,128)(2,1)S(1)}, bf16[96,4096]{1,0:T(8,128)(2,1)S(1)}) custom-call(bf16[56,4224]{1,0:T(8,128)(2,1)S(1)} %collective-permute-done.refs_0_.refs_5_, bf16[56,4224]{1,0:T(8,128)(2,1)S(1)} %collective-permute-done.7.refs_1_.refs_6_, bf16[56,4224]{1,0:T(8,128)(2,1)S(1)} %collective-permute-done.8.refs_2_.refs_7_, ...), custom_call_target="tpu_custom_call" | custom-call | tf_op jit(solution)/shard_map/pick/pallas_call | solution.py:183
  60.4 6.1 %collective-permute-done.20.refs_1_.refs_6_ = bf16[56,4224]{1,0:T(8,128)(2,1)S(1)} collective-permute-done((bf16[56,4224]{1,0:T(8,128)(2,1)S(1)}, bf16[56,4224]{1,0:T(8,128)(2,1)S(1)}, u32[]{:S(2)}, u32[]{:S(2)}) %collective-permute-start.20) | collective-permute-done | bytes 473120 | tf_op jit(solution)/shard_map/ppermute | solution.py:325
  66.6 1.9 %collective-permute-done.21.refs_2_.refs_7_ = bf16[56,4224]{1,0:T(8,128)(2,1)S(1)} collective-permute-done((bf16[56,4224]{1,0:T(8,128)(2,1)S(1)}, bf16[56,4224]{1,0:T(8,128)(2,1)S(1)}, u32[]{:S(2)}, u32[]{:S(2)}) %collective-permute-start.21) | collective-permute-done | bytes 473120 | tf_op jit(solution)/shard_map/ppermute | solution.py:325
  68.5 0.2 collective-permute-done.17.refs_4_.refs_9_
  68.7 4.1 %collective-permute-done.16.refs_3_.refs_8_ = bf16[32,4224]{1,0:T(8,128)(2,1)S(1)} collective-permute-done((bf16[32,4224]{1,0:T(8,128)(2,1)S(1)}, bf16[32,4224]{1,0:T(8,128)(2,1)S(1)}, u32[]{:S(2)}, u32[]{:S(2)}) %collective-permute-start.16) | collective-permute-done | bytes 270368 | tf_op jit(solution)/shard_map/ppermute | solution.py:325
  72.8 1.5 %collective-permute-start.22 = (bf16[32,4224]{1,0:T(8,128)(2,1)S(1)}, bf16[32,4224]{1,0:T(8,128)(2,1)S(1)}, u32[]{:S(2)}, u32[]{:S(2)}) collective-permute-start(bf16[32,4224]{1,0:T(8,128)(2,1)S(1)} %slice.33), channel_id=1, source_target_pairs={{0,4},{1,5},{2,6},{3,7},{4,0},{5,1},{6,2},{7,3},{8,12},{9,13},{10,... | collective-permute-start | bytes 811016 | tf_op jit(solution)/shard_map/ppermute | solution.py:325
  74.3 0.5 collective-permute-start.23
  74.9 0.5 collective-permute-start.11
  75.4 1.8 %pick.6 = (bf16[96,4096]{1,0:T(8,128)(2,1)S(1)}, bf16[96,4096]{1,0:T(8,128)(2,1)S(1)}) custom-call(bf16[56,4224]{1,0:T(8,128)(2,1)S(1)} %broadcast_select_fusion.1.refs_0_.refs_5_, bf16[56,4224]{1,0:T(8,128)(2,1)S(1)} %collective-permute-done.14.refs_1_.refs_6_, bf16[56,4224]{1,0:T(8,128)(2,1)S(1)} %collective-permute-done.15.refs_2_.refs_7_, ...), custom_call_target="tpu_custom_call" | custom-call | tf_op jit(solution)/shard_map/pick/pallas_call | solution.py:183
  77.2 0.1 collective-permute-start.18
  77.3 2.8 %collective-permute-done.23.refs_4_.refs_9_ = bf16[24,4224]{1,0:T(8,128)(2,1)S(1)} collective-permute-done((bf16[24,4224]{1,0:T(8,128)(2,1)S(1)}, bf16[24,4224]{1,0:T(8,128)(2,1)S(1)}, u32[]{:S(2)}, u32[]{:S(2)}) %collective-permute-start.23) | collective-permute-done | bytes 202784 | tf_op jit(solution)/shard_map/ppermute | solution.py:325
  80.1 1.8 %pick.7 = (bf16[96,4096]{1,0:T(8,128)(2,1)S(1)}, bf16[96,4096]{1,0:T(8,128)(2,1)S(1)}) custom-call(bf16[56,4224]{1,0:T(8,128)(2,1)S(1)} %broadcast_select_fusion.refs_0_.refs_5_, bf16[56,4224]{1,0:T(8,128)(2,1)S(1)} %collective-permute-done.20.refs_1_.refs_6_, bf16[56,4224]{1,0:T(8,128)(2,1)S(1)} %collective-permute-done.21.refs_2_.refs_7_, ...), custom_call_target="tpu_custom_call" | custom-call | tf_op jit(solution)/shard_map/pick/pallas_call | solution.py:183
  81.9 0.9 copy-done.3
  82.8 0.0 copy-start.10
  82.8 2.3 %collective-permute-done.24.refs_7_ = bf16[96,4096]{1,0:T(8,128)(2,1)S(1)} collective-permute-done((bf16[96,4096]{1,0:T(8,128)(2,1)S(1)}, bf16[96,4096]{1,0:T(8,128)(2,1)S(1)}, u32[]{:S(2)}, u32[]{:S(2)}) %collective-permute-start.24) | collective-permute-done | bytes 786464 | tf_op jit(solution)/shard_map/ppermute | solution.py:325
  85.1 0.9 copy-done.11
  86.0 17.9 %experts.1 = bf16[32,24,768]{2,1,0:T(8,128)(2,1)} custom-call(s32[32]{0:T(128)S(1)} %xor_add_fusion.owners_ref, bf16[96,4096]{1,0:T(8,128)(2,1)S(1)} %get-tuple-element.25.refs_0_, bf16[96,4096]{1,0:T(8,128)(2,1)S(1)} %collective-permute-done.6.refs_1_, bf16[96,4096]{1,0:T(8,128)(2,1)S(1)} %get-tuple-element.28.refs_2_, ...), custom_call_target="tpu_custom_call" | custom-call | tf_op jit(solution)/shard_map/experts/pallas_call | solution.py:242
  103.9 0.0 copy-start.12
  103.9 0.0 copy-start
  103.9 0.0 copy-start.5
  103.9 0.0 copy-start.6
  103.9 0.0 copy-start.9
  103.9 2.8 %all-to-all-start = ((bf16[32,24,768]{2,1,0:T(8,128)(2,1)}), bf16[32,24,768]{2,1,0:T(8,128)(2,1)S(1)}, u32[]{:S(2)}, u32[]{:S(2)}) async-start(bf16[32,24,768]{2,1,0:T(8,128)(2,1)} %experts.1), calls=%async_computation | async-start | bytes 2359296 | tf_op jit(solution)/shard_map/all_to_all | solution.py:408
  106.8 0.1 copy.23
  106.9 0.0 copy-start.1
  106.9 1.5 %copy-done.1 = bf16[14,128,512]{2,1,0:T(8,128)(2,1)S(1)} copy-done((bf16[14,128,512]{2,1,0:T(8,128)(2,1)S(1)}, bf16[14,128,512]{2,1,0:T(8,128)(2,1)}, u32[]{:S(2)}) %copy-start.1) | copy-done | bytes 1835032
  108.4 1.2 copy-done.2
  109.6 8.1 %attention.1 = bf16[14,4,8192]{2,1,0:T(4,128)(2,1)} custom-call(s32[14]{0:T(128)S(1)} %copy-done.9, bf16[14,4,8192]{2,1,0:T(4,128)(2,1)S(1)} %bitcast.11, bf16[14,4,512]{2,1,0:T(4,128)(2,1)S(1)} %bitcast.14, bf16[14,4,512]{2,1,0:T(4,128)(2,1)S(1)} %bitcast.15, bf16[14,128,512]{2,1,0:T(8,128)(2,1)S(1)} %copy-done, bf16[14,128,512]{2,1,0:T(8,128)(2,1)S(1)} %copy-done.1), custom_call_target="tpu_custom_call" | custom-call | tf_op jit(solution)/shard_map/attention/pallas_call | solution.py:64
  117.7 18.2 %all-to-all-done = bf16[32,24,768]{2,1,0:T(8,128)(2,1)S(1)} async-done(((bf16[32,24,768]{2,1,0:T(8,128)(2,1)}), bf16[32,24,768]{2,1,0:T(8,128)(2,1)S(1)}, u32[]{:S(2)}, u32[]{:S(2)}) %all-to-all-start) | async-done | bytes 1179680 | tf_op jit(solution)/shard_map/all_to_all | solution.py:408
  135.9 1.6 %combine.1 = bf16[14,4,6144]{2,1,0:T(4,128)(2,1)} custom-call(bf16[768,768]{1,0:T(8,128)(2,1)S(1)} %bitcast.10, s32[56,128]{1,0:T(8,128)S(1)} %get-tuple-element.21.columns_ref, f32[56,8]{1,0:T(8,128)S(1)} %bitcast.13), custom_call_target="tpu_custom_call" | custom-call | tf_op jit(solution)/shard_map/combine/pallas_call | solution.py:288
  (34 shorter events, 0.2 us)
Async XLA Ops:
  0.6 41.1 %copy-start.7 = (f32[1,224]{1,0:T(1,128)S(1)}, f32[1,224]{1,0:T(1,128)}, u32[]{:S(2)}) copy-start(f32[1,224]{1,0:T(1,128)} %constant.115.refs_10_) | copy-start | bytes 2692
  0.6 1.0 copy-start.4
  1.7 0.7 copy-start.8
  3.3 13.9 %collective-permute-start = (bf16[56,4224]{1,0:T(8,128)(2,1)S(1)}, bf16[56,4224]{1,0:T(8,128)(2,1)S(1)}, u32[]{:S(2)}, u32[]{:S(2)}) collective-permute-start(bf16[56,4224]{1,0:T(8,128)(2,1)S(1)} %get-tuple-element.30.refs_0_.refs_5_), channel_id=1, source_target_pairs={{0,8},{1,9},{2,10},{3,11},{4,12},{5,13},{6,14},{7,15},{8,0},{9,1},... | collective-permute-start | bytes 1419272 | tf_op jit(solution)/shard_map/ppermute | solution.py:325
  7.2 11.5 %collective-permute-start.12 = (bf16[56,4224]{1,0:T(8,128)(2,1)S(1)}, bf16[56,4224]{1,0:T(8,128)(2,1)S(1)}, u32[]{:S(2)}, u32[]{:S(2)}) collective-permute-start(bf16[56,4224]{1,0:T(8,128)(2,1)S(1)} %get-tuple-element.30.refs_0_.refs_5_), channel_id=1, source_target_pairs={{8,16},{9,17},{10,18},{11,19},{12,20},{13,21},{14,22},{15,23},{16,... | collective-permute-start | bytes 1419272 | tf_op jit(solution)/shard_map/ppermute | solution.py:325
  7.9 12.4 %collective-permute-start.2 = (bf16[56,4224]{1,0:T(8,128)(2,1)S(1)}, bf16[56,4224]{1,0:T(8,128)(2,1)S(1)}, u32[]{:S(2)}, u32[]{:S(2)}) collective-permute-start(bf16[56,4224]{1,0:T(8,128)(2,1)S(1)} %get-tuple-element.30.refs_0_.refs_5_), channel_id=1, source_target_pairs={{0,2},{1,3},{2,0},{3,1},{4,6},{5,7},{6,4},{7,5},{8,10},{9,11},{10,... | collective-permute-start | bytes 1419272 | tf_op jit(solution)/shard_map/ppermute | solution.py:325
  9.4 12.4 %collective-permute-start.3 = (bf16[56,4224]{1,0:T(8,128)(2,1)S(1)}, bf16[56,4224]{1,0:T(8,128)(2,1)S(1)}, u32[]{:S(2)}, u32[]{:S(2)}) collective-permute-start(bf16[56,4224]{1,0:T(8,128)(2,1)S(1)} %get-tuple-element.30.refs_0_.refs_5_), channel_id=1, source_target_pairs={{0,4},{1,5},{2,6},{3,7},{4,0},{5,1},{6,2},{7,3},{8,12},{9,13},{10,... | collective-permute-start | bytes 1419272 | tf_op jit(solution)/shard_map/ppermute | solution.py:325
  17.2 18.2 %collective-permute-start.1 = (bf16[56,4224]{1,0:T(8,128)(2,1)S(1)}, bf16[56,4224]{1,0:T(8,128)(2,1)}, u32[]{:S(2)}, u32[]{:S(2)}) collective-permute-start(bf16[56,4224]{1,0:T(8,128)(2,1)S(1)} %collective-permute-done.refs_0_.refs_5_), channel_id=1, source_target_pairs={{8,16},{9,17},{10,18},{11,19},{12,20},{13,21},{14,22},{15,23},{16,... | collective-permute-start | bytes 1419272 | tf_op jit(solution)/shard_map/ppermute | solution.py:325
  18.7 17.6 %collective-permute-start.13 = (bf16[56,4224]{1,0:T(8,128)(2,1)S(1)}, bf16[56,4224]{1,0:T(8,128)(2,1)}, u32[]{:S(2)}, u32[]{:S(2)}) collective-permute-start(bf16[56,4224]{1,0:T(8,128)(2,1)S(1)} %collective-permute-done.12), channel_id=1, source_target_pairs={{8,0},{9,1},{10,2},{11,3},{12,4},{13,5},{14,6},{15,7},{16,24},{17,... | collective-permute-start | bytes 1419272 | tf_op jit(solution)/shard_map/ppermute | solution.py:325
  20.3 10.8 %collective-permute-start.4 = (bf16[32,4224]{1,0:T(8,128)(2,1)S(1)}, bf16[32,4224]{1,0:T(8,128)(2,1)S(1)}, u32[]{:S(2)}, u32[]{:S(2)}) collective-permute-start(bf16[32,4224]{1,0:T(8,128)(2,1)S(1)} %slice.29), channel_id=1, source_target_pairs={{0,4},{1,5},{2,6},{3,7},{4,0},{5,1},{6,2},{7,3},{8,12},{9,13},{10,... | collective-permute-start | bytes 811016 | tf_op jit(solution)/shard_map/ppermute | solution.py:325
  21.9 8.0 %collective-permute-start.5 = (bf16[24,4224]{1,0:T(8,128)(2,1)S(1)}, bf16[24,4224]{1,0:T(8,128)(2,1)S(1)}, u32[]{:S(2)}, u32[]{:S(2)}) collective-permute-start(bf16[24,4224]{1,0:T(8,128)(2,1)S(1)} %slice.30), channel_id=1, source_target_pairs={{0,2},{1,3},{2,0},{3,1},{4,6},{5,7},{6,4},{7,5},{8,10},{9,11},{10,... | collective-permute-start | bytes 608264 | tf_op jit(solution)/shard_map/ppermute | solution.py:325
  24.2 14.4 %collective-permute-start.7 = (bf16[56,4224]{1,0:T(8,128)(2,1)S(1)}, bf16[56,4224]{1,0:T(8,128)(2,1)S(1)}, u32[]{:S(2)}, u32[]{:S(2)}) collective-permute-start(bf16[56,4224]{1,0:T(8,128)(2,1)S(1)} %collective-permute-done.refs_0_.refs_5_), channel_id=1, source_target_pairs={{0,2},{1,3},{2,0},{3,1},{4,6},{5,7},{6,4},{7,5},{8,10},{9,11},{10,... | collective-permute-start | bytes 1419272 | tf_op jit(solution)/shard_map/ppermute | solution.py:325
  29.9 8.7 %collective-permute-start.8 = (bf16[56,4224]{1,0:T(8,128)(2,1)S(1)}, bf16[56,4224]{1,0:T(8,128)(2,1)S(1)}, u32[]{:S(2)}, u32[]{:S(2)}) collective-permute-start(bf16[56,4224]{1,0:T(8,128)(2,1)S(1)} %collective-permute-done.refs_0_.refs_5_), channel_id=1, source_target_pairs={{0,4},{1,5},{2,6},{3,7},{4,0},{5,1},{6,2},{7,3},{8,12},{9,13},{10,... | collective-permute-start | bytes 1419272 | tf_op jit(solution)/shard_map/ppermute | solution.py:325
  31.0 23.4 %collective-permute-start.10 = (bf16[24,4224]{1,0:T(8,128)(2,1)S(1)}, bf16[24,4224]{1,0:T(8,128)(2,1)S(1)}, u32[]{:S(2)}, u32[]{:S(2)}) collective-permute-start(bf16[24,4224]{1,0:T(8,128)(2,1)S(1)} %collective-permute-done.5.refs_4_.refs_9_), channel_id=1, source_target_pairs={{0,8},{1,9},{2,10},{3,11},{4,12},{5,13},{6,14},{7,15},{8,0},{9,1},... | collective-permute-start | bytes 608264 | tf_op jit(solution)/shard_map/ppermute | solution.py:325
  35.4 19.0 %collective-permute-start.9 = (bf16[32,4224]{1,0:T(8,128)(2,1)S(1)}, bf16[32,4224]{1,0:T(8,128)(2,1)S(1)}, u32[]{:S(2)}, u32[]{:S(2)}) collective-permute-start(bf16[32,4224]{1,0:T(8,128)(2,1)S(1)} %collective-permute-done.4.refs_3_.refs_8_), channel_id=1, source_target_pairs={{0,8},{1,9},{2,10},{3,11},{4,12},{5,13},{6,14},{7,15},{8,0},{9,1},... | collective-permute-start | bytes 811016 | tf_op jit(solution)/shard_map/ppermute | solution.py:325
  36.2 18.1 %collective-permute-start.19 = (bf16[56,4224]{1,0:T(8,128)(2,1)}, bf16[56,4224]{1,0:T(8,128)(2,1)S(1)}, u32[]{:S(2)}, u32[]{:S(2)}) collective-permute-start(bf16[56,4224]{1,0:T(8,128)(2,1)} %collective-permute-done.1), channel_id=1, source_target_pairs={{8,0},{9,1},{10,2},{11,3},{12,4},{13,5},{14,6},{15,7},{16,24},{17,... | collective-permute-start | bytes 1419272 | tf_op jit(solution)/shard_map/ppermute | solution.py:325
  38.6 15.7 %collective-permute-start.14 = (bf16[56,4224]{1,0:T(8,128)(2,1)S(1)}, bf16[56,4224]{1,0:T(8,128)(2,1)S(1)}, u32[]{:S(2)}, u32[]{:S(2)}) collective-permute-start(bf16[56,4224]{1,0:T(8,128)(2,1)S(1)} %broadcast_select_fusion.1.refs_0_.refs_5_), channel_id=1, source_target_pairs={{0,2},{1,3},{2,0},{3,1},{4,6},{5,7},{6,4},{7,5},{8,10},{9,11},{10,... | collective-permute-start | bytes 1419272 | tf_op jit(solution)/shard_map/ppermute | solution.py:325
  40.3 14.1 %collective-permute-start.15 = (bf16[56,4224]{1,0:T(8,128)(2,1)S(1)}, bf16[56,4224]{1,0:T(8,128)(2,1)S(1)}, u32[]{:S(2)}, u32[]{:S(2)}) collective-permute-start(bf16[56,4224]{1,0:T(8,128)(2,1)S(1)} %broadcast_select_fusion.1.refs_0_.refs_5_), channel_id=1, source_target_pairs={{0,4},{1,5},{2,6},{3,7},{4,0},{5,1},{6,2},{7,3},{8,12},{9,13},{10,... | collective-permute-start | bytes 1419272 | tf_op jit(solution)/shard_map/ppermute | solution.py:325
  54.5 12.1 %collective-permute-start.20 = (bf16[56,4224]{1,0:T(8,128)(2,1)S(1)}, bf16[56,4224]{1,0:T(8,128)(2,1)S(1)}, u32[]{:S(2)}, u32[]{:S(2)}) collective-permute-start(bf16[56,4224]{1,0:T(8,128)(2,1)S(1)} %broadcast_select_fusion.refs_0_.refs_5_), channel_id=1, source_target_pairs={{0,2},{1,3},{2,0},{3,1},{4,6},{5,7},{6,4},{7,5},{8,10},{9,11},{10,... | collective-permute-start | bytes 1419272 | tf_op jit(solution)/shard_map/ppermute | solution.py:325
  56.0 12.5 %collective-permute-start.21 = (bf16[56,4224]{1,0:T(8,128)(2,1)S(1)}, bf16[56,4224]{1,0:T(8,128)(2,1)S(1)}, u32[]{:S(2)}, u32[]{:S(2)}) collective-permute-start(bf16[56,4224]{1,0:T(8,128)(2,1)S(1)} %broadcast_select_fusion.refs_0_.refs_5_), channel_id=1, source_target_pairs={{0,4},{1,5},{2,6},{3,7},{4,0},{5,1},{6,2},{7,3},{8,12},{9,13},{10,... | collective-permute-start | bytes 1419272 | tf_op jit(solution)/shard_map/ppermute | solution.py:325
  57.5 15.3 %collective-permute-start.16 = (bf16[32,4224]{1,0:T(8,128)(2,1)S(1)}, bf16[32,4224]{1,0:T(8,128)(2,1)S(1)}, u32[]{:S(2)}, u32[]{:S(2)}) collective-permute-start(bf16[32,4224]{1,0:T(8,128)(2,1)S(1)} %slice.31), channel_id=1, source_target_pairs={{0,4},{1,5},{2,6},{3,7},{4,0},{5,1},{6,2},{7,3},{8,12},{9,13},{10,... | collective-permute-start | bytes 811016 | tf_op jit(solution)/shard_map/ppermute | solution.py:325
  58.0 10.7 %collective-permute-start.17 = (bf16[24,4224]{1,0:T(8,128)(2,1)S(1)}, bf16[24,4224]{1,0:T(8,128)(2,1)S(1)}, u32[]{:S(2)}, u32[]{:S(2)}) collective-permute-start(bf16[24,4224]{1,0:T(8,128)(2,1)S(1)} %slice.32), channel_id=1, source_target_pairs={{0,2},{1,3},{2,0},{3,1},{4,6},{5,7},{6,4},{7,5},{8,10},{9,11},{10,... | collective-permute-start | bytes 608264 | tf_op jit(solution)/shard_map/ppermute | solution.py:325
  72.8 7.3 %collective-permute-start.22 = (bf16[32,4224]{1,0:T(8,128)(2,1)S(1)}, bf16[32,4224]{1,0:T(8,128)(2,1)S(1)}, u32[]{:S(2)}, u32[]{:S(2)}) collective-permute-start(bf16[32,4224]{1,0:T(8,128)(2,1)S(1)} %slice.33), channel_id=1, source_target_pairs={{0,4},{1,5},{2,6},{3,7},{4,0},{5,1},{6,2},{7,3},{8,12},{9,13},{10,... | collective-permute-start | bytes 811016 | tf_op jit(solution)/shard_map/ppermute | solution.py:325
  74.3 5.7 %collective-permute-start.23 = (bf16[24,4224]{1,0:T(8,128)(2,1)S(1)}, bf16[24,4224]{1,0:T(8,128)(2,1)S(1)}, u32[]{:S(2)}, u32[]{:S(2)}) collective-permute-start(bf16[24,4224]{1,0:T(8,128)(2,1)S(1)} %slice.34), channel_id=1, source_target_pairs={{0,2},{1,3},{2,0},{3,1},{4,6},{5,7},{6,4},{7,5},{8,10},{9,11},{10,... | collective-permute-start | bytes 608264 | tf_op jit(solution)/shard_map/ppermute | solution.py:325
  74.9 7.9 %collective-permute-start.6 = (bf16[96,4096]{1,0:T(8,128)(2,1)S(1)}, bf16[96,4096]{1,0:T(8,128)(2,1)S(1)}, u32[]{:S(2)}, u32[]{:S(2)}) collective-permute-start(bf16[96,4096]{1,0:T(8,128)(2,1)S(1)} %get-tuple-element.26), channel_id=1, source_target_pairs={{0,1},{1,0},{2,3},{3,2},{4,5},{5,4},{6,7},{7,6},{8,9},{9,8},{10,11... | collective-permute-start | bytes 2359304 | tf_op jit(solution)/shard_map/ppermute | solution.py:325
  74.9 7.9 %collective-permute-start.11 = (bf16[96,4096]{1,0:T(8,128)(2,1)S(1)}, bf16[96,4096]{1,0:T(8,128)(2,1)S(1)}, u32[]{:S(2)}, u32[]{:S(2)}) collective-permute-start(bf16[96,4096]{1,0:T(8,128)(2,1)S(1)} %get-tuple-element.29), channel_id=1, source_target_pairs={{0,1},{1,0},{2,3},{3,2},{4,5},{5,4},{6,7},{7,6},{8,9},{9,8},{10,11... | collective-permute-start | bytes 2359304 | tf_op jit(solution)/shard_map/ppermute | solution.py:325
  77.2 5.6 %collective-permute-start.18 = (bf16[96,4096]{1,0:T(8,128)(2,1)S(1)}, bf16[96,4096]{1,0:T(8,128)(2,1)S(1)}, u32[]{:S(2)}, u32[]{:S(2)}) collective-permute-start(bf16[96,4096]{1,0:T(8,128)(2,1)S(1)} %get-tuple-element.33), channel_id=1, source_target_pairs={{0,1},{1,0},{2,3},{3,2},{4,5},{5,4},{6,7},{7,6},{8,9},{9,8},{10,11... | collective-permute-start | bytes 2359304 | tf_op jit(solution)/shard_map/ppermute | solution.py:325
  81.9 0.9 copy-start.3
  82.8 2.3 %collective-permute-start.24 = (bf16[96,4096]{1,0:T(8,128)(2,1)S(1)}, bf16[96,4096]{1,0:T(8,128)(2,1)S(1)}, u32[]{:S(2)}, u32[]{:S(2)}) collective-permute-start(bf16[96,4096]{1,0:T(8,128)(2,1)S(1)} %get-tuple-element.38), channel_id=1, source_target_pairs={{0,1},{1,0},{2,3},{3,2},{4,5},{5,4},{6,7},{7,6},{8,9},{9,8},{10,11... | collective-permute-start | bytes 2359304 | tf_op jit(solution)/shard_map/ppermute | solution.py:325
  82.8 2.3 %copy-start.10 = (bf16[96,4096]{1,0:T(8,128)(2,1)}, bf16[96,4096]{1,0:T(8,128)(2,1)S(1)}, u32[]{:S(2)}) copy-start(bf16[96,4096]{1,0:T(8,128)(2,1)S(1)} %collective-permute-done.18.refs_5_) | copy-start | bytes 2359300
  85.1 0.9 copy-start.11
  103.9 2.9 %copy-start.12 = (f32[4,14,8]{1,2,0:T(8,128)S(1)}, f32[4,14,8]{1,2,0:T(8,128)}, u32[]{:S(2)}) copy-start(f32[4,14,8]{1,2,0:T(8,128)} %param.23) | copy-start | bytes 5380
  103.9 3.0 %copy-start = (bf16[14,128,512]{2,1,0:T(8,128)(2,1)S(1)}, bf16[14,128,512]{2,1,0:T(8,128)(2,1)}, u32[]{:S(2)}) copy-start(bf16[14,128,512]{2,1,0:T(8,128)(2,1)} %k_ref.1) | copy-start | bytes 5505028
  103.9 3.0 %copy-start.5 = (bf16[4,14,512]{2,0,1:T(4,128)(2,1)S(1)}, bf16[4,14,512]{2,0,1:T(4,128)(2,1)}, u32[]{:S(2)}) copy-start(bf16[4,14,512]{2,0,1:T(4,128)(2,1)} %param.27) | copy-start | bytes 172036
  103.9 3.0 %copy-start.6 = (bf16[4,14,512]{2,0,1:T(4,128)(2,1)S(1)}, bf16[4,14,512]{2,0,1:T(4,128)(2,1)}, u32[]{:S(2)}) copy-start(bf16[4,14,512]{2,0,1:T(4,128)(2,1)} %param.28) | copy-start | bytes 172036
  103.9 3.0 %copy-start.9 = (s32[14]{0:T(128)S(1)}, s32[14]{0:T(128)}, u32[]{:S(2)}) copy-start(s32[14]{0:T(128)} %lengths_ref) | copy-start | bytes 172
  103.9 31.9 %all-to-all-start = ((bf16[32,24,768]{2,1,0:T(8,128)(2,1)}), bf16[32,24,768]{2,1,0:T(8,128)(2,1)S(1)}, u32[]{:S(2)}, u32[]{:S(2)}) async-start(bf16[32,24,768]{2,1,0:T(8,128)(2,1)} %experts.1), calls=%async_computation | async-start | bytes 2359296 | tf_op jit(solution)/shard_map/all_to_all | solution.py:408
  106.9 1.5 %copy-start.1 = (bf16[14,128,512]{2,1,0:T(8,128)(2,1)S(1)}, bf16[14,128,512]{2,1,0:T(8,128)(2,1)}, u32[]{:S(2)}) copy-start(bf16[14,128,512]{2,1,0:T(8,128)(2,1)} %v_ref.1) | copy-start | bytes 5505028
  108.4 1.2 copy-start.2

commit v4 on v3

--- a/solution.py
+++ b/solution.py
@@ -194,8 +194,10 @@
     )(*arrays, *arrays, group, wanted)
 
 
-def expert_kernel(owners_ref, *refs, count, part):
-    x_refs, (gate_ref, up_ref, out_ref, rows_ref, arrived) = refs[:count], refs[count:]
+def expert_kernel(owners_ref, *refs, count, part, earlier):
+    x_refs, refs = refs[:count], refs[count:]
+    done_ref, refs = (refs[0], refs[1:]) if earlier else (None, refs)
+    gate_ref, up_ref, out_ref, rows_ref, arrived = refs
     hidden_part, expert = pl.program_id(0), pl.program_id(1)
     experts_local = rows_ref.shape[0]
     span = out_ref.shape[1] // experts_local
@@ -220,6 +222,13 @@
             for number in range(count):
                 copy(number, which).wait()
 
+    if earlier:
+
+        @pl.when(expert == 0)
+        def _():
+            first = owners_ref[owners_ref.shape[0] - 1]
+            out_ref[pl.ds(first, done_ref.shape[0])] = done_ref[...]
+
     rows = rows_ref[expert]
     gate = jnp.dot(rows, gate_ref[0], preferred_element_type=jnp.float32)
     up = jnp.dot(rows, up_ref[0], preferred_element_type=jnp.float32)
@@ -228,28 +237,33 @@
 
         @pl.when(expert == which)
         def _():
-            for group in range(owners_ref.shape[0]):
+            for group in range(rows_ref.shape[1] // span):
                 out_ref[owners_ref[group], which * span : (which + 1) * span, :] = inner[
                     group * span : (group + 1) * span
                 ]
 
 
-def run_experts(arrays, owners, span, w_gate, w_up):
+def run_experts(arrays, owners, span, w_gate, w_up, earlier=None):
     experts_local, width, hidden = w_gate.shape
     part, count = arrays[0].shape[0] // experts_local, len(arrays)
     rows = count * part
     block = 2 * LANES
+    done = [] if earlier is None else [earlier]
+    places = rows // span + sum(a.shape[0] for a in done)
     return pl.pallas_call(
-        functools.partial(expert_kernel, count=count, part=part),
+        functools.partial(
+            expert_kernel, count=count, part=part, earlier=earlier is not None
+        ),
         grid=(hidden // block, experts_local),
         in_specs=[pl.BlockSpec(memory_space=pltpu.SMEM)]
         + [pl.BlockSpec(memory_space=pl.ANY)] * count
+        + [pl.BlockSpec(a.shape[:2] + (block,), lambda f, e: (0, 0, f)) for a in done]
         + [pl.BlockSpec((1, width, block), lambda f, e: (e, 0, f))] * 2,
         out_specs=pl.BlockSpec(
-            (owners.shape[0], experts_local * span, block), lambda f, e: (0, 0, f)
+            (places, experts_local * span, block), lambda f, e: (0, 0, f)
         ),
         out_shape=jax.ShapeDtypeStruct(
-            (owners.shape[0], experts_local * span, hidden), jnp.bfloat16
+            (places, experts_local * span, hidden), jnp.bfloat16
         ),
         scratch_shapes=[
             pltpu.VMEM((experts_local, rows, width), jnp.bfloat16),
@@ -257,7 +271,7 @@
         ],
         compiler_params=pltpu.CompilerParams(vmem_limit_bytes=EXPERT_VMEM),
         name="experts",
-    )(owners, *arrays, w_gate, w_up)
+    )(owners, *arrays, *done, w_gate, w_up)
 
 
 def combine_kernel(back_ref, columns_ref, gates_ref, out_ref):
@@ -394,7 +408,11 @@
         add_item([own, column, row, *far])
         own = after(jnp.where(inner, far_plane, far_out), *halves, *past, keeps[0])
         column, row = send(own, to_column), send(own, to_row)
-        halves = lax.optimization_barrier((column[:cut], row[cut:], *far, keeps[1]))[:2]
+        split = 2 * INNER
+        early = run_experts(
+            blocks[:4], owners[:split] % split, slot_span, gate_full, up_full
+        )
+        halves = lax.optimization_barrier((column[:cut], row[cut:], *far, early))[:2]
         far = send(halves[0], to_row), send(halves[1], to_column)
         add_item([own, column, row, *far])
     else:
@@ -404,7 +422,11 @@
                 column, row = send(own, to_column), send(own, to_row)
             far = send(column[:cut], to_row), send(row[cut:], to_column)
             add_item([own, column, row, *far])
-    outgoing = run_experts(blocks, owners, slot_span, gate_full, up_full)
+    if lines == 4:
+        places = jnp.concatenate([owners[split:], (z // 2 * split)[None]])
+        outgoing = run_experts(blocks[4:], places, slot_span, gate_full, up_full, early)
+    else:
+        outgoing = run_experts(blocks, owners, slot_span, gate_full, up_full)
     returned = lax.all_to_all(outgoing, "expert", split_axis=0, concat_axis=0, tiled=True)
     attn_out = attention(
         queries, new_keys, new_values, cache_keys, cache_values, after(lengths, outgoing)

time: 138 us -> 134 us (0.971)
  waiting for transfers between devices: 58.7 us -> 45 us
  Pallas kernels: 35.9 us -> 47.4 us
    ppermute x25, waiting for transfers between devices: 40.5 us -> 26.9 us  [per_device(): lax.ppermute(array, 'expert', moves(peers, target))]
    pallas_call x1 -> x2, Pallas kernels: 17.9 us -> 28 us  [run_experts(): pl.pallas_call(functools.partial(expert_kernel, count=count, part=part, e...]
    unnamed x26 -> x20, local copies, waits for them, and re-layouts: 6.2 us -> 4.45 us
  transfers between devices with their start and end apart: 26 -> 26, of which waited for: 12 -> 11; matrix products, arithmetic and copies ran while one was open for 2% -> 2% of each run, Pallas kernels for 11% -> 23%
where the time goes in v4:
time: 134 us
  Pallas kernels  47.4 us (35%)
  waiting for transfers between devices  45 us (34%)
  starting transfers between devices  33.3 us (25%)
  local copies, waits for them, and re-layouts  5.44 us (4%)
  other arithmetic  1.73 us (1%)
    ppermute x25, starting transfers between devices, per_device(): lax.ppermute(array, 'expert', moves(peers, target))  29.5 us
    pallas_call x2, Pallas kernels, run_experts(): pl.pallas_call(functools.partial(expert_kernel, count=count, part=part, e...  28 us
    ppermute x25, waiting for transfers between devices, per_device(): lax.ppermute(array, 'expert', moves(peers, target))  26.9 us
    all_to_all x1, waiting for transfers between devices, per_device(): lax.all_to_all(outgoing, 'expert', split_axis=0, concat_axis=0, tiled=True)  18.2 us
    pallas_call x4, Pallas kernels, pick(): pl.pallas_call(functools.partial(pick_kernel, parts=len(sources)), grid=(...  8.76 us
    pallas_call x1, Pallas kernels, attention(): pl.pallas_call(functools.partial(attention_kernel, groups=groups), grid=(...  8.08 us
    unnamed x20, local copies, waits for them, and re-layouts  4.45 us
    all_to_all x1, starting transfers between devices, per_device(): lax.all_to_all(outgoing, 'expert', split_axis=0, concat_axis=0, tiled=True)  3.77 us
  transfers between devices with their start and end apart: 26, of which 11 were waited for; matrix products, arithmetic and copies ran while one was open for 2% of the time, Pallas kernels for 23%

profile of v4, /device:TPU:0, one launch (start us, length us, event | category | flops | bytes accessed | tf_op | source)
XLA Modules:
  0.0 133.8 jit_solution(5715564996564869941)
XLA Ops:
  0.6 0.0 copy-start.6
  0.7 1.0 copy-done.3
  1.7 0.7 copy-done.7
  2.4 0.9 prepare.1
  3.3 3.1 %collective-permute-start.2 = (bf16[56,4224]{1,0:T(8,128)(2,1)S(1)}, bf16[56,4224]{1,0:T(8,128)(2,1)S(1)}, u32[]{:S(2)}, u32[]{:S(2)}) collective-permute-start(bf16[56,4224]{1,0:T(8,128)(2,1)S(1)} %get-tuple-element.29.refs_0_.refs_5_), channel_id=1, source_target_pairs={{0,8},{1,9},{2,10},{3,11},{4,12},{5,13},{6,14},{7,15},{8,0},{9,1},... | collective-permute-start | bytes 1419272 | tf_op jit(solution)/shard_map/ppermute | solution.py:339
  6.4 0.7 add_convert_fusion
  7.1 0.1 broadcast_in_dim.27.refs_11_
  7.2 0.7 collective-permute-start
  7.9 1.6 %collective-permute-start.3 = (bf16[56,4224]{1,0:T(8,128)(2,1)S(1)}, bf16[56,4224]{1,0:T(8,128)(2,1)S(1)}, u32[]{:S(2)}, u32[]{:S(2)}) collective-permute-start(bf16[56,4224]{1,0:T(8,128)(2,1)S(1)} %get-tuple-element.29.refs_0_.refs_5_), channel_id=1, source_target_pairs={{0,2},{1,3},{2,0},{3,1},{4,6},{5,7},{6,4},{7,5},{8,10},{9,11},{10,... | collective-permute-start | bytes 1419272 | tf_op jit(solution)/shard_map/ppermute | solution.py:339
  9.4 1.5 %collective-permute-start.4 = (bf16[56,4224]{1,0:T(8,128)(2,1)S(1)}, bf16[56,4224]{1,0:T(8,128)(2,1)S(1)}, u32[]{:S(2)}, u32[]{:S(2)}) collective-permute-start(bf16[56,4224]{1,0:T(8,128)(2,1)S(1)} %get-tuple-element.29.refs_0_.refs_5_), channel_id=1, source_target_pairs={{0,4},{1,5},{2,6},{3,7},{4,0},{5,1},{6,2},{7,3},{8,12},{9,13},{10,... | collective-permute-start | bytes 1419272 | tf_op jit(solution)/shard_map/ppermute | solution.py:339
  11.0 6.3 %collective-permute-done.2.refs_0_.refs_5_ = bf16[56,4224]{1,0:T(8,128)(2,1)S(1)} collective-permute-done((bf16[56,4224]{1,0:T(8,128)(2,1)S(1)}, bf16[56,4224]{1,0:T(8,128)(2,1)S(1)}, u32[]{:S(2)}, u32[]{:S(2)}) %collective-permute-start.2) | collective-permute-done | bytes 473120 | tf_op jit(solution)/shard_map/ppermute | solution.py:339
  17.2 1.4 %collective-permute-start.12 = (bf16[56,4224]{1,0:T(8,128)(2,1)S(1)}, bf16[56,4224]{1,0:T(8,128)(2,1)}, u32[]{:S(2)}, u32[]{:S(2)}) collective-permute-start(bf16[56,4224]{1,0:T(8,128)(2,1)S(1)} %collective-permute-done.2.refs_0_.refs_5_), channel_id=1, source_target_pairs={{8,16},{9,17},{10,18},{11,19},{12,20},{13,21},{14,22},{15,23},{16,... | collective-permute-start | bytes 1419272 | tf_op jit(solution)/shard_map/ppermute | solution.py:339
  18.7 1.3 collective-permute-start.1
  19.9 0.3 collective-permute-done.3.refs_1_.refs_6_
  20.2 0.7 slice.37
  21.0 1.5 %collective-permute-start.14 = (bf16[32,4224]{1,0:T(8,128)(2,1)}, bf16[32,4224]{1,0:T(8,128)(2,1)S(1)}, u32[]{:S(2)}, u32[]{:S(2)}) collective-permute-start(bf16[32,4224]{1,0:T(8,128)(2,1)} %slice.37), channel_id=1, source_target_pairs={{0,4},{1,5},{2,6},{3,7},{4,0},{5,1},{6,2},{7,3},{8,12},{9,13},{10,... | collective-permute-start | bytes 811016 | tf_op jit(solution)/shard_map/ppermute | solution.py:339
  22.5 1.6 %collective-permute-start.16 = (bf16[24,4224]{1,0:T(8,128)(2,1)S(1)}, bf16[24,4224]{1,0:T(8,128)(2,1)S(1)}, u32[]{:S(2)}, u32[]{:S(2)}) collective-permute-start(bf16[24,4224]{1,0:T(8,128)(2,1)S(1)} %slice.38), channel_id=1, source_target_pairs={{0,2},{1,3},{2,0},{3,1},{4,6},{5,7},{6,4},{7,5},{8,10},{9,11},{10,... | collective-permute-start | bytes 608264 | tf_op jit(solution)/shard_map/ppermute | solution.py:339
  24.1 0.7 xor_add_fusion
  24.8 0.6 collective-permute-start.5
  25.4 5.1 %collective-permute-done.16.refs_4_.refs_9_ = bf16[24,4224]{1,0:T(8,128)(2,1)S(1)} collective-permute-done((bf16[24,4224]{1,0:T(8,128)(2,1)S(1)}, bf16[24,4224]{1,0:T(8,128)(2,1)S(1)}, u32[]{:S(2)}, u32[]{:S(2)}) %collective-permute-start.16) | collective-permute-done | bytes 202784 | tf_op jit(solution)/shard_map/ppermute | solution.py:339
  30.5 0.5 collective-permute-start.6
  31.1 4.2 %collective-permute-start.17 = (bf16[24,4224]{1,0:T(8,128)(2,1)S(1)}, bf16[24,4224]{1,0:T(8,128)(2,1)S(1)}, u32[]{:S(2)}, u32[]{:S(2)}) collective-permute-start(bf16[24,4224]{1,0:T(8,128)(2,1)S(1)} %collective-permute-done.16.refs_4_.refs_9_), channel_id=1, source_target_pairs={{0,8},{1,9},{2,10},{3,11},{4,12},{5,13},{6,14},{7,15},{8,0},{9,1},... | collective-permute-start | bytes 608264 | tf_op jit(solution)/shard_map/ppermute | solution.py:339
  35.3 0.1 collective-permute-start.15
  35.4 0.8 collective-permute-done.1
  36.1 1.3 collective-permute-start.13
  37.4 0.1 broadcast_select_fusion.1.refs_0_.refs_5_
  37.5 0.7 collective-permute-done.5.refs_1_.refs_6_
  38.2 1.0 collective-permute-done.6.refs_2_.refs_7_
  39.2 1.9 %collective-permute-start.7 = (bf16[56,4224]{1,0:T(8,128)(2,1)S(1)}, bf16[56,4224]{1,0:T(8,128)(2,1)S(1)}, u32[]{:S(2)}, u32[]{:S(2)}) collective-permute-start(bf16[56,4224]{1,0:T(8,128)(2,1)S(1)} %broadcast_select_fusion.1.refs_0_.refs_5_), channel_id=1, source_target_pairs={{0,2},{1,3},{2,0},{3,1},{4,6},{5,7},{6,4},{7,5},{8,10},{9,11},{10,... | collective-permute-start | bytes 1419272 | tf_op jit(solution)/shard_map/ppermute | solution.py:339
  41.1 0.9 collective-permute-start.8
  42.0 1.8 %pick.5 = (bf16[96,4096]{1,0:T(8,128)(2,1)S(1)}, bf16[96,4096]{1,0:T(8,128)(2,1)S(1)}) custom-call(bf16[56,4224]{1,0:T(8,128)(2,1)S(1)} %get-tuple-element.29.refs_0_.refs_5_, bf16[56,4224]{1,0:T(8,128)(2,1)S(1)} %collective-permute-done.3.refs_1_.refs_6_, bf16[56,4224]{1,0:T(8,128)(2,1)S(1)} %collective-permute-done.4.refs_2_.refs_7_, ...), custom_call_target="tpu_custom_call" | custom-call | tf_op jit(solution)/shard_map/pick/pallas_call | solution.py:183
  43.9 0.1 collective-permute-start.20
  44.0 3.1 %collective-permute-done.15.refs_3_.refs_8_ = bf16[32,4224]{1,0:T(8,128)(2,1)S(1)} collective-permute-done((bf16[32,4224]{1,0:T(8,128)(2,1)S(1)}, bf16[32,4224]{1,0:T(8,128)(2,1)S(1)}, u32[]{:S(2)}, u32[]{:S(2)}) %collective-permute-start.15) | collective-permute-done | bytes 270368 | tf_op jit(solution)/shard_map/ppermute | solution.py:339
  47.0 1.8 %pick.6 = (bf16[96,4096]{1,0:T(8,128)(2,1)S(1)}, bf16[96,4096]{1,0:T(8,128)(2,1)S(1)}) custom-call(bf16[56,4224]{1,0:T(8,128)(2,1)S(1)} %collective-permute-done.2.refs_0_.refs_5_, bf16[56,4224]{1,0:T(8,128)(2,1)S(1)} %collective-permute-done.5.refs_1_.refs_6_, bf16[56,4224]{1,0:T(8,128)(2,1)S(1)} %collective-permute-done.6.refs_2_.refs_7_, ...), custom_call_target="tpu_custom_call" | custom-call | tf_op jit(solution)/shard_map/pick/pallas_call | solution.py:183
  48.9 0.1 collective-permute-start.21
  48.9 5.3 %collective-permute-done.13 = bf16[56,4224]{1,0:T(8,128)(2,1)S(1)} collective-permute-done((bf16[56,4224]{1,0:T(8,128)(2,1)}, bf16[56,4224]{1,0:T(8,128)(2,1)S(1)}, u32[]{:S(2)}, u32[]{:S(2)}) %collective-permute-start.13) | collective-permute-done | bytes 473120 | tf_op jit(solution)/shard_map/ppermute | solution.py:339
  54.3 0.1 broadcast_select_fusion.refs_0_.refs_5_
  54.4 1.6 %collective-permute-start.18 = (bf16[56,4224]{1,0:T(8,128)(2,1)S(1)}, bf16[56,4224]{1,0:T(8,128)(2,1)S(1)}, u32[]{:S(2)}, u32[]{:S(2)}) collective-permute-start(bf16[56,4224]{1,0:T(8,128)(2,1)S(1)} %broadcast_select_fusion.refs_0_.refs_5_), channel_id=1, source_target_pairs={{0,2},{1,3},{2,0},{3,1},{4,6},{5,7},{6,4},{7,5},{8,10},{9,11},{10,... | collective-permute-start | bytes 1419272 | tf_op jit(solution)/shard_map/ppermute | solution.py:339
  56.0 1.5 %collective-permute-start.19 = (bf16[56,4224]{1,0:T(8,128)(2,1)S(1)}, bf16[56,4224]{1,0:T(8,128)(2,1)S(1)}, u32[]{:S(2)}, u32[]{:S(2)}) collective-permute-start(bf16[56,4224]{1,0:T(8,128)(2,1)S(1)} %broadcast_select_fusion.refs_0_.refs_5_), channel_id=1, source_target_pairs={{0,4},{1,5},{2,6},{3,7},{4,0},{5,1},{6,2},{7,3},{8,12},{9,13},{10,... | collective-permute-start | bytes 1419272 | tf_op jit(solution)/shard_map/ppermute | solution.py:339
  57.5 0.5 collective-permute-start.9
  58.0 0.5 collective-permute-start.10
  58.6 0.1 and_select_fusion
  58.6 13.5 %experts.2.refs_4_ = bf16[16,24,768]{2,1,0:T(8,128)(2,1)S(1)} custom-call(s32[16]{0:T(128)S(1)} %get-tuple-element.40.owners_ref, bf16[96,4096]{1,0:T(8,128)(2,1)S(1)} %get-tuple-element.30.refs_0_, bf16[96,4096]{1,0:T(8,128)(2,1)S(1)} %collective-permute-done.20.refs_1_, bf16[96,4096]{1,0:T(8,128)(2,1)S(1)} %get-tuple-element.33.refs_2_, ...), custom_call_target="tpu_custom_call" | custom-call | tf_op jit(solution)/shard_map/experts/pallas_call | solution.py:253
  72.2 1.6 %collective-permute-start.22 = (bf16[32,4224]{1,0:T(8,128)(2,1)S(1)}, bf16[32,4224]{1,0:T(8,128)(2,1)S(1)}, u32[]{:S(2)}, u32[]{:S(2)}) collective-permute-start(bf16[32,4224]{1,0:T(8,128)(2,1)S(1)} %slice.41), channel_id=1, source_target_pairs={{0,4},{1,5},{2,6},{3,7},{4,0},{5,1},{6,2},{7,3},{8,12},{9,13},{10,... | collective-permute-start | bytes 811016 | tf_op jit(solution)/shard_map/ppermute | solution.py:339
  73.8 1.5 %collective-permute-start.23 = (bf16[24,4224]{1,0:T(8,128)(2,1)S(1)}, bf16[24,4224]{1,0:T(8,128)(2,1)S(1)}, u32[]{:S(2)}, u32[]{:S(2)}) collective-permute-start(bf16[24,4224]{1,0:T(8,128)(2,1)S(1)} %slice.42), channel_id=1, source_target_pairs={{0,2},{1,3},{2,0},{3,1},{4,6},{5,7},{6,4},{7,5},{8,10},{9,11},{10,... | collective-permute-start | bytes 608264 | tf_op jit(solution)/shard_map/ppermute | solution.py:339
  75.3 2.5 %pick.4 = (bf16[96,4096]{1,0:T(8,128)(2,1)S(1)}, bf16[96,4096]{1,0:T(8,128)(2,1)}) custom-call(bf16[56,4224]{1,0:T(8,128)(2,1)S(1)} %broadcast_select_fusion.1.refs_0_.refs_5_, bf16[56,4224]{1,0:T(8,128)(2,1)S(1)} %collective-permute-done.7.refs_1_.refs_6_, bf16[56,4224]{1,0:T(8,128)(2,1)S(1)} %collective-permute-done.8.refs_2_.refs_7_, ...), custom_call_target="tpu_custom_call" | custom-call | tf_op jit(solution)/shard_map/pick/pallas_call | solution.py:183
  77.8 1.7 %collective-permute-done.23.refs_4_.refs_9_ = bf16[24,4224]{1,0:T(8,128)(2,1)S(1)} collective-permute-done((bf16[24,4224]{1,0:T(8,128)(2,1)S(1)}, bf16[24,4224]{1,0:T(8,128)(2,1)S(1)}, u32[]{:S(2)}, u32[]{:S(2)}) %collective-permute-start.23) | collective-permute-done | bytes 202784 | tf_op jit(solution)/shard_map/ppermute | solution.py:339
  79.5 2.6 %pick.7 = (bf16[96,4096]{1,0:T(8,128)(2,1)S(1)}, bf16[96,4096]{1,0:T(8,128)(2,1)}) custom-call(bf16[56,4224]{1,0:T(8,128)(2,1)S(1)} %broadcast_select_fusion.refs_0_.refs_5_, bf16[56,4224]{1,0:T(8,128)(2,1)S(1)} %collective-permute-done.18.refs_1_.refs_6_, bf16[56,4224]{1,0:T(8,128)(2,1)S(1)} %collective-permute-done.19.refs_2_.refs_7_, ...), custom_call_target="tpu_custom_call" | custom-call | tf_op jit(solution)/shard_map/pick/pallas_call | solution.py:183
  82.1 0.1 pad_add_fusion.owners_ref
  82.1 2.5 %collective-permute-done.24.refs_3_ = bf16[96,4096]{1,0:T(8,128)(2,1)} collective-permute-done((bf16[96,4096]{1,0:T(8,128)(2,1)}, bf16[96,4096]{1,0:T(8,128)(2,1)}, u32[]{:S(2)}, u32[]{:S(2)}) %collective-permute-start.24) | collective-permute-done | bytes 786464 | tf_op jit(solution)/shard_map/ppermute | solution.py:339
  84.7 14.5 %experts.3 = bf16[32,24,768]{2,1,0:T(8,128)(2,1)} custom-call(s32[17]{0:T(128)S(1)} %pad_add_fusion.owners_ref, bf16[96,4096]{1,0:T(8,128)(2,1)S(1)} %get-tuple-element.27.refs_0_, bf16[96,4096]{1,0:T(8,128)(2,1)S(1)} %collective-permute-done.11.refs_1_, bf16[96,4096]{1,0:T(8,128)(2,1)S(1)} %get-tuple-element.37.refs_2_, ...), custom_call_target="tpu_custom_call" | custom-call | tf_op jit(solution)/shard_map/experts/pallas_call | solution.py:253
  99.2 0.0 copy-start.9
  99.2 0.0 copy-start
  99.2 0.0 copy-start.4
  99.3 0.0 copy-start.5
  99.3 0.0 copy-start.8
  99.3 3.8 %all-to-all-start = ((bf16[32,24,768]{2,1,0:T(8,128)(2,1)}), bf16[32,24,768]{2,1,0:T(8,128)(2,1)S(1)}, u32[]{:S(2)}, u32[]{:S(2)}) async-start(bf16[32,24,768]{2,1,0:T(8,128)(2,1)} %experts.3), calls=%async_computation | async-start | bytes 2359296 | tf_op jit(solution)/shard_map/all_to_all | solution.py:430
  103.1 0.1 copy.23
  103.2 0.0 copy-start.1
  103.2 1.5 %copy-done.1 = bf16[14,128,512]{2,1,0:T(8,128)(2,1)S(1)} copy-done((bf16[14,128,512]{2,1,0:T(8,128)(2,1)S(1)}, bf16[14,128,512]{2,1,0:T(8,128)(2,1)}, u32[]{:S(2)}) %copy-start.1) | copy-done | bytes 1835032
  104.7 1.2 copy-done.2
  105.9 8.1 %attention.1 = bf16[14,4,8192]{2,1,0:T(4,128)(2,1)} custom-call(s32[14]{0:T(128)S(1)} %copy-done.8, bf16[14,4,8192]{2,1,0:T(4,128)(2,1)S(1)} %bitcast.12, bf16[14,4,512]{2,1,0:T(4,128)(2,1)S(1)} %bitcast.15, bf16[14,4,512]{2,1,0:T(4,128)(2,1)S(1)} %bitcast.16, bf16[14,128,512]{2,1,0:T(8,128)(2,1)S(1)} %copy-done, bf16[14,128,512]{2,1,0:T(8,128)(2,1)S(1)} %copy-done.1), custom_call_target="tpu_custom_call" | custom-call | tf_op jit(solution)/shard_map/attention/pallas_call | solution.py:64
  114.0 18.2 %all-to-all-done = bf16[32,24,768]{2,1,0:T(8,128)(2,1)S(1)} async-done(((bf16[32,24,768]{2,1,0:T(8,128)(2,1)}), bf16[32,24,768]{2,1,0:T(8,128)(2,1)S(1)}, u32[]{:S(2)}, u32[]{:S(2)}) %all-to-all-start) | async-done | bytes 1179680 | tf_op jit(solution)/shard_map/all_to_all | solution.py:430
  132.1 1.6 %combine.1 = bf16[14,4,6144]{2,1,0:T(4,128)(2,1)} custom-call(bf16[768,768]{1,0:T(8,128)(2,1)S(1)} %bitcast.11, s32[56,128]{1,0:T(8,128)S(1)} %get-tuple-element.21.columns_ref, f32[56,8]{1,0:T(8,128)S(1)} %bitcast.14), custom_call_target="tpu_custom_call" | custom-call | tf_op jit(solution)/shard_map/combine/pallas_call | solution.py:302
  (31 shorter events, 0.2 us)
Async XLA Ops:
  0.6 41.4 %copy-start.6 = (f32[1,224]{1,0:T(1,128)S(1)}, f32[1,224]{1,0:T(1,128)}, u32[]{:S(2)}) copy-start(f32[1,224]{1,0:T(1,128)} %constant.132.refs_10_) | copy-start | bytes 2692
  0.6 1.0 copy-start.3
  1.7 0.7 copy-start.7
  3.3 13.9 %collective-permute-start.2 = (bf16[56,4224]{1,0:T(8,128)(2,1)S(1)}, bf16[56,4224]{1,0:T(8,128)(2,1)S(1)}, u32[]{:S(2)}, u32[]{:S(2)}) collective-permute-start(bf16[56,4224]{1,0:T(8,128)(2,1)S(1)} %get-tuple-element.29.refs_0_.refs_5_), channel_id=1, source_target_pairs={{0,8},{1,9},{2,10},{3,11},{4,12},{5,13},{6,14},{7,15},{8,0},{9,1},... | collective-permute-start | bytes 1419272 | tf_op jit(solution)/shard_map/ppermute | solution.py:339
  7.2 11.5 %collective-permute-start = (bf16[56,4224]{1,0:T(8,128)(2,1)S(1)}, bf16[56,4224]{1,0:T(8,128)(2,1)S(1)}, u32[]{:S(2)}, u32[]{:S(2)}) collective-permute-start(bf16[56,4224]{1,0:T(8,128)(2,1)S(1)} %get-tuple-element.29.refs_0_.refs_5_), channel_id=1, source_target_pairs={{8,16},{9,17},{10,18},{11,19},{12,20},{13,21},{14,22},{15,23},{16,... | collective-permute-start | bytes 1419272 | tf_op jit(solution)/shard_map/ppermute | solution.py:339
  7.9 12.4 %collective-permute-start.3 = (bf16[56,4224]{1,0:T(8,128)(2,1)S(1)}, bf16[56,4224]{1,0:T(8,128)(2,1)S(1)}, u32[]{:S(2)}, u32[]{:S(2)}) collective-permute-start(bf16[56,4224]{1,0:T(8,128)(2,1)S(1)} %get-tuple-element.29.refs_0_.refs_5_), channel_id=1, source_target_pairs={{0,2},{1,3},{2,0},{3,1},{4,6},{5,7},{6,4},{7,5},{8,10},{9,11},{10,... | collective-permute-start | bytes 1419272 | tf_op jit(solution)/shard_map/ppermute | solution.py:339
  9.4 13.0 %collective-permute-start.4 = (bf16[56,4224]{1,0:T(8,128)(2,1)S(1)}, bf16[56,4224]{1,0:T(8,128)(2,1)S(1)}, u32[]{:S(2)}, u32[]{:S(2)}) collective-permute-start(bf16[56,4224]{1,0:T(8,128)(2,1)S(1)} %get-tuple-element.29.refs_0_.refs_5_), channel_id=1, source_target_pairs={{0,4},{1,5},{2,6},{3,7},{4,0},{5,1},{6,2},{7,3},{8,12},{9,13},{10,... | collective-permute-start | bytes 1419272 | tf_op jit(solution)/shard_map/ppermute | solution.py:339
  17.2 18.1 %collective-permute-start.12 = (bf16[56,4224]{1,0:T(8,128)(2,1)S(1)}, bf16[56,4224]{1,0:T(8,128)(2,1)}, u32[]{:S(2)}, u32[]{:S(2)}) collective-permute-start(bf16[56,4224]{1,0:T(8,128)(2,1)S(1)} %collective-permute-done.2.refs_0_.refs_5_), channel_id=1, source_target_pairs={{8,16},{9,17},{10,18},{11,19},{12,20},{13,21},{14,22},{15,23},{16,... | collective-permute-start | bytes 1419272 | tf_op jit(solution)/shard_map/ppermute | solution.py:339
  18.7 17.5 %collective-permute-start.1 = (bf16[56,4224]{1,0:T(8,128)(2,1)S(1)}, bf16[56,4224]{1,0:T(8,128)(2,1)S(1)}, u32[]{:S(2)}, u32[]{:S(2)}) collective-permute-start(bf16[56,4224]{1,0:T(8,128)(2,1)S(1)} %collective-permute-done), channel_id=1, source_target_pairs={{8,0},{9,1},{10,2},{11,3},{12,4},{13,5},{14,6},{15,7},{16,24},{17,... | collective-permute-start | bytes 1419272 | tf_op jit(solution)/shard_map/ppermute | solution.py:339
  21.0 10.1 %collective-permute-start.14 = (bf16[32,4224]{1,0:T(8,128)(2,1)}, bf16[32,4224]{1,0:T(8,128)(2,1)S(1)}, u32[]{:S(2)}, u32[]{:S(2)}) collective-permute-start(bf16[32,4224]{1,0:T(8,128)(2,1)} %slice.37), channel_id=1, source_target_pairs={{0,4},{1,5},{2,6},{3,7},{4,0},{5,1},{6,2},{7,3},{8,12},{9,13},{10,... | collective-permute-start | bytes 811016 | tf_op jit(solution)/shard_map/ppermute | solution.py:339
  22.5 8.0 %collective-permute-start.16 = (bf16[24,4224]{1,0:T(8,128)(2,1)S(1)}, bf16[24,4224]{1,0:T(8,128)(2,1)S(1)}, u32[]{:S(2)}, u32[]{:S(2)}) collective-permute-start(bf16[24,4224]{1,0:T(8,128)(2,1)S(1)} %slice.38), channel_id=1, source_target_pairs={{0,2},{1,3},{2,0},{3,1},{4,6},{5,7},{6,4},{7,5},{8,10},{9,11},{10,... | collective-permute-start | bytes 608264 | tf_op jit(solution)/shard_map/ppermute | solution.py:339
  24.8 13.4 %collective-permute-start.5 = (bf16[56,4224]{1,0:T(8,128)(2,1)S(1)}, bf16[56,4224]{1,0:T(8,128)(2,1)S(1)}, u32[]{:S(2)}, u32[]{:S(2)}) collective-permute-start(bf16[56,4224]{1,0:T(8,128)(2,1)S(1)} %collective-permute-done.2.refs_0_.refs_5_), channel_id=1, source_target_pairs={{0,2},{1,3},{2,0},{3,1},{4,6},{5,7},{6,4},{7,5},{8,10},{9,11},{10,... | collective-permute-start | bytes 1419272 | tf_op jit(solution)/shard_map/ppermute | solution.py:339
  30.5 8.6 %collective-permute-start.6 = (bf16[56,4224]{1,0:T(8,128)(2,1)S(1)}, bf16[56,4224]{1,0:T(8,128)(2,1)S(1)}, u32[]{:S(2)}, u32[]{:S(2)}) collective-permute-start(bf16[56,4224]{1,0:T(8,128)(2,1)S(1)} %collective-permute-done.2.refs_0_.refs_5_), channel_id=1, source_target_pairs={{0,4},{1,5},{2,6},{3,7},{4,0},{5,1},{6,2},{7,3},{8,12},{9,13},{10,... | collective-permute-start | bytes 1419272 | tf_op jit(solution)/shard_map/ppermute | solution.py:339
  31.1 12.8 %collective-permute-start.17 = (bf16[24,4224]{1,0:T(8,128)(2,1)S(1)}, bf16[24,4224]{1,0:T(8,128)(2,1)S(1)}, u32[]{:S(2)}, u32[]{:S(2)}) collective-permute-start(bf16[24,4224]{1,0:T(8,128)(2,1)S(1)} %collective-permute-done.16.refs_4_.refs_9_), channel_id=1, source_target_pairs={{0,8},{1,9},{2,10},{3,11},{4,12},{5,13},{6,14},{7,15},{8,0},{9,1},... | collective-permute-start | bytes 608264 | tf_op jit(solution)/shard_map/ppermute | solution.py:339
  35.3 11.7 %collective-permute-start.15 = (bf16[32,4224]{1,0:T(8,128)(2,1)S(1)}, bf16[32,4224]{1,0:T(8,128)(2,1)S(1)}, u32[]{:S(2)}, u32[]{:S(2)}) collective-permute-start(bf16[32,4224]{1,0:T(8,128)(2,1)S(1)} %collective-permute-done.14.refs_3_.refs_8_), channel_id=1, source_target_pairs={{0,8},{1,9},{2,10},{3,11},{4,12},{5,13},{6,14},{7,15},{8,0},{9,1},... | collective-permute-start | bytes 811016 | tf_op jit(solution)/shard_map/ppermute | solution.py:339
  36.1 18.2 %collective-permute-start.13 = (bf16[56,4224]{1,0:T(8,128)(2,1)}, bf16[56,4224]{1,0:T(8,128)(2,1)S(1)}, u32[]{:S(2)}, u32[]{:S(2)}) collective-permute-start(bf16[56,4224]{1,0:T(8,128)(2,1)} %collective-permute-done.12), channel_id=1, source_target_pairs={{8,0},{9,1},{10,2},{11,3},{12,4},{13,5},{14,6},{15,7},{16,24},{17,... | collective-permute-start | bytes 1419272 | tf_op jit(solution)/shard_map/ppermute | solution.py:339
  39.2 15.2 %collective-permute-start.7 = (bf16[56,4224]{1,0:T(8,128)(2,1)S(1)}, bf16[56,4224]{1,0:T(8,128)(2,1)S(1)}, u32[]{:S(2)}, u32[]{:S(2)}) collective-permute-start(bf16[56,4224]{1,0:T(8,128)(2,1)S(1)} %broadcast_select_fusion.1.refs_0_.refs_5_), channel_id=1, source_target_pairs={{0,2},{1,3},{2,0},{3,1},{4,6},{5,7},{6,4},{7,5},{8,10},{9,11},{10,... | collective-permute-start | bytes 1419272 | tf_op jit(solution)/shard_map/ppermute | solution.py:339
  41.1 13.3 %collective-permute-start.8 = (bf16[56,4224]{1,0:T(8,128)(2,1)S(1)}, bf16[56,4224]{1,0:T(8,128)(2,1)S(1)}, u32[]{:S(2)}, u32[]{:S(2)}) collective-permute-start(bf16[56,4224]{1,0:T(8,128)(2,1)S(1)} %broadcast_select_fusion.1.refs_0_.refs_5_), channel_id=1, source_target_pairs={{0,4},{1,5},{2,6},{3,7},{4,0},{5,1},{6,2},{7,3},{8,12},{9,13},{10,... | collective-permute-start | bytes 1419272 | tf_op jit(solution)/shard_map/ppermute | solution.py:339
  43.9 14.1 %collective-permute-start.20 = (bf16[96,4096]{1,0:T(8,128)(2,1)S(1)}, bf16[96,4096]{1,0:T(8,128)(2,1)S(1)}, u32[]{:S(2)}, u32[]{:S(2)}) collective-permute-start(bf16[96,4096]{1,0:T(8,128)(2,1)S(1)} %get-tuple-element.32), channel_id=1, source_target_pairs={{0,1},{1,0},{2,3},{3,2},{4,5},{5,4},{6,7},{7,6},{8,9},{9,8},{10,11... | collective-permute-start | bytes 2359304 | tf_op jit(solution)/shard_map/ppermute | solution.py:339
  48.9 9.8 %collective-permute-start.21 = (bf16[96,4096]{1,0:T(8,128)(2,1)S(1)}, bf16[96,4096]{1,0:T(8,128)(2,1)S(1)}, u32[]{:S(2)}, u32[]{:S(2)}) collective-permute-start(bf16[96,4096]{1,0:T(8,128)(2,1)S(1)} %get-tuple-element.34), channel_id=1, source_target_pairs={{0,1},{1,0},{2,3},{3,2},{4,5},{5,4},{6,7},{7,6},{8,9},{9,8},{10,11... | collective-permute-start | bytes 2359304 | tf_op jit(solution)/shard_map/ppermute | solution.py:339
  54.4 17.7 %collective-permute-start.18 = (bf16[56,4224]{1,0:T(8,128)(2,1)S(1)}, bf16[56,4224]{1,0:T(8,128)(2,1)S(1)}, u32[]{:S(2)}, u32[]{:S(2)}) collective-permute-start(bf16[56,4224]{1,0:T(8,128)(2,1)S(1)} %broadcast_select_fusion.refs_0_.refs_5_), channel_id=1, source_target_pairs={{0,2},{1,3},{2,0},{3,1},{4,6},{5,7},{6,4},{7,5},{8,10},{9,11},{10,... | collective-permute-start | bytes 1419272 | tf_op jit(solution)/shard_map/ppermute | solution.py:339
  56.0 16.1 %collective-permute-start.19 = (bf16[56,4224]{1,0:T(8,128)(2,1)S(1)}, bf16[56,4224]{1,0:T(8,128)(2,1)S(1)}, u32[]{:S(2)}, u32[]{:S(2)}) collective-permute-start(bf16[56,4224]{1,0:T(8,128)(2,1)S(1)} %broadcast_select_fusion.refs_0_.refs_5_), channel_id=1, source_target_pairs={{0,4},{1,5},{2,6},{3,7},{4,0},{5,1},{6,2},{7,3},{8,12},{9,13},{10,... | collective-permute-start | bytes 1419272 | tf_op jit(solution)/shard_map/ppermute | solution.py:339
  57.5 14.7 %collective-permute-start.9 = (bf16[32,4224]{1,0:T(8,128)(2,1)S(1)}, bf16[32,4224]{1,0:T(8,128)(2,1)S(1)}, u32[]{:S(2)}, u32[]{:S(2)}) collective-permute-start(bf16[32,4224]{1,0:T(8,128)(2,1)S(1)} %slice.39), channel_id=1, source_target_pairs={{0,4},{1,5},{2,6},{3,7},{4,0},{5,1},{6,2},{7,3},{8,12},{9,13},{10,... | collective-permute-start | bytes 811016 | tf_op jit(solution)/shard_map/ppermute | solution.py:339
  58.0 14.2 %collective-permute-start.10 = (bf16[24,4224]{1,0:T(8,128)(2,1)S(1)}, bf16[24,4224]{1,0:T(8,128)(2,1)S(1)}, u32[]{:S(2)}, u32[]{:S(2)}) collective-permute-start(bf16[24,4224]{1,0:T(8,128)(2,1)S(1)} %slice.40), channel_id=1, source_target_pairs={{0,2},{1,3},{2,0},{3,1},{4,6},{5,7},{6,4},{7,5},{8,10},{9,11},{10,... | collective-permute-start | bytes 608264 | tf_op jit(solution)/shard_map/ppermute | solution.py:339
  72.2 7.3 %collective-permute-start.22 = (bf16[32,4224]{1,0:T(8,128)(2,1)S(1)}, bf16[32,4224]{1,0:T(8,128)(2,1)S(1)}, u32[]{:S(2)}, u32[]{:S(2)}) collective-permute-start(bf16[32,4224]{1,0:T(8,128)(2,1)S(1)} %slice.41), channel_id=1, source_target_pairs={{0,4},{1,5},{2,6},{3,7},{4,0},{5,1},{6,2},{7,3},{8,12},{9,13},{10,... | collective-permute-start | bytes 811016 | tf_op jit(solution)/shard_map/ppermute | solution.py:339
  73.8 5.7 %collective-permute-start.23 = (bf16[24,4224]{1,0:T(8,128)(2,1)S(1)}, bf16[24,4224]{1,0:T(8,128)(2,1)S(1)}, u32[]{:S(2)}, u32[]{:S(2)}) collective-permute-start(bf16[24,4224]{1,0:T(8,128)(2,1)S(1)} %slice.42), channel_id=1, source_target_pairs={{0,2},{1,3},{2,0},{3,1},{4,6},{5,7},{6,4},{7,5},{8,10},{9,11},{10,... | collective-permute-start | bytes 608264 | tf_op jit(solution)/shard_map/ppermute | solution.py:339
  77.8 4.4 %collective-permute-start.11 = (bf16[96,4096]{1,0:T(8,128)(2,1)}, bf16[96,4096]{1,0:T(8,128)(2,1)S(1)}, u32[]{:S(2)}, u32[]{:S(2)}) collective-permute-start(bf16[96,4096]{1,0:T(8,128)(2,1)} %get-tuple-element.28), channel_id=1, source_target_pairs={{0,1},{1,0},{2,3},{3,2},{4,5},{5,4},{6,7},{7,6},{8,9},{9,8},{10,11... | collective-permute-start | bytes 2359304 | tf_op jit(solution)/shard_map/ppermute | solution.py:339
  82.1 2.6 %collective-permute-start.24 = (bf16[96,4096]{1,0:T(8,128)(2,1)}, bf16[96,4096]{1,0:T(8,128)(2,1)}, u32[]{:S(2)}, u32[]{:S(2)}) collective-permute-start(bf16[96,4096]{1,0:T(8,128)(2,1)} %get-tuple-element.38), channel_id=1, source_target_pairs={{0,1},{1,0},{2,3},{3,2},{4,5},{5,4},{6,7},{7,6},{8,9},{9,8},{10,11... | collective-permute-start | bytes 2359304 | tf_op jit(solution)/shard_map/ppermute | solution.py:339
  99.2 3.8 %copy-start.9 = (f32[4,14,8]{1,2,0:T(8,128)S(1)}, f32[4,14,8]{1,2,0:T(8,128)}, u32[]{:S(2)}) copy-start(f32[4,14,8]{1,2,0:T(8,128)} %param.23) | copy-start | bytes 5380
  99.2 3.9 %copy-start = (bf16[14,128,512]{2,1,0:T(8,128)(2,1)S(1)}, bf16[14,128,512]{2,1,0:T(8,128)(2,1)}, u32[]{:S(2)}) copy-start(bf16[14,128,512]{2,1,0:T(8,128)(2,1)} %k_ref.1) | copy-start | bytes 5505028
  99.2 3.9 %copy-start.4 = (bf16[4,14,512]{2,0,1:T(4,128)(2,1)S(1)}, bf16[4,14,512]{2,0,1:T(4,128)(2,1)}, u32[]{:S(2)}) copy-start(bf16[4,14,512]{2,0,1:T(4,128)(2,1)} %param.27) | copy-start | bytes 172036
  99.3 3.9 %copy-start.5 = (bf16[4,14,512]{2,0,1:T(4,128)(2,1)S(1)}, bf16[4,14,512]{2,0,1:T(4,128)(2,1)}, u32[]{:S(2)}) copy-start(bf16[4,14,512]{2,0,1:T(4,128)(2,1)} %param.28) | copy-start | bytes 172036
  99.3 3.9 %copy-start.8 = (s32[14]{0:T(128)S(1)}, s32[14]{0:T(128)}, u32[]{:S(2)}) copy-start(s32[14]{0:T(128)} %lengths_ref) | copy-start | bytes 172
  99.3 32.9 %all-to-all-start = ((bf16[32,24,768]{2,1,0:T(8,128)(2,1)}), bf16[32,24,768]{2,1,0:T(8,128)(2,1)S(1)}, u32[]{:S(2)}, u32[]{:S(2)}) async-start(bf16[32,24,768]{2,1,0:T(8,128)(2,1)} %experts.3), calls=%async_computation | async-start | bytes 2359296 | tf_op jit(solution)/shard_map/all_to_all | solution.py:430
  103.2 1.5 %copy-start.1 = (bf16[14,128,512]{2,1,0:T(8,128)(2,1)S(1)}, bf16[14,128,512]{2,1,0:T(8,128)(2,1)}, u32[]{:S(2)}) copy-start(bf16[14,128,512]{2,1,0:T(8,128)(2,1)} %v_ref.1) | copy-start | bytes 5505028
  104.7 1.2 copy-start.2

commit v5 on v4

--- a/solution.py
+++ b/solution.py
@@ -173,7 +173,7 @@
 
 def pick(sources, group, wanted, width):
     rows, slots = group.shape[1], wanted.shape[0]
-    cuts = 2 if width % (2 * LANES) == 0 else 1
+    cuts = 4 if width % (4 * LANES) == 0 else 1
     block = width // cuts
     sources = [source if isinstance(source, tuple) else (source, 0, 1) for source in sources]
     arrays = [source[0] for source in sources]

time: 134 us -> 135 us (level)
  Pallas kernels: 47.4 us -> 50.1 us
  waiting for transfers between devices: 45 us -> 43 us
    pallas_call x4, Pallas kernels: 8.76 us -> 11.5 us  [pick(): pl.pallas_call(functools.partial(pick_kernel, parts=len(sources)), grid=(...]
    ppermute x25, waiting for transfers between devices: 26.9 us -> 24.8 us  [per_device(): lax.ppermute(array, 'expert', moves(peers, target))]
  transfers between devices with their start and end apart: 26 -> 26, of which waited for: 11 -> 11; matrix products, arithmetic and copies ran while one was open for 2% -> 2% of each run, Pallas kernels for 23% -> 25%
where the time goes in v5:
time: 135 us; the launch traced here: 134 us
  Pallas kernels  50.1 us (37%)
  waiting for transfers between devices  43 us (32%)
  starting transfers between devices  33.3 us (25%)
  local copies, waits for them, and re-layouts  5.44 us (4%)
  other arithmetic  1.73 us (1%)
    ppermute x25, starting transfers between devices, per_device(): lax.ppermute(array, 'expert', moves(peers, target))  29.5 us
    pallas_call x2, Pallas kernels, run_experts(): pl.pallas_call(functools.partial(expert_kernel, count=count, part=part, e...  28 us
    ppermute x25, waiting for transfers between devices, per_device(): lax.ppermute(array, 'expert', moves(peers, target))  24.8 us
    all_to_all x1, waiting for transfers between devices, per_device(): lax.all_to_all(outgoing, 'expert', split_axis=0, concat_axis=0, tiled=True)  18.2 us
    pallas_call x4, Pallas kernels, pick(): pl.pallas_call(functools.partial(pick_kernel, parts=len(sources)), grid=(...  11.5 us
    pallas_call x1, Pallas kernels, attention(): pl.pallas_call(functools.partial(attention_kernel, groups=groups), grid=(...  8.08 us
    unnamed x20, local copies, waits for them, and re-layouts  4.45 us
    all_to_all x1, starting transfers between devices, per_device(): lax.all_to_all(outgoing, 'expert', split_axis=0, concat_axis=0, tiled=True)  3.77 us
  transfers between devices with their start and end apart: 26, of which 11 were waited for; matrix products, arithmetic and copies ran while one was open for 2% of the time, Pallas kernels for 25%

profile of v5, /device:TPU:0, one launch (start us, length us, event | category | flops | bytes accessed | tf_op | source)
XLA Modules:
  0.0 134.5 jit_solution(12270593307604214194)
XLA Ops:
  0.6 0.0 copy-start.6
  0.7 1.0 copy-done.3
  1.7 0.7 copy-done.7
  2.4 0.9 prepare.1
  3.3 3.1 %collective-permute-start.2 = (bf16[56,4224]{1,0:T(8,128)(2,1)S(1)}, bf16[56,4224]{1,0:T(8,128)(2,1)S(1)}, u32[]{:S(2)}, u32[]{:S(2)}) collective-permute-start(bf16[56,4224]{1,0:T(8,128)(2,1)S(1)} %get-tuple-element.29.refs_0_.refs_5_), channel_id=1, source_target_pairs={{0,8},{1,9},{2,10},{3,11},{4,12},{5,13},{6,14},{7,15},{8,0},{9,1},... | collective-permute-start | bytes 1419272 | tf_op jit(solution)/shard_map/ppermute | solution.py:339
  6.4 0.7 add_convert_fusion
  7.1 0.1 broadcast_in_dim.27.refs_11_
  7.2 0.7 collective-permute-start
  7.9 1.6 %collective-permute-start.3 = (bf16[56,4224]{1,0:T(8,128)(2,1)S(1)}, bf16[56,4224]{1,0:T(8,128)(2,1)S(1)}, u32[]{:S(2)}, u32[]{:S(2)}) collective-permute-start(bf16[56,4224]{1,0:T(8,128)(2,1)S(1)} %get-tuple-element.29.refs_0_.refs_5_), channel_id=1, source_target_pairs={{0,2},{1,3},{2,0},{3,1},{4,6},{5,7},{6,4},{7,5},{8,10},{9,11},{10,... | collective-permute-start | bytes 1419272 | tf_op jit(solution)/shard_map/ppermute | solution.py:339
  9.4 1.5 %collective-permute-start.4 = (bf16[56,4224]{1,0:T(8,128)(2,1)S(1)}, bf16[56,4224]{1,0:T(8,128)(2,1)S(1)}, u32[]{:S(2)}, u32[]{:S(2)}) collective-permute-start(bf16[56,4224]{1,0:T(8,128)(2,1)S(1)} %get-tuple-element.29.refs_0_.refs_5_), channel_id=1, source_target_pairs={{0,4},{1,5},{2,6},{3,7},{4,0},{5,1},{6,2},{7,3},{8,12},{9,13},{10,... | collective-permute-start | bytes 1419272 | tf_op jit(solution)/shard_map/ppermute | solution.py:339
  11.0 6.3 %collective-permute-done.2.refs_0_.refs_5_ = bf16[56,4224]{1,0:T(8,128)(2,1)S(1)} collective-permute-done((bf16[56,4224]{1,0:T(8,128)(2,1)S(1)}, bf16[56,4224]{1,0:T(8,128)(2,1)S(1)}, u32[]{:S(2)}, u32[]{:S(2)}) %collective-permute-start.2) | collective-permute-done | bytes 473120 | tf_op jit(solution)/shard_map/ppermute | solution.py:339
  17.2 1.4 %collective-permute-start.12 = (bf16[56,4224]{1,0:T(8,128)(2,1)S(1)}, bf16[56,4224]{1,0:T(8,128)(2,1)}, u32[]{:S(2)}, u32[]{:S(2)}) collective-permute-start(bf16[56,4224]{1,0:T(8,128)(2,1)S(1)} %collective-permute-done.2.refs_0_.refs_5_), channel_id=1, source_target_pairs={{8,16},{9,17},{10,18},{11,19},{12,20},{13,21},{14,22},{15,23},{16,... | collective-permute-start | bytes 1419272 | tf_op jit(solution)/shard_map/ppermute | solution.py:339
  18.7 1.3 collective-permute-start.1
  19.9 0.3 collective-permute-done.3.refs_1_.refs_6_
  20.2 0.7 slice.37
  21.0 1.5 %collective-permute-start.14 = (bf16[32,4224]{1,0:T(8,128)(2,1)}, bf16[32,4224]{1,0:T(8,128)(2,1)S(1)}, u32[]{:S(2)}, u32[]{:S(2)}) collective-permute-start(bf16[32,4224]{1,0:T(8,128)(2,1)} %slice.37), channel_id=1, source_target_pairs={{0,4},{1,5},{2,6},{3,7},{4,0},{5,1},{6,2},{7,3},{8,12},{9,13},{10,... | collective-permute-start | bytes 811016 | tf_op jit(solution)/shard_map/ppermute | solution.py:339
  22.5 1.6 %collective-permute-start.16 = (bf16[24,4224]{1,0:T(8,128)(2,1)S(1)}, bf16[24,4224]{1,0:T(8,128)(2,1)S(1)}, u32[]{:S(2)}, u32[]{:S(2)}) collective-permute-start(bf16[24,4224]{1,0:T(8,128)(2,1)S(1)} %slice.38), channel_id=1, source_target_pairs={{0,2},{1,3},{2,0},{3,1},{4,6},{5,7},{6,4},{7,5},{8,10},{9,11},{10,... | collective-permute-start | bytes 608264 | tf_op jit(solution)/shard_map/ppermute | solution.py:339
  24.1 0.7 xor_add_fusion
  24.8 0.6 collective-permute-start.5
  25.4 5.1 %collective-permute-done.16.refs_4_.refs_9_ = bf16[24,4224]{1,0:T(8,128)(2,1)S(1)} collective-permute-done((bf16[24,4224]{1,0:T(8,128)(2,1)S(1)}, bf16[24,4224]{1,0:T(8,128)(2,1)S(1)}, u32[]{:S(2)}, u32[]{:S(2)}) %collective-permute-start.16) | collective-permute-done | bytes 202784 | tf_op jit(solution)/shard_map/ppermute | solution.py:339
  30.5 0.5 collective-permute-start.6
  31.1 4.2 %collective-permute-start.17 = (bf16[24,4224]{1,0:T(8,128)(2,1)S(1)}, bf16[24,4224]{1,0:T(8,128)(2,1)S(1)}, u32[]{:S(2)}, u32[]{:S(2)}) collective-permute-start(bf16[24,4224]{1,0:T(8,128)(2,1)S(1)} %collective-permute-done.16.refs_4_.refs_9_), channel_id=1, source_target_pairs={{0,8},{1,9},{2,10},{3,11},{4,12},{5,13},{6,14},{7,15},{8,0},{9,1},... | collective-permute-start | bytes 608264 | tf_op jit(solution)/shard_map/ppermute | solution.py:339
  35.3 0.1 collective-permute-start.15
  35.4 0.8 collective-permute-done.1
  36.1 1.3 collective-permute-start.13
  37.4 0.1 broadcast_select_fusion.1.refs_0_.refs_5_
  37.5 0.7 collective-permute-done.5.refs_1_.refs_6_
  38.2 1.0 collective-permute-done.6.refs_2_.refs_7_
  39.2 1.9 %collective-permute-start.7 = (bf16[56,4224]{1,0:T(8,128)(2,1)S(1)}, bf16[56,4224]{1,0:T(8,128)(2,1)S(1)}, u32[]{:S(2)}, u32[]{:S(2)}) collective-permute-start(bf16[56,4224]{1,0:T(8,128)(2,1)S(1)} %broadcast_select_fusion.1.refs_0_.refs_5_), channel_id=1, source_target_pairs={{0,2},{1,3},{2,0},{3,1},{4,6},{5,7},{6,4},{7,5},{8,10},{9,11},{10,... | collective-permute-start | bytes 1419272 | tf_op jit(solution)/shard_map/ppermute | solution.py:339
  41.1 0.9 collective-permute-start.8
  42.0 2.5 %pick.5 = (bf16[96,4096]{1,0:T(8,128)(2,1)S(1)}, bf16[96,4096]{1,0:T(8,128)(2,1)S(1)}) custom-call(bf16[56,4224]{1,0:T(8,128)(2,1)S(1)} %get-tuple-element.29.refs_0_.refs_5_, bf16[56,4224]{1,0:T(8,128)(2,1)S(1)} %collective-permute-done.3.refs_1_.refs_6_, bf16[56,4224]{1,0:T(8,128)(2,1)S(1)} %collective-permute-done.4.refs_2_.refs_7_, ...), custom_call_target="tpu_custom_call" | custom-call | tf_op jit(solution)/shard_map/pick/pallas_call | solution.py:183
  44.6 0.1 collective-permute-start.20
  44.7 2.4 %collective-permute-done.15.refs_3_.refs_8_ = bf16[32,4224]{1,0:T(8,128)(2,1)S(1)} collective-permute-done((bf16[32,4224]{1,0:T(8,128)(2,1)S(1)}, bf16[32,4224]{1,0:T(8,128)(2,1)S(1)}, u32[]{:S(2)}, u32[]{:S(2)}) %collective-permute-start.15) | collective-permute-done | bytes 270368 | tf_op jit(solution)/shard_map/ppermute | solution.py:339
  47.0 2.5 %pick.6 = (bf16[96,4096]{1,0:T(8,128)(2,1)S(1)}, bf16[96,4096]{1,0:T(8,128)(2,1)S(1)}) custom-call(bf16[56,4224]{1,0:T(8,128)(2,1)S(1)} %collective-permute-done.2.refs_0_.refs_5_, bf16[56,4224]{1,0:T(8,128)(2,1)S(1)} %collective-permute-done.5.refs_1_.refs_6_, bf16[56,4224]{1,0:T(8,128)(2,1)S(1)} %collective-permute-done.6.refs_2_.refs_7_, ...), custom_call_target="tpu_custom_call" | custom-call | tf_op jit(solution)/shard_map/pick/pallas_call | solution.py:183
  49.6 0.1 collective-permute-start.21
  49.6 4.6 %collective-permute-done.13 = bf16[56,4224]{1,0:T(8,128)(2,1)S(1)} collective-permute-done((bf16[56,4224]{1,0:T(8,128)(2,1)}, bf16[56,4224]{1,0:T(8,128)(2,1)S(1)}, u32[]{:S(2)}, u32[]{:S(2)}) %collective-permute-start.13) | collective-permute-done | bytes 473120 | tf_op jit(solution)/shard_map/ppermute | solution.py:339
  54.3 0.1 broadcast_select_fusion.refs_0_.refs_5_
  54.4 1.6 %collective-permute-start.18 = (bf16[56,4224]{1,0:T(8,128)(2,1)S(1)}, bf16[56,4224]{1,0:T(8,128)(2,1)S(1)}, u32[]{:S(2)}, u32[]{:S(2)}) collective-permute-start(bf16[56,4224]{1,0:T(8,128)(2,1)S(1)} %broadcast_select_fusion.refs_0_.refs_5_), channel_id=1, source_target_pairs={{0,2},{1,3},{2,0},{3,1},{4,6},{5,7},{6,4},{7,5},{8,10},{9,11},{10,... | collective-permute-start | bytes 1419272 | tf_op jit(solution)/shard_map/ppermute | solution.py:339
  56.0 1.5 %collective-permute-start.19 = (bf16[56,4224]{1,0:T(8,128)(2,1)S(1)}, bf16[56,4224]{1,0:T(8,128)(2,1)S(1)}, u32[]{:S(2)}, u32[]{:S(2)}) collective-permute-start(bf16[56,4224]{1,0:T(8,128)(2,1)S(1)} %broadcast_select_fusion.refs_0_.refs_5_), channel_id=1, source_target_pairs={{0,4},{1,5},{2,6},{3,7},{4,0},{5,1},{6,2},{7,3},{8,12},{9,13},{10,... | collective-permute-start | bytes 1419272 | tf_op jit(solution)/shard_map/ppermute | solution.py:339
  57.5 0.5 collective-permute-start.9
  58.0 0.5 collective-permute-start.10
  58.6 0.1 and_select_fusion
  58.6 13.5 %experts.2.refs_4_ = bf16[16,24,768]{2,1,0:T(8,128)(2,1)S(1)} custom-call(s32[16]{0:T(128)S(1)} %get-tuple-element.40.owners_ref, bf16[96,4096]{1,0:T(8,128)(2,1)S(1)} %get-tuple-element.30.refs_0_, bf16[96,4096]{1,0:T(8,128)(2,1)S(1)} %collective-permute-done.20.refs_1_, bf16[96,4096]{1,0:T(8,128)(2,1)S(1)} %get-tuple-element.33.refs_2_, ...), custom_call_target="tpu_custom_call" | custom-call | tf_op jit(solution)/shard_map/experts/pallas_call | solution.py:253
  72.2 1.6 %collective-permute-start.22 = (bf16[32,4224]{1,0:T(8,128)(2,1)S(1)}, bf16[32,4224]{1,0:T(8,128)(2,1)S(1)}, u32[]{:S(2)}, u32[]{:S(2)}) collective-permute-start(bf16[32,4224]{1,0:T(8,128)(2,1)S(1)} %slice.41), channel_id=1, source_target_pairs={{0,4},{1,5},{2,6},{3,7},{4,0},{5,1},{6,2},{7,3},{8,12},{9,13},{10,... | collective-permute-start | bytes 811016 | tf_op jit(solution)/shard_map/ppermute | solution.py:339
  73.8 1.5 %collective-permute-start.23 = (bf16[24,4224]{1,0:T(8,128)(2,1)S(1)}, bf16[24,4224]{1,0:T(8,128)(2,1)S(1)}, u32[]{:S(2)}, u32[]{:S(2)}) collective-permute-start(bf16[24,4224]{1,0:T(8,128)(2,1)S(1)} %slice.42), channel_id=1, source_target_pairs={{0,2},{1,3},{2,0},{3,1},{4,6},{5,7},{6,4},{7,5},{8,10},{9,11},{10,... | collective-permute-start | bytes 608264 | tf_op jit(solution)/shard_map/ppermute | solution.py:339
  75.3 3.2 %pick.4 = (bf16[96,4096]{1,0:T(8,128)(2,1)S(1)}, bf16[96,4096]{1,0:T(8,128)(2,1)}) custom-call(bf16[56,4224]{1,0:T(8,128)(2,1)S(1)} %broadcast_select_fusion.1.refs_0_.refs_5_, bf16[56,4224]{1,0:T(8,128)(2,1)S(1)} %collective-permute-done.7.refs_1_.refs_6_, bf16[56,4224]{1,0:T(8,128)(2,1)S(1)} %collective-permute-done.8.refs_2_.refs_7_, ...), custom_call_target="tpu_custom_call" | custom-call | tf_op jit(solution)/shard_map/pick/pallas_call | solution.py:183
  78.5 1.0 collective-permute-done.23.refs_4_.refs_9_
  79.5 3.3 %pick.7 = (bf16[96,4096]{1,0:T(8,128)(2,1)S(1)}, bf16[96,4096]{1,0:T(8,128)(2,1)}) custom-call(bf16[56,4224]{1,0:T(8,128)(2,1)S(1)} %broadcast_select_fusion.refs_0_.refs_5_, bf16[56,4224]{1,0:T(8,128)(2,1)S(1)} %collective-permute-done.18.refs_1_.refs_6_, bf16[56,4224]{1,0:T(8,128)(2,1)S(1)} %collective-permute-done.19.refs_2_.refs_7_, ...), custom_call_target="tpu_custom_call" | custom-call | tf_op jit(solution)/shard_map/pick/pallas_call | solution.py:183
  82.8 0.1 pad_add_fusion.owners_ref
  82.8 2.5 %collective-permute-done.24.refs_3_ = bf16[96,4096]{1,0:T(8,128)(2,1)} collective-permute-done((bf16[96,4096]{1,0:T(8,128)(2,1)}, bf16[96,4096]{1,0:T(8,128)(2,1)}, u32[]{:S(2)}, u32[]{:S(2)}) %collective-permute-start.24) | collective-permute-done | bytes 786464 | tf_op jit(solution)/shard_map/ppermute | solution.py:339
  85.4 14.5 %experts.3 = bf16[32,24,768]{2,1,0:T(8,128)(2,1)} custom-call(s32[17]{0:T(128)S(1)} %pad_add_fusion.owners_ref, bf16[96,4096]{1,0:T(8,128)(2,1)S(1)} %get-tuple-element.27.refs_0_, bf16[96,4096]{1,0:T(8,128)(2,1)S(1)} %collective-permute-done.11.refs_1_, bf16[96,4096]{1,0:T(8,128)(2,1)S(1)} %get-tuple-element.37.refs_2_, ...), custom_call_target="tpu_custom_call" | custom-call | tf_op jit(solution)/shard_map/experts/pallas_call | solution.py:253
  99.9 0.0 copy-start.9
  99.9 0.0 copy-start
  99.9 0.0 copy-start.4
  100.0 0.0 copy-start.5
  100.0 0.0 copy-start.8
  100.0 3.8 %all-to-all-start = ((bf16[32,24,768]{2,1,0:T(8,128)(2,1)}), bf16[32,24,768]{2,1,0:T(8,128)(2,1)S(1)}, u32[]{:S(2)}, u32[]{:S(2)}) async-start(bf16[32,24,768]{2,1,0:T(8,128)(2,1)} %experts.3), calls=%async_computation | async-start | bytes 2359296 | tf_op jit(solution)/shard_map/all_to_all | solution.py:430
  103.8 0.1 copy.23
  103.9 0.0 copy-start.1
  103.9 1.5 %copy-done.1 = bf16[14,128,512]{2,1,0:T(8,128)(2,1)S(1)} copy-done((bf16[14,128,512]{2,1,0:T(8,128)(2,1)S(1)}, bf16[14,128,512]{2,1,0:T(8,128)(2,1)}, u32[]{:S(2)}) %copy-start.1) | copy-done | bytes 1835032
  105.4 1.2 copy-done.2
  106.6 8.1 %attention.1 = bf16[14,4,8192]{2,1,0:T(4,128)(2,1)} custom-call(s32[14]{0:T(128)S(1)} %copy-done.8, bf16[14,4,8192]{2,1,0:T(4,128)(2,1)S(1)} %bitcast.12, bf16[14,4,512]{2,1,0:T(4,128)(2,1)S(1)} %bitcast.15, bf16[14,4,512]{2,1,0:T(4,128)(2,1)S(1)} %bitcast.16, bf16[14,128,512]{2,1,0:T(8,128)(2,1)S(1)} %copy-done, bf16[14,128,512]{2,1,0:T(8,128)(2,1)S(1)} %copy-done.1), custom_call_target="tpu_custom_call" | custom-call | tf_op jit(solution)/shard_map/attention/pallas_call | solution.py:64
  114.7 18.2 %all-to-all-done = bf16[32,24,768]{2,1,0:T(8,128)(2,1)S(1)} async-done(((bf16[32,24,768]{2,1,0:T(8,128)(2,1)}), bf16[32,24,768]{2,1,0:T(8,128)(2,1)S(1)}, u32[]{:S(2)}, u32[]{:S(2)}) %all-to-all-start) | async-done | bytes 1179680 | tf_op jit(solution)/shard_map/all_to_all | solution.py:430
  132.8 1.6 %combine.1 = bf16[14,4,6144]{2,1,0:T(4,128)(2,1)} custom-call(bf16[768,768]{1,0:T(8,128)(2,1)S(1)} %bitcast.11, s32[56,128]{1,0:T(8,128)S(1)} %get-tuple-element.21.columns_ref, f32[56,8]{1,0:T(8,128)S(1)} %bitcast.14), custom_call_target="tpu_custom_call" | custom-call | tf_op jit(solution)/shard_map/combine/pallas_call | solution.py:302
  (31 shorter events, 0.1 us)
Async XLA Ops:
  0.6 41.4 %copy-start.6 = (f32[1,224]{1,0:T(1,128)S(1)}, f32[1,224]{1,0:T(1,128)}, u32[]{:S(2)}) copy-start(f32[1,224]{1,0:T(1,128)} %constant.132.refs_10_) | copy-start | bytes 2692
  0.6 1.0 copy-start.3
  1.7 0.7 copy-start.7
  3.3 13.9 %collective-permute-start.2 = (bf16[56,4224]{1,0:T(8,128)(2,1)S(1)}, bf16[56,4224]{1,0:T(8,128)(2,1)S(1)}, u32[]{:S(2)}, u32[]{:S(2)}) collective-permute-start(bf16[56,4224]{1,0:T(8,128)(2,1)S(1)} %get-tuple-element.29.refs_0_.refs_5_), channel_id=1, source_target_pairs={{0,8},{1,9},{2,10},{3,11},{4,12},{5,13},{6,14},{7,15},{8,0},{9,1},... | collective-permute-start | bytes 1419272 | tf_op jit(solution)/shard_map/ppermute | solution.py:339
  7.2 11.5 %collective-permute-start = (bf16[56,4224]{1,0:T(8,128)(2,1)S(1)}, bf16[56,4224]{1,0:T(8,128)(2,1)S(1)}, u32[]{:S(2)}, u32[]{:S(2)}) collective-permute-start(bf16[56,4224]{1,0:T(8,128)(2,1)S(1)} %get-tuple-element.29.refs_0_.refs_5_), channel_id=1, source_target_pairs={{8,16},{9,17},{10,18},{11,19},{12,20},{13,21},{14,22},{15,23},{16,... | collective-permute-start | bytes 1419272 | tf_op jit(solution)/shard_map/ppermute | solution.py:339
  7.9 12.4 %collective-permute-start.3 = (bf16[56,4224]{1,0:T(8,128)(2,1)S(1)}, bf16[56,4224]{1,0:T(8,128)(2,1)S(1)}, u32[]{:S(2)}, u32[]{:S(2)}) collective-permute-start(bf16[56,4224]{1,0:T(8,128)(2,1)S(1)} %get-tuple-element.29.refs_0_.refs_5_), channel_id=1, source_target_pairs={{0,2},{1,3},{2,0},{3,1},{4,6},{5,7},{6,4},{7,5},{8,10},{9,11},{10,... | collective-permute-start | bytes 1419272 | tf_op jit(solution)/shard_map/ppermute | solution.py:339
  9.4 13.0 %collective-permute-start.4 = (bf16[56,4224]{1,0:T(8,128)(2,1)S(1)}, bf16[56,4224]{1,0:T(8,128)(2,1)S(1)}, u32[]{:S(2)}, u32[]{:S(2)}) collective-permute-start(bf16[56,4224]{1,0:T(8,128)(2,1)S(1)} %get-tuple-element.29.refs_0_.refs_5_), channel_id=1, source_target_pairs={{0,4},{1,5},{2,6},{3,7},{4,0},{5,1},{6,2},{7,3},{8,12},{9,13},{10,... | collective-permute-start | bytes 1419272 | tf_op jit(solution)/shard_map/ppermute | solution.py:339
  17.2 18.1 %collective-permute-start.12 = (bf16[56,4224]{1,0:T(8,128)(2,1)S(1)}, bf16[56,4224]{1,0:T(8,128)(2,1)}, u32[]{:S(2)}, u32[]{:S(2)}) collective-permute-start(bf16[56,4224]{1,0:T(8,128)(2,1)S(1)} %collective-permute-done.2.refs_0_.refs_5_), channel_id=1, source_target_pairs={{8,16},{9,17},{10,18},{11,19},{12,20},{13,21},{14,22},{15,23},{16,... | collective-permute-start | bytes 1419272 | tf_op jit(solution)/shard_map/ppermute | solution.py:339
  18.7 17.5 %collective-permute-start.1 = (bf16[56,4224]{1,0:T(8,128)(2,1)S(1)}, bf16[56,4224]{1,0:T(8,128)(2,1)S(1)}, u32[]{:S(2)}, u32[]{:S(2)}) collective-permute-start(bf16[56,4224]{1,0:T(8,128)(2,1)S(1)} %collective-permute-done), channel_id=1, source_target_pairs={{8,0},{9,1},{10,2},{11,3},{12,4},{13,5},{14,6},{15,7},{16,24},{17,... | collective-permute-start | bytes 1419272 | tf_op jit(solution)/shard_map/ppermute | solution.py:339
  21.0 10.1 %collective-permute-start.14 = (bf16[32,4224]{1,0:T(8,128)(2,1)}, bf16[32,4224]{1,0:T(8,128)(2,1)S(1)}, u32[]{:S(2)}, u32[]{:S(2)}) collective-permute-start(bf16[32,4224]{1,0:T(8,128)(2,1)} %slice.37), channel_id=1, source_target_pairs={{0,4},{1,5},{2,6},{3,7},{4,0},{5,1},{6,2},{7,3},{8,12},{9,13},{10,... | collective-permute-start | bytes 811016 | tf_op jit(solution)/shard_map/ppermute | solution.py:339
  22.5 8.0 %collective-permute-start.16 = (bf16[24,4224]{1,0:T(8,128)(2,1)S(1)}, bf16[24,4224]{1,0:T(8,128)(2,1)S(1)}, u32[]{:S(2)}, u32[]{:S(2)}) collective-permute-start(bf16[24,4224]{1,0:T(8,128)(2,1)S(1)} %slice.38), channel_id=1, source_target_pairs={{0,2},{1,3},{2,0},{3,1},{4,6},{5,7},{6,4},{7,5},{8,10},{9,11},{10,... | collective-permute-start | bytes 608264 | tf_op jit(solution)/shard_map/ppermute | solution.py:339
  24.8 13.4 %collective-permute-start.5 = (bf16[56,4224]{1,0:T(8,128)(2,1)S(1)}, bf16[56,4224]{1,0:T(8,128)(2,1)S(1)}, u32[]{:S(2)}, u32[]{:S(2)}) collective-permute-start(bf16[56,4224]{1,0:T(8,128)(2,1)S(1)} %collective-permute-done.2.refs_0_.refs_5_), channel_id=1, source_target_pairs={{0,2},{1,3},{2,0},{3,1},{4,6},{5,7},{6,4},{7,5},{8,10},{9,11},{10,... | collective-permute-start | bytes 1419272 | tf_op jit(solution)/shard_map/ppermute | solution.py:339
  30.5 8.6 %collective-permute-start.6 = (bf16[56,4224]{1,0:T(8,128)(2,1)S(1)}, bf16[56,4224]{1,0:T(8,128)(2,1)S(1)}, u32[]{:S(2)}, u32[]{:S(2)}) collective-permute-start(bf16[56,4224]{1,0:T(8,128)(2,1)S(1)} %collective-permute-done.2.refs_0_.refs_5_), channel_id=1, source_target_pairs={{0,4},{1,5},{2,6},{3,7},{4,0},{5,1},{6,2},{7,3},{8,12},{9,13},{10,... | collective-permute-start | bytes 1419272 | tf_op jit(solution)/shard_map/ppermute | solution.py:339
  31.1 13.5 %collective-permute-start.17 = (bf16[24,4224]{1,0:T(8,128)(2,1)S(1)}, bf16[24,4224]{1,0:T(8,128)(2,1)S(1)}, u32[]{:S(2)}, u32[]{:S(2)}) collective-permute-start(bf16[24,4224]{1,0:T(8,128)(2,1)S(1)} %collective-permute-done.16.refs_4_.refs_9_), channel_id=1, source_target_pairs={{0,8},{1,9},{2,10},{3,11},{4,12},{5,13},{6,14},{7,15},{8,0},{9,1},... | collective-permute-start | bytes 608264 | tf_op jit(solution)/shard_map/ppermute | solution.py:339
  35.3 11.7 %collective-permute-start.15 = (bf16[32,4224]{1,0:T(8,128)(2,1)S(1)}, bf16[32,4224]{1,0:T(8,128)(2,1)S(1)}, u32[]{:S(2)}, u32[]{:S(2)}) collective-permute-start(bf16[32,4224]{1,0:T(8,128)(2,1)S(1)} %collective-permute-done.14.refs_3_.refs_8_), channel_id=1, source_target_pairs={{0,8},{1,9},{2,10},{3,11},{4,12},{5,13},{6,14},{7,15},{8,0},{9,1},... | collective-permute-start | bytes 811016 | tf_op jit(solution)/shard_map/ppermute | solution.py:339
  36.1 18.2 %collective-permute-start.13 = (bf16[56,4224]{1,0:T(8,128)(2,1)}, bf16[56,4224]{1,0:T(8,128)(2,1)S(1)}, u32[]{:S(2)}, u32[]{:S(2)}) collective-permute-start(bf16[56,4224]{1,0:T(8,128)(2,1)} %collective-permute-done.12), channel_id=1, source_target_pairs={{8,0},{9,1},{10,2},{11,3},{12,4},{13,5},{14,6},{15,7},{16,24},{17,... | collective-permute-start | bytes 1419272 | tf_op jit(solution)/shard_map/ppermute | solution.py:339
  39.2 15.2 %collective-permute-start.7 = (bf16[56,4224]{1,0:T(8,128)(2,1)S(1)}, bf16[56,4224]{1,0:T(8,128)(2,1)S(1)}, u32[]{:S(2)}, u32[]{:S(2)}) collective-permute-start(bf16[56,4224]{1,0:T(8,128)(2,1)S(1)} %broadcast_select_fusion.1.refs_0_.refs_5_), channel_id=1, source_target_pairs={{0,2},{1,3},{2,0},{3,1},{4,6},{5,7},{6,4},{7,5},{8,10},{9,11},{10,... | collective-permute-start | bytes 1419272 | tf_op jit(solution)/shard_map/ppermute | solution.py:339
  41.1 13.3 %collective-permute-start.8 = (bf16[56,4224]{1,0:T(8,128)(2,1)S(1)}, bf16[56,4224]{1,0:T(8,128)(2,1)S(1)}, u32[]{:S(2)}, u32[]{:S(2)}) collective-permute-start(bf16[56,4224]{1,0:T(8,128)(2,1)S(1)} %broadcast_select_fusion.1.refs_0_.refs_5_), channel_id=1, source_target_pairs={{0,4},{1,5},{2,6},{3,7},{4,0},{5,1},{6,2},{7,3},{8,12},{9,13},{10,... | collective-permute-start | bytes 1419272 | tf_op jit(solution)/shard_map/ppermute | solution.py:339
  44.6 13.4 %collective-permute-start.20 = (bf16[96,4096]{1,0:T(8,128)(2,1)S(1)}, bf16[96,4096]{1,0:T(8,128)(2,1)S(1)}, u32[]{:S(2)}, u32[]{:S(2)}) collective-permute-start(bf16[96,4096]{1,0:T(8,128)(2,1)S(1)} %get-tuple-element.32), channel_id=1, source_target_pairs={{0,1},{1,0},{2,3},{3,2},{4,5},{5,4},{6,7},{7,6},{8,9},{9,8},{10,11... | collective-permute-start | bytes 2359304 | tf_op jit(solution)/shard_map/ppermute | solution.py:339
  49.6 9.1 %collective-permute-start.21 = (bf16[96,4096]{1,0:T(8,128)(2,1)S(1)}, bf16[96,4096]{1,0:T(8,128)(2,1)S(1)}, u32[]{:S(2)}, u32[]{:S(2)}) collective-permute-start(bf16[96,4096]{1,0:T(8,128)(2,1)S(1)} %get-tuple-element.34), channel_id=1, source_target_pairs={{0,1},{1,0},{2,3},{3,2},{4,5},{5,4},{6,7},{7,6},{8,9},{9,8},{10,11... | collective-permute-start | bytes 2359304 | tf_op jit(solution)/shard_map/ppermute | solution.py:339
  54.4 17.7 %collective-permute-start.18 = (bf16[56,4224]{1,0:T(8,128)(2,1)S(1)}, bf16[56,4224]{1,0:T(8,128)(2,1)S(1)}, u32[]{:S(2)}, u32[]{:S(2)}) collective-permute-start(bf16[56,4224]{1,0:T(8,128)(2,1)S(1)} %broadcast_select_fusion.refs_0_.refs_5_), channel_id=1, source_target_pairs={{0,2},{1,3},{2,0},{3,1},{4,6},{5,7},{6,4},{7,5},{8,10},{9,11},{10,... | collective-permute-start | bytes 1419272 | tf_op jit(solution)/shard_map/ppermute | solution.py:339
  56.0 16.1 %collective-permute-start.19 = (bf16[56,4224]{1,0:T(8,128)(2,1)S(1)}, bf16[56,4224]{1,0:T(8,128)(2,1)S(1)}, u32[]{:S(2)}, u32[]{:S(2)}) collective-permute-start(bf16[56,4224]{1,0:T(8,128)(2,1)S(1)} %broadcast_select_fusion.refs_0_.refs_5_), channel_id=1, source_target_pairs={{0,4},{1,5},{2,6},{3,7},{4,0},{5,1},{6,2},{7,3},{8,12},{9,13},{10,... | collective-permute-start | bytes 1419272 | tf_op jit(solution)/shard_map/ppermute | solution.py:339
  57.5 14.7 %collective-permute-start.9 = (bf16[32,4224]{1,0:T(8,128)(2,1)S(1)}, bf16[32,4224]{1,0:T(8,128)(2,1)S(1)}, u32[]{:S(2)}, u32[]{:S(2)}) collective-permute-start(bf16[32,4224]{1,0:T(8,128)(2,1)S(1)} %slice.39), channel_id=1, source_target_pairs={{0,4},{1,5},{2,6},{3,7},{4,0},{5,1},{6,2},{7,3},{8,12},{9,13},{10,... | collective-permute-start | bytes 811016 | tf_op jit(solution)/shard_map/ppermute | solution.py:339
  58.0 14.2 %collective-permute-start.10 = (bf16[24,4224]{1,0:T(8,128)(2,1)S(1)}, bf16[24,4224]{1,0:T(8,128)(2,1)S(1)}, u32[]{:S(2)}, u32[]{:S(2)}) collective-permute-start(bf16[24,4224]{1,0:T(8,128)(2,1)S(1)} %slice.40), channel_id=1, source_target_pairs={{0,2},{1,3},{2,0},{3,1},{4,6},{5,7},{6,4},{7,5},{8,10},{9,11},{10,... | collective-permute-start | bytes 608264 | tf_op jit(solution)/shard_map/ppermute | solution.py:339
  72.2 7.3 %collective-permute-start.22 = (bf16[32,4224]{1,0:T(8,128)(2,1)S(1)}, bf16[32,4224]{1,0:T(8,128)(2,1)S(1)}, u32[]{:S(2)}, u32[]{:S(2)}) collective-permute-start(bf16[32,4224]{1,0:T(8,128)(2,1)S(1)} %slice.41), channel_id=1, source_target_pairs={{0,4},{1,5},{2,6},{3,7},{4,0},{5,1},{6,2},{7,3},{8,12},{9,13},{10,... | collective-permute-start | bytes 811016 | tf_op jit(solution)/shard_map/ppermute | solution.py:339
  73.8 5.7 %collective-permute-start.23 = (bf16[24,4224]{1,0:T(8,128)(2,1)S(1)}, bf16[24,4224]{1,0:T(8,128)(2,1)S(1)}, u32[]{:S(2)}, u32[]{:S(2)}) collective-permute-start(bf16[24,4224]{1,0:T(8,128)(2,1)S(1)} %slice.42), channel_id=1, source_target_pairs={{0,2},{1,3},{2,0},{3,1},{4,6},{5,7},{6,4},{7,5},{8,10},{9,11},{10,... | collective-permute-start | bytes 608264 | tf_op jit(solution)/shard_map/ppermute | solution.py:339
  78.5 4.4 %collective-permute-start.11 = (bf16[96,4096]{1,0:T(8,128)(2,1)}, bf16[96,4096]{1,0:T(8,128)(2,1)S(1)}, u32[]{:S(2)}, u32[]{:S(2)}) collective-permute-start(bf16[96,4096]{1,0:T(8,128)(2,1)} %get-tuple-element.28), channel_id=1, source_target_pairs={{0,1},{1,0},{2,3},{3,2},{4,5},{5,4},{6,7},{7,6},{8,9},{9,8},{10,11... | collective-permute-start | bytes 2359304 | tf_op jit(solution)/shard_map/ppermute | solution.py:339
  82.8 2.6 %collective-permute-start.24 = (bf16[96,4096]{1,0:T(8,128)(2,1)}, bf16[96,4096]{1,0:T(8,128)(2,1)}, u32[]{:S(2)}, u32[]{:S(2)}) collective-permute-start(bf16[96,4096]{1,0:T(8,128)(2,1)} %get-tuple-element.38), channel_id=1, source_target_pairs={{0,1},{1,0},{2,3},{3,2},{4,5},{5,4},{6,7},{7,6},{8,9},{9,8},{10,11... | collective-permute-start | bytes 2359304 | tf_op jit(solution)/shard_map/ppermute | solution.py:339
  99.9 3.8 %copy-start.9 = (f32[4,14,8]{1,2,0:T(8,128)S(1)}, f32[4,14,8]{1,2,0:T(8,128)}, u32[]{:S(2)}) copy-start(f32[4,14,8]{1,2,0:T(8,128)} %param.23) | copy-start | bytes 5380
  99.9 3.9 %copy-start = (bf16[14,128,512]{2,1,0:T(8,128)(2,1)S(1)}, bf16[14,128,512]{2,1,0:T(8,128)(2,1)}, u32[]{:S(2)}) copy-start(bf16[14,128,512]{2,1,0:T(8,128)(2,1)} %k_ref.1) | copy-start | bytes 5505028
  99.9 3.9 %copy-start.4 = (bf16[4,14,512]{2,0,1:T(4,128)(2,1)S(1)}, bf16[4,14,512]{2,0,1:T(4,128)(2,1)}, u32[]{:S(2)}) copy-start(bf16[4,14,512]{2,0,1:T(4,128)(2,1)} %param.27) | copy-start | bytes 172036
  100.0 3.9 %copy-start.5 = (bf16[4,14,512]{2,0,1:T(4,128)(2,1)S(1)}, bf16[4,14,512]{2,0,1:T(4,128)(2,1)}, u32[]{:S(2)}) copy-start(bf16[4,14,512]{2,0,1:T(4,128)(2,1)} %param.28) | copy-start | bytes 172036
  100.0 3.9 %copy-start.8 = (s32[14]{0:T(128)S(1)}, s32[14]{0:T(128)}, u32[]{:S(2)}) copy-start(s32[14]{0:T(128)} %lengths_ref) | copy-start | bytes 172
  100.0 32.9 %all-to-all-start = ((bf16[32,24,768]{2,1,0:T(8,128)(2,1)}), bf16[32,24,768]{2,1,0:T(8,128)(2,1)S(1)}, u32[]{:S(2)}, u32[]{:S(2)}) async-start(bf16[32,24,768]{2,1,0:T(8,128)(2,1)} %experts.3), calls=%async_computation | async-start | bytes 2359296 | tf_op jit(solution)/shard_map/all_to_all | solution.py:430
  103.9 1.5 %copy-start.1 = (bf16[14,128,512]{2,1,0:T(8,128)(2,1)S(1)}, bf16[14,128,512]{2,1,0:T(8,128)(2,1)}, u32[]{:S(2)}) copy-start(bf16[14,128,512]{2,1,0:T(8,128)(2,1)} %v_ref.1) | copy-start | bytes 5505028
  105.4 1.2 copy-start.2
